TPU v7x, 32 devices: a whole 2x2x4 slice. The times are simulated.
32 devices in a mesh: dp: 16 (over z, y, core), fsdp: 2 (over x).
Axes of the slice: x: 2, y: 2, z: 4, core: 2. Of those that a mesh axis runs over, the one named last changes fastest.
Arguments:
- tokens: bfloat16 [32768, 1152], P(('dp', 'fsdp')), may hold values from -6 to 6
- image_lengths: int32 [128], P(('dp', 'fsdp')), may hold values from 0 to 1024, as said below
- timesteps: int32 [128], P(('dp', 'fsdp')), may hold values from 0 to 999
- patch_cells: int32 [32768], P(('dp', 'fsdp')), may hold values from 0 to 1023, as said below
- norm1_gain: bfloat16 [1152], P(('dp', 'fsdp')), may hold values from 0.5 to 1.5
- norm1_bias: bfloat16 [1152], P(('dp', 'fsdp')), may hold values from -2.5 to 2.5
- qkv_weight: bfloat16 [1152, 3456], P(None, ('dp', 'fsdp')), may hold values from -0.1875 to 0.1875
- time_weight: bfloat16 [1152, 2304], P(None, ('dp', 'fsdp')), may hold values from -0.1875 to 0.1875
- out_weight: bfloat16 [1152, 1152], P(('dp', 'fsdp')), may hold values from -1 to 1
- out_bias: bfloat16 [1152], P(('dp', 'fsdp')), may hold values from -2.5 to 2.5
- norm2_gain: bfloat16 [1152], P(('dp', 'fsdp')), may hold values from 0.5 to 1.5
- norm2_bias: bfloat16 [1152], P(('dp', 'fsdp')), may hold values from -2.5 to 2.5
- fc1_weight: bfloat16 [1152, 4608], P(None, ('dp', 'fsdp')), may hold values from -0.1875 to 0.1875
- fc1_bias: bfloat16 [4608], P(('dp', 'fsdp')), may hold values from -2.5 to 2.5
- fc2_weight: bfloat16 [4608, 1152], P(('dp', 'fsdp')), may hold values from -0.09375 to 0.09375
- fc2_bias: bfloat16 [1152], P(('dp', 'fsdp')), may hold values from -2.5 to 2.5
- row_table: bfloat16 [16, 63], P('fsdp'), may hold values from -4 to 4
- col_table: bfloat16 [16, 63], P('fsdp'), may hold values from -4 to 4
- cotangent: bfloat16 [32768, 1152], P(('dp', 'fsdp')), may hold values from -6 to 6
Outputs:
- layer_out: bfloat16 [32768, 1152], P(('dp', 'fsdp'))
- input_grad: bfloat16 [32768, 1152], P(('dp', 'fsdp'))
- norm1_gain_grad: float32 [1152], P(('dp', 'fsdp'))
- norm1_bias_grad: float32 [1152], P(('dp', 'fsdp'))
- qkv_weight_grad: float32 [1152, 3456], P(None, ('dp', 'fsdp'))
- time_weight_grad: float32 [1152, 2304], P(None, ('dp', 'fsdp'))
- out_weight_grad: float32 [1152, 1152], P(('dp', 'fsdp'))
- out_bias_grad: float32 [1152], P(('dp', 'fsdp'))
- norm2_gain_grad: float32 [1152], P(('dp', 'fsdp'))
- norm2_bias_grad: float32 [1152], P(('dp', 'fsdp'))
- fc1_weight_grad: float32 [1152, 4608], P(None, ('dp', 'fsdp'))
- fc1_bias_grad: float32 [4608], P(('dp', 'fsdp'))
- fc2_weight_grad: float32 [4608, 1152], P(('dp', 'fsdp'))
- fc2_bias_grad: float32 [1152], P(('dp', 'fsdp'))
- row_table_grad: float32 [16, 63], P('fsdp')
- col_table_grad: float32 [16, 63], P('fsdp')
Inputs may be any that keep to these rules, and one draw needn't show every extreme that they name: `image_lengths`: entries come in aligned groups of 4, one group for each frame of 1024 token rows. A frame holds either one large image: its first entry is the image's length, 512 to 1024, and the other entries are 0; or 4 small images in slots of 256 rows, each of length 128 to 256. An image's tokens are the first rows of its slot (of the frame for a large image); the other rows are padding. Every draw has a large image of length 1024 and a small image of length 256. `patch_cells`: A row's patch as patch_row * 32 + patch_column on its image's grid (32 x 32 for a large image, 16 x 16 for a small one); within an image's slot, padding rows included, no patch repeats.
All inputs are finite; a program needn't handle non-finite values.
Results may differ from a plain program's by a relative error of at most 0.013.
Values may be sent and summed in bfloat16 or wider, within the bound.
A program may use at most 384 MiB of HBM per device.

v0:
```python
import math

import jax
import jax.numpy as jnp
from jax import lax
from jax.sharding import PartitionSpec as P

HEADS = 16
GRID = 32
SMALL = 16


def norm_rows(values, row_gain, offset):
    centre = values - jnp.mean(values, axis=-1, keepdims=True)
    spread = jnp.mean(centre * centre, axis=-1, keepdims=True)
    return centre * lax.rsqrt(spread + 1e-06) * row_gain + offset


def time_embed(stamps, feat_width):
    half_width = feat_width // 2
    frequency = jnp.exp(-math.log(10000.0) * jnp.arange(half_width, dtype=jnp.float32) / half_width)
    angles = stamps.astype(jnp.float32)[:, None] * frequency[None, :]
    return jnp.concatenate([jnp.cos(angles), jnp.sin(angles)], axis=1)


def exact_gelu(values):
    return jax.nn.gelu(values, approximate=False)


def local(
    tokens,
    image_lengths,
    timesteps,
    patch_cells,
    norm1_gain,
    norm1_bias,
    qkv_weight,
    time_weight,
    out_weight,
    out_bias,
    norm2_gain,
    norm2_bias,
    fc1_weight,
    fc1_bias,
    fc2_weight,
    fc2_bias,
    row_table,
    col_table,
    cotangent,
):
    (
        gain_one,
        shift_one,
        w_qkv,
        w_time,
        w_out,
        b_out,
        gain_two,
        shift_two,
        w_up,
        b_up,
        w_down,
        b_down,
    ) = (
        lax.all_gather(norm1_gain, ("dp", "fsdp"), axis=0, tiled=True),
        lax.all_gather(norm1_bias, ("dp", "fsdp"), axis=0, tiled=True),
        lax.all_gather(qkv_weight, ("dp", "fsdp"), axis=1, tiled=True),
        lax.all_gather(time_weight, ("dp", "fsdp"), axis=1, tiled=True),
        lax.all_gather(out_weight, ("dp", "fsdp"), axis=0, tiled=True),
        lax.all_gather(out_bias, ("dp", "fsdp"), axis=0, tiled=True),
        lax.all_gather(norm2_gain, ("dp", "fsdp"), axis=0, tiled=True),
        lax.all_gather(norm2_bias, ("dp", "fsdp"), axis=0, tiled=True),
        lax.all_gather(fc1_weight, ("dp", "fsdp"), axis=1, tiled=True),
        lax.all_gather(fc1_bias, ("dp", "fsdp"), axis=0, tiled=True),
        lax.all_gather(fc2_weight, ("dp", "fsdp"), axis=0, tiled=True),
        lax.all_gather(fc2_bias, ("dp", "fsdp"), axis=0, tiled=True),
    )
    row_full, col_full = (
        lax.all_gather(row_table, "fsdp", axis=0, tiled=True),
        lax.all_gather(col_table, "fsdp", axis=0, tiled=True),
    )
    highest = lax.Precision.HIGHEST
    total_rows, feat_width = tokens.shape
    head_dim = feat_width // HEADS
    frame_rows = GRID * GRID
    slot_rows = SMALL * SMALL
    per_frame = frame_rows // slot_rows
    frames = total_rows // frame_rows
    head_group = min(HEADS, 4)
    block_rows = min(512, frame_rows)
    score_scale = 1.0 / math.sqrt(head_dim)
    grid_index = jnp.arange(GRID, dtype=jnp.int32)
    lengths = image_lengths.reshape(frames, per_frame)
    local_rows = jnp.arange(frame_rows, dtype=jnp.int32)
    large_image = lengths[:, 0:1] > slot_rows
    slot_index = jnp.where(large_image, 0, local_rows[None, :] // slot_rows)
    slot_start = jnp.where(large_image, 0, slot_index * slot_rows)
    slot_pick = slot_index[:, :, None] == jnp.arange(per_frame, dtype=jnp.int32)[None, None, :]
    slot_length = jnp.sum(jnp.where(slot_pick, lengths[:, None, :], 0), axis=2)
    valid_rows = local_rows[None, :] - slot_start < slot_length
    valid_flat = valid_rows.reshape(total_rows)
    image_index = (slot_index + per_frame * jnp.arange(frames, dtype=jnp.int32)[:, None]).reshape(
        total_rows
    )
    image_pick = image_index[:, None] == jnp.arange(frames * per_frame, dtype=jnp.int32)[None, :]
    pick_float = image_pick.astype(jnp.float32)
    pick_low = image_pick.astype(jnp.bfloat16)
    embedded = time_embed(timesteps, feat_width).astype(jnp.bfloat16)
    time_proj = jnp.dot(embedded, w_time, preferred_element_type=jnp.float32)
    time_rows = jnp.dot(pick_float, time_proj, precision=highest)
    token_float = tokens.astype(jnp.float32)
    normed_one = norm_rows(
        token_float, gain_one.astype(jnp.float32), shift_one.astype(jnp.float32)
    ).astype(jnp.bfloat16)
    projected = jnp.dot(normed_one, w_qkv, preferred_element_type=jnp.float32)
    query_low = (projected[:, :feat_width] + time_rows[:, :feat_width]).astype(jnp.bfloat16)
    key_low = projected[:, feat_width : 2 * feat_width].astype(jnp.bfloat16)
    value_low = (projected[:, 2 * feat_width :] + time_rows[:, feat_width:]).astype(jnp.bfloat16)
    patch_row = (patch_cells // GRID).reshape(frames, frame_rows)
    patch_col = (patch_cells % GRID).reshape(frames, frame_rows)

    def head_view(matrix):
        return matrix.reshape(frames, frame_rows, HEADS, head_dim)

    def pair_onehot(row_frame, col_frame):
        onehot_row = row_frame[:, None] == grid_index[None, :]
        onehot_col = col_frame[:, None] == grid_index[None, :]
        return jnp.concatenate([onehot_row, onehot_col], axis=1).astype(jnp.bfloat16)

    def scores(query_block, key_group, head_start, row_block, col_block, onehot_both, allowed):
        raw_scores = (
            jnp.einsum("qhd,khd->hqk", query_block, key_group, preferred_element_type=jnp.float32)
            * score_scale
        )
        row_choice = row_block[:, None] - grid_index[None, :] + GRID - 1
        col_choice = col_block[:, None] - grid_index[None, :] + GRID - 1
        row_bias = jnp.take(row_full[head_start : head_start + head_group], row_choice, axis=1)
        col_bias = jnp.take(col_full[head_start : head_start + head_group], col_choice, axis=1)
        both_bias = jnp.concatenate([row_bias, col_bias], axis=2)
        bias_sum = jnp.einsum(
            "hqg,kg->hqk", both_bias, onehot_both, preferred_element_type=jnp.float32
        )
        return jnp.where(allowed[None], raw_scores + bias_sum, -1e30)

    def frame_forward(frame_inputs):
        query_frame, key_frame, value_frame, row_frame, col_frame, slot_frame, valid_frame = (
            frame_inputs
        )
        onehot_both = pair_onehot(row_frame, col_frame)
        mixed_groups = []
        logsum_groups = []
        for head_start in range(0, HEADS, head_group):
            head_end = head_start + head_group
            mixed_blocks = []
            logsum_blocks = []
            for block_start in range(0, frame_rows, block_rows):
                block_end = block_start + block_rows
                allowed = (
                    slot_frame[block_start:block_end, None] == slot_frame[None, :]
                ) & valid_frame[None, :]
                score_block = scores(
                    query_frame[block_start:block_end, head_start:head_end],
                    key_frame[:, head_start:head_end],
                    head_start,
                    row_frame[block_start:block_end],
                    col_frame[block_start:block_end],
                    onehot_both,
                    allowed,
                )
                top_score = jnp.max(score_block, axis=2, keepdims=True)
                exponent = jnp.exp(score_block - top_score)
                row_total = jnp.sum(exponent, axis=2, keepdims=True)
                weights_low = (exponent / row_total).astype(jnp.bfloat16)
                mixed_blocks.append(
                    jnp.einsum(
                        "hqk,khd->qhd",
                        weights_low,
                        value_frame[:, head_start:head_end],
                        preferred_element_type=jnp.float32,
                    )
                )
                logsum_blocks.append((top_score + jnp.log(row_total))[:, :, 0])
            mixed_groups.append(jnp.concatenate(mixed_blocks, axis=0))
            logsum_groups.append(jnp.concatenate(logsum_blocks, axis=1))
        return (
            jnp.concatenate(mixed_groups, axis=1).astype(jnp.bfloat16),
            jnp.concatenate(logsum_groups, axis=0),
        )

    attended, logsum = lax.map(
        frame_forward,
        (
            head_view(query_low),
            head_view(key_low),
            head_view(value_low),
            patch_row,
            patch_col,
            slot_index,
            valid_rows,
        ),
    )
    attended = attended.reshape(total_rows, feat_width)
    branch_one = jnp.dot(attended, w_out, preferred_element_type=jnp.float32) + b_out.astype(
        jnp.float32
    )
    hidden_one = token_float + branch_one
    normed_two = norm_rows(
        hidden_one, gain_two.astype(jnp.float32), shift_two.astype(jnp.float32)
    ).astype(jnp.bfloat16)
    pre_act = jnp.dot(normed_two, w_up, preferred_element_type=jnp.float32) + b_up.astype(
        jnp.float32
    )
    activated = exact_gelu(pre_act).astype(jnp.bfloat16)
    layer_out = (
        hidden_one
        + (
            jnp.dot(activated, w_down, preferred_element_type=jnp.float32)
            + b_down.astype(jnp.float32)
        )
    ).astype(jnp.bfloat16)
    (
        gain_one,
        shift_one,
        w_qkv,
        w_time,
        w_out,
        b_out,
        gain_two,
        shift_two,
        w_up,
        b_up,
        w_down,
        b_down,
    ) = (
        lax.all_gather(norm1_gain, ("dp", "fsdp"), axis=0, tiled=True),
        lax.all_gather(norm1_bias, ("dp", "fsdp"), axis=0, tiled=True),
        lax.all_gather(qkv_weight, ("dp", "fsdp"), axis=1, tiled=True),
        lax.all_gather(time_weight, ("dp", "fsdp"), axis=1, tiled=True),
        lax.all_gather(out_weight, ("dp", "fsdp"), axis=0, tiled=True),
        lax.all_gather(out_bias, ("dp", "fsdp"), axis=0, tiled=True),
        lax.all_gather(norm2_gain, ("dp", "fsdp"), axis=0, tiled=True),
        lax.all_gather(norm2_bias, ("dp", "fsdp"), axis=0, tiled=True),
        lax.all_gather(fc1_weight, ("dp", "fsdp"), axis=1, tiled=True),
        lax.all_gather(fc1_bias, ("dp", "fsdp"), axis=0, tiled=True),
        lax.all_gather(fc2_weight, ("dp", "fsdp"), axis=0, tiled=True),
        lax.all_gather(fc2_bias, ("dp", "fsdp"), axis=0, tiled=True),
    )
    out_cot = cotangent.astype(jnp.float32) * valid_flat[:, None].astype(jnp.float32)
    cot_low = out_cot.astype(jnp.bfloat16)
    down_grad = jnp.einsum("rf,rd->fd", activated, cot_low, preferred_element_type=jnp.float32)
    down_bias_grad = jnp.sum(out_cot, axis=0)
    act_grad = jnp.dot(cot_low, w_down.T, preferred_element_type=jnp.float32)
    gelu_pull = jax.vjp(exact_gelu, pre_act)[1]
    pre_grad = gelu_pull(act_grad)[0].astype(jnp.bfloat16)
    up_grad_turned = jnp.einsum(
        "rf,rd->fd", pre_grad, normed_two, preferred_element_type=jnp.float32
    )
    up_bias_grad = jnp.sum(pre_grad, axis=0, dtype=jnp.float32)
    normed_two_grad = jnp.dot(pre_grad, w_up.T, preferred_element_type=jnp.float32)
    norm_two_pull = jax.vjp(
        norm_rows, hidden_one, gain_two.astype(jnp.float32), shift_two.astype(jnp.float32)
    )[1]
    hidden_part, gain_two_grad, shift_two_grad = norm_two_pull(normed_two_grad)
    hidden_grad = out_cot + hidden_part
    branch_grad = hidden_grad.astype(jnp.bfloat16)
    out_grad = jnp.einsum("ra,rd->ad", attended, branch_grad, preferred_element_type=jnp.float32)
    out_bias_grad = jnp.sum(branch_grad, axis=0, dtype=jnp.float32)
    attended_grad = jnp.dot(branch_grad, w_out.T, preferred_element_type=jnp.float32).astype(
        jnp.bfloat16
    )

    def frame_backward(frame_inputs):
        (
            query_frame,
            key_frame,
            value_frame,
            grad_frame,
            logsum_frame,
            row_frame,
            col_frame,
            slot_frame,
            valid_frame,
        ) = frame_inputs
        onehot_both = pair_onehot(row_frame, col_frame)
        both_float = onehot_both.astype(jnp.float32)
        query_groups = []
        key_groups = []
        value_groups = []
        pair_groups = []
        for head_start in range(0, HEADS, head_group):
            head_end = head_start + head_group
            query_blocks = []
            key_sum = jnp.zeros((frame_rows, head_group, head_dim), jnp.float32)
            value_sum = jnp.zeros((frame_rows, head_group, head_dim), jnp.float32)
            pair_sum = jnp.zeros((head_group, 2 * GRID, 2 * GRID), jnp.float32)
            for block_start in range(0, frame_rows, block_rows):
                block_end = block_start + block_rows
                allowed = (
                    slot_frame[block_start:block_end, None] == slot_frame[None, :]
                ) & valid_frame[None, :]
                query_block = query_frame[block_start:block_end, head_start:head_end]
                grad_block = grad_frame[block_start:block_end, head_start:head_end]
                score_block = scores(
                    query_block,
                    key_frame[:, head_start:head_end],
                    head_start,
                    row_frame[block_start:block_end],
                    col_frame[block_start:block_end],
                    onehot_both,
                    allowed,
                )
                softmax_block = jnp.exp(
                    score_block - logsum_frame[head_start:head_end, block_start:block_end, None]
                )
                prob_grad = jnp.einsum(
                    "qhd,khd->hqk",
                    grad_block,
                    value_frame[:, head_start:head_end],
                    preferred_element_type=jnp.float32,
                )
                centred = jnp.sum(softmax_block * prob_grad, axis=2, keepdims=True)
                score_grad = (softmax_block * (prob_grad - centred)).astype(jnp.bfloat16)
                query_blocks.append(
                    jnp.einsum(
                        "hqk,khd->qhd",
                        score_grad,
                        key_frame[:, head_start:head_end],
                        preferred_element_type=jnp.float32,
                    )
                    * score_scale
                )
                key_sum = (
                    key_sum
                    + jnp.einsum(
                        "hqk,qhd->khd", score_grad, query_block, preferred_element_type=jnp.float32
                    )
                    * score_scale
                )
                value_sum = value_sum + jnp.einsum(
                    "hqk,qhd->khd",
                    softmax_block.astype(jnp.bfloat16),
                    grad_block,
                    preferred_element_type=jnp.float32,
                )
                pair_part = jnp.einsum(
                    "hqk,qg->hgk",
                    score_grad,
                    onehot_both[block_start:block_end],
                    preferred_element_type=jnp.float32,
                )
                pair_sum = pair_sum + jnp.einsum(
                    "hgk,kj->hgj", pair_part, both_float, precision=highest
                )
            query_groups.append(jnp.concatenate(query_blocks, axis=0))
            key_groups.append(key_sum)
            value_groups.append(value_sum)
            pair_groups.append(pair_sum)
        return (
            jnp.concatenate(query_groups, axis=1),
            jnp.concatenate(key_groups, axis=1),
            jnp.concatenate(value_groups, axis=1),
            jnp.concatenate(pair_groups, axis=0),
        )

    query_grad, key_grad, value_grad, pair_terms = lax.map(
        frame_backward,
        (
            head_view(query_low),
            head_view(key_low),
            head_view(value_low),
            head_view(attended_grad),
            logsum,
            patch_row,
            patch_col,
            slot_index,
            valid_rows,
        ),
    )
    qkv_grad = jnp.concatenate(
        [
            query_grad.reshape(total_rows, feat_width),
            key_grad.reshape(total_rows, feat_width),
            value_grad.reshape(total_rows, feat_width),
        ],
        axis=1,
    ).astype(jnp.bfloat16)
    qkv_grad_turned = jnp.einsum(
        "rc,rd->cd", qkv_grad, normed_one, preferred_element_type=jnp.float32
    )
    normed_one_grad = jnp.dot(qkv_grad, w_qkv.T, preferred_element_type=jnp.float32)
    time_query = jnp.dot(pick_low.T, qkv_grad[:, :feat_width], preferred_element_type=jnp.float32)
    time_value = jnp.dot(
        pick_low.T, qkv_grad[:, 2 * feat_width :], preferred_element_type=jnp.float32
    )
    time_sums = jnp.concatenate([time_query, time_value], axis=1)
    time_grad_turned = jnp.dot(time_sums.T, embedded.astype(jnp.float32), precision=highest)
    norm_one_pull = jax.vjp(
        norm_rows, token_float, gain_one.astype(jnp.float32), shift_one.astype(jnp.float32)
    )[1]
    token_part, gain_one_grad, shift_one_grad = norm_one_pull(normed_one_grad)
    input_grad = (hidden_grad + token_part).astype(jnp.bfloat16)
    pair_total = jnp.sum(pair_terms, axis=0)
    offsets = grid_index[:, None] - grid_index[None, :] + GRID - 1
    diagonal_pick = (
        offsets[:, :, None] == jnp.arange(2 * GRID - 1, dtype=jnp.int32)[None, None, :]
    ).astype(jnp.float32)
    row_grad = jnp.einsum(
        "hgj,gjt->ht", pair_total[:, :GRID, :GRID], diagonal_pick, precision=highest
    )
    col_grad = jnp.einsum(
        "hgj,gjt->ht", pair_total[:, GRID:, GRID:], diagonal_pick, precision=highest
    )
    row_total, col_total = lax.psum((row_grad, col_grad), ("dp", "fsdp"))
    head_share = HEADS // lax.axis_size("fsdp")
    head_offset = lax.axis_index("fsdp") * head_share
    row_share = lax.dynamic_slice_in_dim(row_total, head_offset, head_share, 0)
    col_share = lax.dynamic_slice_in_dim(col_total, head_offset, head_share, 0)
    parts = (
        lax.psum_scatter(gain_one_grad, ("dp", "fsdp"), scatter_dimension=0, tiled=True),
        lax.psum_scatter(shift_one_grad, ("dp", "fsdp"), scatter_dimension=0, tiled=True),
        lax.psum_scatter(qkv_grad_turned, ("dp", "fsdp"), scatter_dimension=0, tiled=True),
        lax.psum_scatter(time_grad_turned, ("dp", "fsdp"), scatter_dimension=0, tiled=True),
        lax.psum_scatter(out_grad, ("dp", "fsdp"), scatter_dimension=0, tiled=True),
        lax.psum_scatter(out_bias_grad, ("dp", "fsdp"), scatter_dimension=0, tiled=True),
        lax.psum_scatter(gain_two_grad, ("dp", "fsdp"), scatter_dimension=0, tiled=True),
        lax.psum_scatter(shift_two_grad, ("dp", "fsdp"), scatter_dimension=0, tiled=True),
        lax.psum_scatter(up_grad_turned, ("dp", "fsdp"), scatter_dimension=0, tiled=True),
        lax.psum_scatter(up_bias_grad, ("dp", "fsdp"), scatter_dimension=0, tiled=True),
        lax.psum_scatter(down_grad, ("dp", "fsdp"), scatter_dimension=0, tiled=True),
        lax.psum_scatter(down_bias_grad, ("dp", "fsdp"), scatter_dimension=0, tiled=True),
    )
    summed = (
        parts[0],
        parts[1],
        parts[2].T,
        parts[3].T,
        parts[4],
        parts[5],
        parts[6],
        parts[7],
        parts[8].T,
        parts[9],
        parts[10],
        parts[11],
    )
    return (layer_out, input_grad) + tuple(summed) + (row_share, col_share)


def solution(mesh):
    in_specs = (
        P(("dp", "fsdp"), None),
        P(("dp", "fsdp")),
        P(("dp", "fsdp")),
        P(("dp", "fsdp")),
        P(("dp", "fsdp")),
        P(("dp", "fsdp")),
        P(None, ("dp", "fsdp")),
        P(None, ("dp", "fsdp")),
        P(("dp", "fsdp"), None),
        P(("dp", "fsdp")),
        P(("dp", "fsdp")),
        P(("dp", "fsdp")),
        P(None, ("dp", "fsdp")),
        P(("dp", "fsdp")),
        P(("dp", "fsdp"), None),
        P(("dp", "fsdp")),
        P("fsdp", None),
        P("fsdp", None),
        P(("dp", "fsdp"), None),
    )
    out_specs = (
        P(("dp", "fsdp"), None),
        P(("dp", "fsdp"), None),
        P(("dp", "fsdp")),
        P(("dp", "fsdp")),
        P(None, ("dp", "fsdp")),
        P(None, ("dp", "fsdp")),
        P(("dp", "fsdp"), None),
        P(("dp", "fsdp")),
        P(("dp", "fsdp")),
        P(("dp", "fsdp")),
        P(None, ("dp", "fsdp")),
        P(("dp", "fsdp")),
        P(("dp", "fsdp"), None),
        P(("dp", "fsdp")),
        P("fsdp", None),
        P("fsdp", None),
    )
    return jax.shard_map(local, mesh=mesh, in_specs=in_specs, out_specs=out_specs, check_vma=False)
```

profile of v0, /device:TPU:0, one launch (start us, length us, event | category | flops | bytes accessed | tf_op | source)
XLA Modules:
  0.0 2429.8 jit_solution(9523614264824253196)
XLA Ops:
  19.3 57.8 %gather_fusion = bf16[16384,4]{1,0:T(8,128)(2,1)} fusion(bf16[4,63]{0,1:T(8,128)(2,1)S(1)} %copy.337, s32[16384]{0:T(1024)S(1)} %broadcast_clamp_fusion.3), kind=kCustom, calls=%fused_computation.clone | custom fusion | bytes 327680 | tf_op jit(solution)/shard_map/while/body/eval_jaxpr/jit(_take)/gather | solution.py:137
  77.1 57.8 %gather_fusion.4 = bf16[16384,4]{1,0:T(8,128)(2,1)} fusion(bf16[4,63]{0,1:T(8,128)(2,1)S(1)} %copy.339, s32[16384]{0:T(1024)S(1)} %broadcast_clamp_fusion.3), kind=kCustom, calls=%fused_computation.4.clone | custom fusion | bytes 327680 | tf_op jit(solution)/shard_map/while/body/eval_jaxpr/jit(_take)/gather | solution.py:137
  135.2 57.8 %gather_fusion.2 = bf16[16384,4]{1,0:T(8,128)(2,1)} fusion(bf16[4,63]{0,1:T(8,128)(2,1)S(1)} %copy.337, s32[16384]{0:T(1024)S(1)} %broadcast_clamp_fusion.1), kind=kCustom, calls=%fused_computation.2.clone | custom fusion | bytes 327680 | tf_op jit(solution)/shard_map/while/body/eval_jaxpr/jit(_take)/gather | solution.py:137
  193.0 57.8 %gather_fusion.6 = bf16[16384,4]{1,0:T(8,128)(2,1)} fusion(bf16[4,63]{0,1:T(8,128)(2,1)S(1)} %copy.339, s32[16384]{0:T(1024)S(1)} %broadcast_clamp_fusion.1), kind=kCustom, calls=%fused_computation.6.clone | custom fusion | bytes 327680 | tf_op jit(solution)/shard_map/while/body/eval_jaxpr/jit(_take)/gather | solution.py:137
  250.9 57.8 %gather_fusion.8 = bf16[16384,4]{1,0:T(8,128)(2,1)} fusion(bf16[4,63]{0,1:T(8,128)(2,1)S(1)} %copy.341, s32[16384]{0:T(1024)S(1)} %broadcast_clamp_fusion.3), kind=kCustom, calls=%fused_computation.8.clone | custom fusion | bytes 327680 | tf_op jit(solution)/shard_map/while/body/eval_jaxpr/jit(_take)/gather | solution.py:137
  308.7 57.7 %gather_fusion.10 = bf16[16384,4]{1,0:T(8,128)(2,1)} fusion(bf16[4,63]{0,1:T(8,128)(2,1)S(1)} %copy.341, s32[16384]{0:T(1024)S(1)} %broadcast_clamp_fusion.1), kind=kCustom, calls=%fused_computation.10.clone | custom fusion | bytes 327680 | tf_op jit(solution)/shard_map/while/body/eval_jaxpr/jit(_take)/gather | solution.py:137
  366.6 57.8 %gather_fusion.12 = bf16[16384,4]{1,0:T(8,128)(2,1)} fusion(bf16[4,63]{0,1:T(8,128)(2,1)S(1)} %copy.343, s32[16384]{0:T(1024)S(1)} %broadcast_clamp_fusion.3), kind=kCustom, calls=%fused_computation.12.clone | custom fusion | bytes 327680 | tf_op jit(solution)/shard_map/while/body/eval_jaxpr/jit(_take)/gather | solution.py:137
  424.4 57.8 %gather_fusion.14 = bf16[16384,4]{1,0:T(8,128)(2,1)} fusion(bf16[4,63]{0,1:T(8,128)(2,1)S(1)} %copy.343, s32[16384]{0:T(1024)S(1)} %broadcast_clamp_fusion.1), kind=kCustom, calls=%fused_computation.14.clone | custom fusion | bytes 327680 | tf_op jit(solution)/shard_map/while/body/eval_jaxpr/jit(_take)/gather | solution.py:137
  487.1 57.8 %gather_fusion.1 = bf16[16384,4]{1,0:T(8,128)(2,1)} fusion(bf16[4,63]{0,1:T(8,128)(2,1)S(1)} %copy.338, s32[16384]{0:T(1024)S(1)} %broadcast_clamp_fusion.2), kind=kCustom, calls=%fused_computation.1.clone | custom fusion | bytes 327680 | tf_op jit(solution)/shard_map/while/body/eval_jaxpr/jit(_take)/gather | solution.py:138
  544.9 57.8 %gather_fusion.5 = bf16[16384,4]{1,0:T(8,128)(2,1)} fusion(bf16[4,63]{0,1:T(8,128)(2,1)S(1)} %copy.340, s32[16384]{0:T(1024)S(1)} %broadcast_clamp_fusion.2), kind=kCustom, calls=%fused_computation.5.clone | custom fusion | bytes 327680 | tf_op jit(solution)/shard_map/while/body/eval_jaxpr/jit(_take)/gather | solution.py:138
  602.9 57.8 %gather_fusion.3 = bf16[16384,4]{1,0:T(8,128)(2,1)} fusion(bf16[4,63]{0,1:T(8,128)(2,1)S(1)} %copy.338, s32[16384]{0:T(1024)S(1)} %broadcast_clamp_fusion), kind=kCustom, calls=%fused_computation.3.clone | custom fusion | bytes 327680 | tf_op jit(solution)/shard_map/while/body/eval_jaxpr/jit(_take)/gather | solution.py:138
  660.7 57.8 %gather_fusion.7 = bf16[16384,4]{1,0:T(8,128)(2,1)} fusion(bf16[4,63]{0,1:T(8,128)(2,1)S(1)} %copy.340, s32[16384]{0:T(1024)S(1)} %broadcast_clamp_fusion), kind=kCustom, calls=%fused_computation.7.clone | custom fusion | bytes 327680 | tf_op jit(solution)/shard_map/while/body/eval_jaxpr/jit(_take)/gather | solution.py:138
  718.7 57.8 %gather_fusion.9 = bf16[16384,4]{1,0:T(8,128)(2,1)} fusion(bf16[4,63]{0,1:T(8,128)(2,1)S(1)} %copy.342, s32[16384]{0:T(1024)S(1)} %broadcast_clamp_fusion.2), kind=kCustom, calls=%fused_computation.9.clone | custom fusion | bytes 327680 | tf_op jit(solution)/shard_map/while/body/eval_jaxpr/jit(_take)/gather | solution.py:138
  776.4 57.8 %gather_fusion.11 = bf16[16384,4]{1,0:T(8,128)(2,1)} fusion(bf16[4,63]{0,1:T(8,128)(2,1)S(1)} %copy.342, s32[16384]{0:T(1024)S(1)} %broadcast_clamp_fusion), kind=kCustom, calls=%fused_computation.11.clone | custom fusion | bytes 327680 | tf_op jit(solution)/shard_map/while/body/eval_jaxpr/jit(_take)/gather | solution.py:138
  834.4 57.8 %gather_fusion.13 = bf16[16384,4]{1,0:T(8,128)(2,1)} fusion(bf16[4,63]{0,1:T(8,128)(2,1)S(1)} %copy.344, s32[16384]{0:T(1024)S(1)} %broadcast_clamp_fusion.2), kind=kCustom, calls=%fused_computation.13.clone | custom fusion | bytes 327680 | tf_op jit(solution)/shard_map/while/body/eval_jaxpr/jit(_take)/gather | solution.py:138
  892.3 57.8 %gather_fusion.15 = bf16[16384,4]{1,0:T(8,128)(2,1)} fusion(bf16[4,63]{0,1:T(8,128)(2,1)S(1)} %copy.344, s32[16384]{0:T(1024)S(1)} %broadcast_clamp_fusion), kind=kCustom, calls=%fused_computation.15.clone | custom fusion | bytes 327680 | tf_op jit(solution)/shard_map/while/body/eval_jaxpr/jit(_take)/gather | solution.py:138
  951.9 42.7 %all-reduce.20 = (bf16[1152]{0:T(1024)(128)(2,1)S(1)}, bf16[1152]{0:T(1024)(128)(2,1)S(1)}, bf16[1152]{0:T(1024)(128)(2,1)}, bf16[1152]{0:T(1024)(128)(2,1)}, bf...) all-reduce(bf16[1152]{0:T(1024)(128)(2,1)S(1)} %dynamic-update-slic, ...), channel_id=1, replica_groups=mesh['dp'=16,'fsdp'=2] {'dp','fsdp'}, use_global_device_ids=true, to_apply=%add.1 | all-reduce | flops 11520 | bytes 46080
  1071.6 5.6 copy.287
  1106.4 6.5 fusion.163
  1112.9 9.3 reshape.693
  1122.2 15.6 fusion.301
  1141.9 5.7 fusion.36
  1155.4 5.8 fusion.194
  1196.6 6.4 fusion.345
  1284.8 59.9 %multiply_convert_fusion = (bf16[1024,4608]{1,0:T(8,128)(2,1)}, f32[1024,4608]{1,0:T(8,128)}, f32[1024,4608]{1,0:T(8,128)}) fusion(f32[4608]{0:T(1024)S(1)} %copy-done.132, bf16[1152,4608]{0,1:T(8,128)(2,1)} %all-gather.10.cloned.1.call-done, f32[1024,1152]{1,0:T(8,128)} %copy-done.42, f32[1152]{0:T(1024)S(1)} %copy-done.138, f32[1152]{0:T(1024)S(1)} %copy-done.129, ...), kind=kOutput, calls=%fused_computation.20 | convolution fusion | flops 11188961280 | bytes 62557184 | tf_op jit(solution)/shard_map/dot_general | solution.py:210
  1344.8 26.5 %convert_reduce_fusion = (f32[4608]{0:T(1024)}, bf16[1024,4608]{1,0:T(8,128)(2,1)}) fusion(f32[1024,4608]{1,0:T(8,128)} %get-tuple-element.141, bf16[4608,1152]{1,0:T(8,128)(2,1)} %all-gather.12.cloned.1.call-done, bf16[1024,1152]{1,0:T(8,128)(2,1)S(1)} %copy-done.50, f32[1024]{0:T(1024)S(1)} %copy-done.119, f32[1024,4608]{1,0:T(8,128)} %get-tuple-element.204, ...), kind=kOutput, calls=%fused_computation.18 | convolution fusion | flops 10955386880 | bytes 60203008 | tf_op jit(solution)/shard_map/dot_general | solution.py:252
  1371.3 20.1 multiply_reduce_fusion.8
  1406.5 8.8 multiply_reduce_fusion.6
  1415.3 6.1 fusion.52
  1421.4 7.5 multiply_reduce_fusion.4
  1438.4 8.1 multiply_reduce_fusion
  1469.4 5.8 multiply_convert_fusion.5
  1479.8 6.7 multiply_reduce_fusion.5
  1493.3 7.5 multiply_convert_fusion.3
  1504.5 6.7 multiply_reduce_fusion.3
  1519.2 6.7 multiply_convert_fusion.1
  1529.6 8.8 multiply_reduce_fusion.1
  1538.4 7.0 multiply_convert_fusion.2
  1568.0 7.5 fusion.272
  1576.3 21.2 fusion.304
  1599.2 20.0 fusion.156
  1646.2 18.4 fusion.73
  1664.6 598.2 %fusion.327 = (f32[112,1152]{1,0:T(8,128)S(1)}, f32[48,1152]{1,0:T(8,128)S(1)}) fusion(f32[3456,1152]{1,0:T(8,128)} %fusion.73, f32[1152,1152]{1,0:T(8,128)} %fusion.347), kind=kCustom, calls=%all-reduce-scatter.2 | all-reduce-scatter fusion | flops 5898242 | bytes 21970944
  2263.6 12.8 collective-permute-start.2
  2308.2 15.7 fusion.326
  2330.8 18.8 fusion.72
  2351.4 39.5 %all-reduce.19 = (f32[1152]{0:T(1024)S(1)}, f32[1152]{0:T(1024)S(1)}, f32[1152]{0:T(1024)S(1)}, f32[1152]{0:T(1024)S(1)}, f32[1152]{0:T(1024)S(1)}, /*index=5*/f...) all-reduce(f32[1152]{0:T(1024)S(1)} %get-tuple-element.92, ...), channel_id=2, replica_groups=mesh['dp'=16,'fsdp'=2] {'dp','fsdp'}, use_global_device_ids=true, to_apply=%region_34.36.clone | all-reduce | flops 13536 | bytes 108288
  2413.0 5.9 concatenate.165
  (659 shorter events, 445.9 us)
Async XLA Ops:
  7.2 1090.1 %all-gather.16.cloned.1.call-start = ((), (), s32[]{:S(2)}) async-start(), calls=%async_computation.9 | async-start | bytes 3041280 | tf_op jit(solution)/shard_map/all_gather | solution.py:69
  7.9 1094.5 %all-gather.8.cloned.1.call-start = ((), (), s32[]{:S(2)}) async-start(), calls=%async_computation.3 | async-start | bytes 5474304 | tf_op jit(solution)/shard_map/all_gather | solution.py:68
  8.7 1104.2 %all-gather.14.cloned.1.call-start = ((), (), s32[]{:S(2)}) async-start(), calls=%async_computation.8 | async-start | bytes 8515584 | tf_op jit(solution)/shard_map/all_gather | solution.py:67
  9.4 1275.4 %all-gather.10.cloned.1.call-start = ((), (), s32[]{:S(2)}) async-start(), calls=%async_computation.4 | async-start | bytes 10948608 | tf_op jit(solution)/shard_map/all_gather | solution.py:73
  10.0 1334.8 %all-gather.12.cloned.1.call-start = ((), (), s32[]{:S(2)}) async-start(), calls=%async_computation.5 | async-start | bytes 10948608 | tf_op jit(solution)/shard_map/all_gather | solution.py:75
  10.6 2412.2 %reduce-scatter.14.cloned.1.call-start = ((), (), s32[]{:S(2)}) async-start(), calls=%async_computation.10 | async-start | bytes 10948608
  12.7 1093.7 %copy-start.86 = (s32[1024]{0:T(1024)}, s32[1024]{0:T(1024)S(1)}, u32[]{:S(2)}) copy-start(s32[1024]{0:T(1024)S(1)} %fusion.278) | copy-start | bytes 12292
  13.4 1241.2 %copy-start.46 = (pred[1024,32]{0,1:T(32,128)(4,1)}, pred[1024,32]{0,1:T(32,128)(4,1)S(1)}, u32[]{:S(2)}) copy-start(pred[1024,32]{0,1:T(32,128)(4,1)S(1)} %get-tuple-element.225) | copy-start | bytes 98308
  13.4 1241.2 %copy-start.48 = (pred[1024,32]{0,1:T(32,128)(4,1)}, pred[1024,32]{0,1:T(32,128)(4,1)S(1)}, u32[]{:S(2)}) copy-start(pred[1024,32]{0,1:T(32,128)(4,1)S(1)} %get-tuple-element.226) | copy-start | bytes 98308
  366.6 115.9 %copy-start.144 = (bf16[8,63]{1,0:T(8,128)(2,1)S(1)}, bf16[8,63]{1,0:T(8,128)(2,1)}, u32[]{:S(2)}) copy-start(bf16[8,63]{1,0:T(8,128)(2,1)} %param.38) | copy-start | bytes 3028
  834.3 115.8 %copy-start.145 = (bf16[36]{0:T(256)(128)(2,1)S(1)}, bf16[36]{0:T(256)(128)(2,1)}, u32[]{:S(2)}) copy-start(bf16[36]{0:T(256)(128)(2,1)} %param.25) | copy-start | bytes 220
  834.3 116.0 %copy-start.146 = (bf16[36]{0:T(256)(128)(2,1)S(1)}, bf16[36]{0:T(256)(128)(2,1)}, u32[]{:S(2)}) copy-start(bf16[36]{0:T(256)(128)(2,1)} %param.26) | copy-start | bytes 220
  834.4 116.3 %copy-start.147 = (bf16[36]{0:T(256)(128)(2,1)S(1)}, bf16[36]{0:T(256)(128)(2,1)}, u32[]{:S(2)}) copy-start(bf16[36]{0:T(256)(128)(2,1)} %param.30) | copy-start | bytes 220
  834.4 116.5 %copy-start.148 = (bf16[36]{0:T(256)(128)(2,1)S(1)}, bf16[36]{0:T(256)(128)(2,1)}, u32[]{:S(2)}) copy-start(bf16[36]{0:T(256)(128)(2,1)} %param.31) | copy-start | bytes 220
  834.4 116.7 %copy-start.149 = (bf16[36]{0:T(256)(128)(2,1)S(1)}, bf16[36]{0:T(256)(128)(2,1)}, u32[]{:S(2)}) copy-start(bf16[36]{0:T(256)(128)(2,1)} %param.32) | copy-start | bytes 220
  834.4 117.0 %copy-start.150 = (bf16[36]{0:T(256)(128)(2,1)S(1)}, bf16[36]{0:T(256)(128)(2,1)}, u32[]{:S(2)}) copy-start(bf16[36]{0:T(256)(128)(2,1)} %param.36) | copy-start | bytes 220
  834.4 117.2 %copy-start.151 = (bf16[144]{0:T(256)(128)(2,1)S(1)}, bf16[144]{0:T(256)(128)(2,1)}, u32[]{:S(2)}) copy-start(bf16[144]{0:T(256)(128)(2,1)} %param.34) | copy-start | bytes 868
  834.4 160.8 %copy-start.30 = (bf16[1024,1152]{1,0:T(8,128)(2,1)S(1)}, bf16[1024,1152]{1,0:T(8,128)(2,1)}, u32[]{:S(2)}) copy-start(bf16[1024,1152]{1,0:T(8,128)(2,1)} %param.21) | copy-start | bytes 7077892
  892.3 104.7 %copy-start.152 = (s32[4]{0:T(128)S(1)}, s32[4]{0:T(128)}, u32[]{:S(2)}) copy-start(s32[4]{0:T(128)} %param.23) | copy-start | bytes 52
  994.6 127.6 %copy-start.109 = (f32[1152]{0:T(1024)}, f32[1152]{0:T(1024)S(1)}, u32[]{:S(2)}) copy-start(f32[1152]{0:T(1024)S(1)} %convert_element_type.195) | copy-start | bytes 13828
  995.6 126.6 %copy-start.111 = (f32[1024]{0:T(1024)}, f32[1024]{0:T(1024)S(1)}, u32[]{:S(2)}) copy-start(f32[1024]{0:T(1024)S(1)} %broadcast_multiply_fusion.1) | copy-start | bytes 12292
  1112.9 29.0 %slice-start.16 = ((s8[9437184]{0:T(1024)(128)(4,1)}), s8[1048576]{0:T(1024)(128)(4,1)S(1)}, s32[]{:S(2)}) async-start(s8[9437184]{0:T(1024)(128)(4,1)} %bitcast.268), calls=%async_computation.27 | async-start | bytes 2097152
  1122.2 19.7 slice-start.17
  1150.5 38.6 %copy-start.33 = (bf16[1024,1152]{0,1:T(8,128)(2,1)}, bf16[1024,1152]{0,1:T(8,128)(2,1)S(1)}, u32[]{:S(2)}) copy-start(bf16[1024,1152]{0,1:T(8,128)(2,1)S(1)} %copy.244) | copy-start | bytes 7077892
  1196.5 35.0 %copy-start.37 = (bf16[1024,1152]{0,1:T(8,128)(2,1)}, bf16[1024,1152]{0,1:T(8,128)(2,1)S(1)}, u32[]{:S(2)}) copy-start(bf16[1024,1152]{0,1:T(8,128)(2,1)S(1)} %copy.243) | copy-start | bytes 7077892
  1277.1 114.3 %copy-start.127 = (f32[1024]{0:T(1024)}, f32[1024]{0:T(1024)S(1)}, u32[]{:S(2)}) copy-start(f32[1024]{0:T(1024)S(1)} %broadcast_multiply_fusion) | copy-start | bytes 12292
  1279.9 111.5 %copy-start.134 = (f32[1024]{0:T(1024)}, f32[1024]{0:T(1024)S(1)}, u32[]{:S(2)}) copy-start(f32[1024]{0:T(1024)S(1)} %fusion.284) | copy-start | bytes 12292
  1284.8 60.0 %copy-start.50 = (bf16[1024,1152]{1,0:T(8,128)(2,1)S(1)}, bf16[1024,1152]{1,0:T(8,128)(2,1)}, u32[]{:S(2)}) copy-start(bf16[1024,1152]{1,0:T(8,128)(2,1)} %param.39) | copy-start | bytes 7077892
  1284.8 60.0 %copy-start.119 = (f32[1024]{0:T(1024)S(1)}, f32[1024]{0:T(1024)}, u32[]{:S(2)}) copy-start(f32[1024]{0:T(1024)} %get-tuple-element.138) | copy-start | bytes 12292
  1371.3 20.1 copy-start.126
  1371.3 20.1 copy-start.43
  1575.6 847.2 %reduce-scatter.10.cloned.1.call-start = ((), (), s32[]{:S(2)}) async-start(), calls=%async_computation.6 | async-start | bytes 21897216 | tf_op jit(solution)/shard_map/reduce_scatter | solution.py:427
  1597.5 825.2 %reduce-scatter.12.cloned.1.call-start = ((), (), s32[]{:S(2)}) async-start(), calls=%async_computation.7 | async-start | bytes 21897216 | tf_op jit(solution)/shard_map/reduce_scatter | solution.py:429
  2262.9 33.9 %copy-start.22 = (bf16[4,512,1024]{2,1,0:T(8,128)(2,1)S(1)}, bf16[4,512,1024]{2,1,0:T(8,128)(2,1)}, u32[]{:S(2)}) copy-start(bf16[4,512,1024]{2,1,0:T(8,128)(2,1)} %copy-done.20) | copy-start | bytes 12582916
  2263.6 135.5 %collective-permute-start.2 = (f32[48,1152]{1,0:T(8,128)S(1)}, f32[48,1152]{1,0:T(8,128)S(1)}, u32[]{:S(2)}, u32[]{:S(2)}) collective-permute-start(f32[48,1152]{1,0:T(8,128)S(1)} %get-tuple-element.133), channel_id=1, source_target_pairs={{0,1},{1,2},{2,3},{3,4},{4,5},{5,6},{6,7},{7,8},{8,9},{9,10},{10,1... | collective-permute-start | bytes 663560
  2276.4 127.8 %collective-permute-start.3 = (f32[48,1152]{1,0:T(8,128)S(1)}, f32[48,1152]{1,0:T(8,128)}, u32[]{:S(2)}, u32[]{:S(2)}) collective-permute-start(f32[48,1152]{1,0:T(8,128)S(1)} %get-tuple-element.133), channel_id=1, source_target_pairs={{0,2},{1,3},{2,4},{3,5},{4,6},{5,7},{6,8},{7,9},{8,10},{9,11},{10,... | collective-permute-start | bytes 663560
  2279.7 125.9 %collective-permute-start.4 = (f32[48,1152]{1,0:T(8,128)S(1)}, f32[48,1152]{1,0:T(8,128)}, u32[]{:S(2)}, u32[]{:S(2)}) collective-permute-start(f32[48,1152]{1,0:T(8,128)S(1)} %get-tuple-element.133), channel_id=1, source_target_pairs={{0,3},{1,4},{2,5},{3,6},{4,7},{5,8},{6,9},{7,10},{8,11},{9,12},{10... | collective-permute-start | bytes 663560
  2284.4 110.6 %collective-permute-start.9 = (f32[36,1152]{1,0:T(8,128)}, f32[36,1152]{1,0:T(8,128)}, u32[]{:S(2)}, u32[]{:S(2)}) collective-permute-start(f32[36,1152]{1,0:T(8,128)} %slice.483), channel_id=1, source_target_pairs={{0,8},{1,9},{2,10},{3,11},{4,12},{5,13},{6,14},{7,15},{8,16},{9,17... | collective-permute-start | bytes 497672
  2288.4 131.2 %collective-permute-start = (f32[112,1152]{1,0:T(8,128)S(1)}, f32[112,1152]{1,0:T(8,128)}, u32[]{:S(2)}, u32[]{:S(2)}) collective-permute-start(f32[112,1152]{1,0:T(8,128)S(1)} %get-tuple-element.132), channel_id=1, source_target_pairs={{0,1},{1,2},{2,3},{3,4},{4,5},{5,6},{6,7},{7,8},{8,9},{9,10},{10,1... | collective-permute-start | bytes 1548296
  2330.8 20.6 copy-start.131
  2330.8 20.6 copy-start.133
  2330.8 20.6 copy-start.141
  2330.8 20.6 copy-start.142
  2395.0 15.3 collective-permute-start.5
  2399.1 13.2 collective-permute-start.6
  2404.2 8.1 collective-permute-start.7
  2405.6 7.4 collective-permute-start.8
  2410.3 9.3 collective-permute-start.1
  (160 other events, 822.9 us)
Sparse Core Ops, SparseCore 0:
  10.9 61.5 all-gather.15
  75.4 64.3 all-gather.7
  142.8 75.6 all-gather.13
  221.3 85.9 all-gather.9
  310.0 85.8 all-gather.11
  1575.7 149.6 reduce-scatter.13
  1732.3 268.8 reduce-scatter.9
  2009.4 268.1 reduce-scatter.11
where the time goes:
time: 2440 us; the launch traced here: 2430 us
  local copies, waits for them, and re-layouts  1100 us (45%)
  blocking collectives  690 us (28%)
  matrix products  464 us (19%)
  other arithmetic  109 us (4%)
  starting transfers between devices  45.8 us (2%)
    unnamed x3, blocking collectives  680 us
    gather x16, local copies, waits for them, and re-layouts, scores(): jnp.take(col_full[head_start:head_start + head_group], col_choice, axis=1)  504 us
    gather x16, local copies, waits for them, and re-layouts, scores(): jnp.take(row_full[head_start:head_start + head_group], row_choice, axis=1)  503 us
    unnamed x416, local copies, waits for them, and re-layouts  69.3 us
    dot_general x1, matrix products, local(): jnp.dot(normed_two, w_up, preferred_element_type=jnp.float32)  59.9 us
    dot_general x8, matrix products, frame_backward(): jnp.einsum('qhd,khd->hqk', grad_block, value_frame[:, head_start:head_end...  55.2 us
  transfers between devices with their start and end apart: 18, of which 0 were waited for; matrix products, arithmetic and copies ran while one was open for 83% of the time, Pallas kernels for 0%

commit v1 on v0

v1 whole, which is shorter than its diff:
```python
import functools
import math

import jax
import jax.numpy as jnp
from jax import lax
from jax.experimental import pallas as pl
from jax.experimental.pallas import tpu as pltpu
from jax.sharding import PartitionSpec as P

HEADS = 16
GRID = 32
SMALL = 16
AXES = ("dp", "fsdp")
LANES = 128
PIECE = 48
BIG = -1e30
F32 = jnp.float32
BF16 = jnp.bfloat16
HIGHEST = lax.Precision.HIGHEST
MESH_ID = pl.DeviceIdType.MESH
VMEM_LIMIT = 60 * 1024 * 1024


def dot_nn(a, b):
    return lax.dot_general(a, b, (((1,), (0,)), ((), ())), preferred_element_type=F32)


def dot_nt(a, b):
    return lax.dot_general(a, b, (((1,), (1,)), ((), ())), preferred_element_type=F32)


def dot_tn(a, b):
    return lax.dot_general(a, b, (((0,), (0,)), ((), ())), preferred_element_type=F32)


def params(**more):
    return pltpu.CompilerParams(vmem_limit_bytes=VMEM_LIMIT, **more)


def resident(shape):
    zeros = (0,) * len(shape)
    return pl.BlockSpec(shape, lambda *_: zeros, pipeline_mode=pl.Buffered(1))


def split_dp(dp):
    g2 = 1 if dp <= 16 else 4
    return dp // 4 // g2, g2


class Place:
    def __init__(self, dims):
        self.G1, self.G2 = dims
        dp, self.q = lax.axis_index("dp"), lax.axis_index("fsdp")
        self.c = dp % 2
        rest = dp // 2
        self.g2 = rest % self.G2
        rest = rest // self.G2
        self.p = rest % 2
        self.g1 = rest // 2
        c, p, q = self.c, self.p, self.q
        self.ap, self.aq = (1 - p) * (1 - c) + p * c, q * (1 - c) + (1 - q) * c
        self.bp, self.bq = p * (1 - c) + (1 - p) * c, (1 - q) * (1 - c) + q * c
        self.whole = (pl.ds(0, self.G1), pl.ds(0, self.G2))

    def device(self, g1, p, g2, c, q):
        return (((g1 * 2 + p) * self.G2 + g2) * 2 + c, q)

    def line(self):
        found = []
        for step in range(1, self.G1 * self.G2):
            found.append(((self.g1 + step // self.G2) % self.G1, (self.g2 + step % self.G2) % self.G2))
        return found

    def on_line(self, spot):
        return self.device(spot[0], self.p, spot[1], self.c, self.q)

    def first(self):
        return self.device(self.g1, self.ap, self.g2, self.c, self.aq)

    def second(self):
        return self.device(self.g1, self.bp, self.g2, self.c, self.bq)

    def sibling(self):
        return self.device(self.g1, self.p, self.g2, 1 - self.c, self.q)

    def barrier(self):
        partners = [self.on_line(spot) for spot in self.line()] + [self.first(), self.second(), self.sibling()]
        semaphore = pltpu.get_barrier_semaphore()
        for partner in partners:
            pl.semaphore_signal(semaphore, inc=1, device_id=partner, device_id_type=MESH_ID)
        pl.semaphore_wait(semaphore, len(partners))


def wait_for(view, semaphore):
    pltpu.make_async_copy(view, view, semaphore).wait()


class Gather:
    STAGES = 5

    def __init__(self, dims, pieces, sources, results, sems, own_sems):
        self.at = Place(dims)
        self.pieces, self.sources, self.results = pieces, sources, results
        self.sems, self.own_sems = sems, own_sems

    @staticmethod
    def scratch(dims, pieces):
        return [
            pltpu.SemaphoreType.DMA((len(pieces), 7 + dims[0] * dims[1], 2)),
            pltpu.SemaphoreType.DMA((len(pieces),)),
        ]

    def send(self, k, kind, source, target, to):
        pltpu.make_async_remote_copy(
            src_ref=source,
            dst_ref=target,
            send_sem=self.sems.at[k, kind, 0],
            recv_sem=self.sems.at[k, kind, 1],
            device_id=to,
            device_id_type=MESH_ID,
        ).start()

    def finish(self, k, kind, view):
        wait_for(view, self.sems.at[k, kind, 1])
        wait_for(view, self.sems.at[k, kind, 0])

    def stage(self, k, number):
        at = self.at
        array, start = self.pieces[k]
        rows = pl.ds(start, PIECE)
        result = self.results[array]
        every, every2 = at.whole
        source = self.sources[array].at[rows]
        own = result.at[at.g1, at.p, at.g2, at.c, at.q, rows]

        def plane(p, q):
            return result.at[every, p, every2, at.c, q, rows]

        if number == 0:
            pltpu.make_async_copy(source, own, self.own_sems.at[k]).start()
            for i, spot in enumerate(at.line()):
                self.send(k, 8 + i, source, own, at.on_line(spot))
        if number == 1:
            pltpu.make_async_copy(source, own, self.own_sems.at[k]).wait()
            for i in range(len(at.line())):
                self.finish(k, 8 + i, own)
            mine = plane(at.p, at.q)
            self.send(k, 1, mine, mine, at.first())
            self.send(k, 3, mine, mine, at.sibling())
        if number == 2:
            mine, came = plane(at.p, at.q), plane(at.ap, at.aq)
            self.finish(k, 1, came)
            self.send(k, 2, mine, mine, at.second())
            self.send(k, 4, came, came, at.second())
            self.send(k, 5, came, came, at.sibling())
        if number == 3:
            for kind, came in ((2, plane(at.bp, at.bq)), (4, plane(1 - at.p, 1 - at.q))):
                self.finish(k, kind, came)
                self.send(k, 6 + kind // 4, came, came, at.sibling())
        if number == 4:
            for kind in (3, 5, 6, 7):
                self.finish(k, kind, plane(at.p, at.q))

    def round(self, number):
        for k in range(len(self.pieces)):
            if 0 <= number - k < self.STAGES:
                self.stage(k, number - k)

    def rounds(self):
        return len(self.pieces) + self.STAGES - 1


class Scatter:
    STAGES = 5

    def __init__(self, dims, pieces, sources, results, held, from_core, from_second, from_first, from_line, sems):
        self.at = Place(dims)
        self.pieces, self.sources, self.results = pieces, sources, results
        self.held, self.from_core, self.from_second = held, from_core, from_second
        self.from_first, self.from_line, self.sems = from_first, from_line, sems

    @staticmethod
    def scratch(dims, pieces, width):
        G1, G2 = dims
        n = len(pieces)
        return [
            pltpu.VMEM((n, G1, 2, G2, 2, PIECE, width), BF16),
            pltpu.VMEM((n, G1, 2, G2, 2, PIECE, width), BF16),
            pltpu.VMEM((n, 2, G1, G2, PIECE, width), BF16),
            pltpu.VMEM((n, G1, G2, PIECE, width), BF16),
            pltpu.VMEM((n, G1 * G2 - 1, PIECE, width), BF16),
            pltpu.SemaphoreType.DMA((n, 5 + G1 * G2, 2)),
        ]

    def send(self, k, kind, source, target, to):
        pltpu.make_async_remote_copy(
            src_ref=source,
            dst_ref=target,
            send_sem=self.sems.at[k, kind, 0],
            recv_sem=self.sems.at[k, kind, 1],
            device_id=to,
            device_id_type=MESH_ID,
        ).start()

    def add(self, target, addend):
        at = self.at

        def body(i, carry):
            g1, g2 = i // at.G2, i % at.G2
            total = target[g1, g2].astype(F32) + addend[g1, g2].astype(F32)
            target[g1, g2] = total.astype(BF16)
            return carry

        lax.fori_loop(0, at.G1 * at.G2, body, 0)

    def stage(self, k, number):
        at = self.at
        array, start = self.pieces[k]
        rows = pl.ds(start, PIECE)
        source = self.sources[array]
        every, every2 = at.whole
        both = pl.ds(0, 2)
        held = self.held.at[k]

        def plane(p, q):
            return held.at[every, p, every2, q]

        local_copy = lambda: pltpu.make_async_copy(
            source.at[every, both, every2, at.c, both, rows], held, self.sems.at[k, 4, 0]
        )
        if number == 0:
            self.send(k, 0, source.at[every, both, every2, 1 - at.c, both, rows], self.from_core.at[k], at.sibling())
            local_copy().start()
        if number == 1:
            local_copy().wait()
            wait_for(self.from_core.at[k], self.sems.at[k, 0, 1])
            core = self.from_core.at[k]
            for p, q in ((at.bp, at.bq), (1 - at.p, 1 - at.q)):
                self.add(plane(p, q), core.at[every, p, every2, q])
            self.send(k, 1, plane(at.bp, at.bq), self.from_second.at[k, 0], at.second())
            self.send(k, 2, plane(1 - at.p, 1 - at.q), self.from_second.at[k, 1], at.second())
            for p, q in ((at.p, at.q), (at.ap, at.aq)):
                self.add(plane(p, q), core.at[every, p, every2, q])
        if number == 2:
            for kind in (1, 2):
                wait_for(self.from_second.at[k, kind - 1], self.sems.at[k, kind, 1])
            self.add(plane(at.ap, at.aq), self.from_second.at[k, 1])
            self.send(k, 3, plane(at.ap, at.aq), self.from_first.at[k], at.first())
            self.add(plane(at.p, at.q), self.from_second.at[k, 0])
        if number == 3:
            wait_for(self.from_first.at[k], self.sems.at[k, 3, 1])
            self.add(plane(at.p, at.q), self.from_first.at[k])
            for i, spot in enumerate(at.line()):
                self.send(
                    k, 5 + i, held.at[spot[0], at.p, spot[1], at.q], self.from_line.at[k, i], at.on_line(spot)
                )
        if number == 4:
            total = held[at.g1, at.p, at.g2, at.q].astype(F32)
            for i in range(at.G1 * at.G2 - 1):
                wait_for(self.from_line.at[k, i], self.sems.at[k, 5 + i, 1])
                total = total + self.from_line[k, i].astype(F32)
            self.results[array][rows] = total
            wait_for(self.from_core.at[k], self.sems.at[k, 0, 0])
            for kind in (1, 2):
                wait_for(self.from_second.at[k, kind - 1], self.sems.at[k, kind, 0])
            wait_for(self.from_first.at[k], self.sems.at[k, 3, 0])
            for i in range(at.G1 * at.G2 - 1):
                wait_for(self.from_line.at[k, i], self.sems.at[k, 5 + i, 0])

    def round(self, number):
        for k in range(len(self.pieces)):
            if 0 <= number - k < self.STAGES:
                self.stage(k, number - k)

    def rounds(self):
        return len(self.pieces) + self.STAGES - 1


def pieces_of(shards):
    per = [(array, start) for array, shard in enumerate(shards) for start in range(0, shard, PIECE)]
    return sorted(per, key=lambda piece: piece[1])


def pad_rows(shard):
    rows = shard.shape[0]
    return jnp.pad(shard, ((0, -rows % PIECE), (0, 0)))


def gather(shards, dims, collective):
    pieces = pieces_of([shard.shape[0] for shard in shards])
    count = len(shards)

    def kernel(*refs):
        work = Gather(dims, pieces, refs[:count], refs[count : 2 * count], *refs[2 * count :])
        work.at.barrier()
        for number in range(work.rounds()):
            work.round(number)

    G1, G2 = dims
    anywhere = pl.BlockSpec(memory_space=pl.ANY)
    return pl.pallas_call(
        kernel,
        out_shape=[jax.ShapeDtypeStruct((G1, 2, G2, 2, 2) + s.shape, s.dtype) for s in shards],
        in_specs=[anywhere] * count,
        out_specs=[anywhere] * count,
        scratch_shapes=Gather.scratch(dims, pieces),
        compiler_params=params(collective_id=collective, has_side_effects=True),
    )(*shards)


def scatter(parts, dims, collective):
    pieces = pieces_of([part.shape[5] for part in parts])
    count = len(parts)
    width = parts[0].shape[6]

    def kernel(*refs):
        work = Scatter(dims, pieces, refs[:count], refs[count : 2 * count], *refs[2 * count :])
        work.at.barrier()
        for number in range(work.rounds()):
            work.round(number)

    return pl.pallas_call(
        kernel,
        out_shape=[jax.ShapeDtypeStruct(part.shape[5:], F32) for part in parts],
        in_specs=[pl.BlockSpec(memory_space=pl.ANY)] * count,
        out_specs=[pl.BlockSpec(memory_space=pltpu.VMEM)] * count,
        scratch_shapes=Scatter.scratch(dims, pieces, width),
        compiler_params=params(collective_id=collective, has_side_effects=True),
    )(*parts)


def normalise(values):
    centre = values - jnp.mean(values, axis=-1, keepdims=True)
    inverse = lax.rsqrt(jnp.mean(centre * centre, axis=-1, keepdims=True) + 1e-06)
    return centre * inverse, inverse


def norm_back(values, gain, grad):
    unit, inverse = normalise(values)
    scaled = grad * gain
    inner = jnp.mean(scaled, axis=-1, keepdims=True) + unit * jnp.mean(scaled * unit, axis=-1, keepdims=True)
    return inverse * (scaled - inner), unit


def attend_kernel(factor, block, tokens, gain, shift, weight, time_rows, table, onehot, mask_q, mask_k,
                  normed_out, q_out, k_out, v_out, o_out, p_out, keys):
    rows = tokens.shape[0]

    @pl.when(pl.program_id(0) == 0)
    def _():
        for start in range(0, rows, block):
            span = pl.ds(start, block)
            unit, _ = normalise(tokens[span].astype(F32))
            normed_out[span] = (unit * gain[...] + shift[...]).astype(BF16)

    per = time_rows.shape[1] // 2
    slot = rows // per
    for i in range(per):
        span = pl.ds(i * slot, slot)
        qkv = dot_nt(normed_out[span], weight[0])
        q_out[0, span] = (qkv[:, :LANES] + time_rows[0, i : i + 1]).astype(BF16)
        k_out[0, span] = qkv[:, LANES : 2 * LANES].astype(BF16)
        v_out[0, span] = (qkv[:, 2 * LANES :] + time_rows[0, per + i : per + i + 1]).astype(BF16)
    keys[:, :LANES] = k_out[0] + mask_k[...]
    keys[:, LANES:] = onehot[...]
    for start in range(0, rows, block):
        span = pl.ds(start, block)
        bias = dot_nn(onehot[span], table[0]).astype(BF16)
        query = jnp.concatenate([q_out[0, span] + mask_q[span], bias], axis=1)
        scores = dot_nt(query, keys[...])
        top = jnp.max(scores, axis=1, keepdims=True)
        weights = jnp.exp2((scores - top) * factor)
        total = jnp.sum(weights, axis=1, keepdims=True)
        low = (weights * (1.0 / total)).astype(BF16)
        p_out[0, span] = low
        o_out[span] = dot_nn(low, v_out[0]).astype(BF16)


def attend(tokens, gain, shift, weight, time_rows, table, onehot, mask_q, mask_k, factor):
    rows, width = tokens.shape
    block = min(256, rows)
    per_head = lambda *shape: pl.BlockSpec((1,) + shape, lambda h: (h, 0, 0))
    head_rows = jax.ShapeDtypeStruct((HEADS, rows, LANES), BF16)
    return pl.pallas_call(
        functools.partial(attend_kernel, factor, block),
        grid=(HEADS,),
        in_specs=[
            resident(tokens.shape),
            resident(gain.shape),
            resident(shift.shape),
            per_head(3 * LANES, width),
            per_head(*time_rows.shape[1:]),
            per_head(LANES, LANES),
            resident(onehot.shape),
            resident(mask_q.shape),
            resident(mask_k.shape),
        ],
        out_specs=[
            resident(tokens.shape),
            per_head(rows, LANES),
            per_head(rows, LANES),
            per_head(rows, LANES),
            pl.BlockSpec((rows, LANES), lambda h: (0, h)),
            per_head(rows, rows),
        ],
        out_shape=[
            jax.ShapeDtypeStruct(tokens.shape, BF16),
            head_rows,
            head_rows,
            head_rows,
            jax.ShapeDtypeStruct((rows, HEADS * LANES), BF16),
            jax.ShapeDtypeStruct((HEADS, rows, rows), BF16),
        ],
        scratch_shapes=[pltpu.VMEM((rows, 2 * LANES), BF16)],
        compiler_params=params(),
        name="attend",
    )(tokens, gain, shift, weight, time_rows, table, onehot, mask_q, mask_k)


def attend_back_kernel(block, scale, normed, p, q, k, v, do, o, onehot,
                       dqkv_out, dw_out, sums_out, pair_out, keys, grads, dk_sum, dv_sum):
    rows = normed.shape[0]
    lane = lax.broadcasted_iota(jnp.int32, (rows, LANES), 1)
    head = 72
    delta = jnp.sum(do[...].astype(F32) * o[...].astype(F32), axis=1, keepdims=True)
    high = delta.astype(BF16).astype(F32)
    more = jnp.where(lane == head, -high, jnp.where(lane == head + 1, high - delta, 0.0))
    grads[...] = (do[...].astype(F32) + more).astype(BF16)
    values = v[0] + jnp.where((lane == head) | (lane == head + 1), 1.0, 0.0).astype(BF16)
    keys[:, :LANES] = k[0]
    keys[:, LANES:] = onehot[...]
    pair = jnp.zeros((LANES, LANES), F32)
    for start in range(0, rows, block):
        span = pl.ds(start, block)
        centred = dot_nt(grads[span], values)
        ds = (p[0, span].astype(F32) * centred).astype(BF16)
        both = dot_nn(ds, keys[...])
        dqkv_out[span, :LANES] = (both[:, :LANES] * scale).astype(BF16)
        pair = pair + lax.dot_general(
            onehot[span].astype(F32), both[:, LANES:], (((0,), (0,)), ((), ())),
            preferred_element_type=F32, precision=HIGHEST,
        )
        dk = dot_tn(ds, q[0, span])
        dv = dot_tn(p[0, span], do[span])
        if start == 0:
            dk_sum[...] = dk
            dv_sum[...] = dv
        else:
            dk_sum[...] += dk
            dv_sum[...] += dv
    dqkv_out[:, LANES : 2 * LANES] = (dk_sum[...] * scale).astype(BF16)
    dqkv_out[:, 2 * LANES :] = dv_sum[...].astype(BF16)
    pair_out[0] = pair
    per = sums_out.shape[1]
    slot = rows // per
    for i in range(per):
        sums_out[0, i : i + 1] = jnp.sum(
            dqkv_out[pl.ds(i * slot, slot)].astype(F32), axis=0, keepdims=True
        )
    dw_out[0] = dot_tn(dqkv_out[...], normed[...]).astype(BF16)


def attend_back(normed, p, q, k, v, do, o, onehot, scale, per):
    rows, width = normed.shape
    block = min(256, rows)
    per_head = lambda *shape: pl.BlockSpec((1,) + shape, lambda h: (h, 0, 0))
    head_cols = pl.BlockSpec((rows, LANES), lambda h: (0, h))
    return pl.pallas_call(
        functools.partial(attend_back_kernel, block, scale),
        grid=(HEADS,),
        in_specs=[
            resident(normed.shape),
            per_head(rows, rows),
            per_head(rows, LANES),
            per_head(rows, LANES),
            per_head(rows, LANES),
            head_cols,
            head_cols,
            resident(onehot.shape),
        ],
        out_specs=[
            pl.BlockSpec((rows, 3 * LANES), lambda h: (0, h)),
            per_head(3 * LANES, width),
            per_head(per, 3 * LANES),
            per_head(LANES, LANES),
        ],
        out_shape=[
            jax.ShapeDtypeStruct((rows, HEADS * 3 * LANES), BF16),
            jax.ShapeDtypeStruct((HEADS, 3 * LANES, width), BF16),
            jax.ShapeDtypeStruct((HEADS, per, 3 * LANES), F32),
            jax.ShapeDtypeStruct((HEADS, LANES, LANES), F32),
        ],
        scratch_shapes=[
            pltpu.VMEM((rows, 2 * LANES), BF16),
            pltpu.VMEM((rows, LANES), BF16),
            pltpu.VMEM((rows, LANES), F32),
            pltpu.VMEM((rows, LANES), F32),
        ],
        compiler_params=params(),
        name="attend_back",
    )(normed, p, q, k, v, do, o, onehot)


def project_kernel(tokens, o, weight, bias, gain, shift, hidden_out, normed_out):
    hidden = tokens[...].astype(F32) + (dot_nn(o[...], weight[...]) + bias[...])
    hidden_out[...] = hidden
    unit, _ = normalise(hidden)
    normed_out[...] = (unit * gain[...] + shift[...]).astype(BF16)


def project(tokens, o, weight, bias, gain, shift):
    rows, width = tokens.shape
    block = min(256, rows)
    by_rows = lambda cols: pl.BlockSpec((block, cols), lambda i: (i, 0))
    return pl.pallas_call(
        project_kernel,
        grid=(rows // block,),
        in_specs=[by_rows(width), by_rows(o.shape[1]), resident(weight.shape)] + [resident((1, width))] * 3,
        out_specs=[by_rows(width), by_rows(width)],
        out_shape=[jax.ShapeDtypeStruct(tokens.shape, F32), jax.ShapeDtypeStruct(tokens.shape, BF16)],
        compiler_params=params(),
        name="project",
    )(tokens, o, weight, bias, gain, shift)


def normal_parts(u):
    size = jnp.abs(u)
    bell = jnp.exp(-0.5 * u * u)
    t = 1.0 / (1.0 + (0.3275911 * math.sqrt(0.5)) * size)
    poly = t * (
        0.5 * 0.254829592
        + t * (0.5 * -0.284496736 + t * (0.5 * 1.421413741 + t * (0.5 * -1.453152027 + t * (0.5 * 1.061405429))))
    )
    tail = poly * bell
    return jnp.where(u >= 0.0, 1.0 - tail, tail), bell * (1.0 / math.sqrt(2.0 * math.pi))


def mlp_kernel(normed, dy, up, down, bias, y_out, dn_out, dup_out, ddown_out, dbias_out):
    rows = normed.shape[0]
    first = pl.program_id(0) == 0
    u = dot_nt(normed[...], up[...]) + bias[...]
    phi, density = normal_parts(u)
    act = (u * phi).astype(BF16)
    slope = phi + u * density
    du = (slope * dot_nt(dy[...], down[...])).astype(BF16)
    dbias_out[...] = jnp.sum(du.astype(F32), axis=0, keepdims=True)
    y = dot_nn(act, down[...])
    dn = dot_nn(du, up[...])

    @pl.when(first)
    def _():
        y_out[...] = y
        dn_out[...] = dn

    @pl.when(jnp.logical_not(first))
    def _():
        y_out[...] += y
        dn_out[...] += dn

    ddown_out[...] = dot_tn(act, dy[...]).astype(BF16)
    dup_out[...] = dot_tn(du, normed[...]).astype(BF16)


def mlp(normed, dy, up, down, bias):
    rows, width = normed.shape
    units = up.shape[0]
    block = 512
    by_units = pl.BlockSpec((block, width), lambda i: (i, 0))
    by_bias = pl.BlockSpec((1, block), lambda i: (0, i))
    return pl.pallas_call(
        mlp_kernel,
        grid=(units // block,),
        in_specs=[resident(normed.shape), resident(dy.shape), by_units, by_units, by_bias],
        out_specs=[resident(normed.shape), resident(normed.shape), by_units, by_units, by_bias],
        out_shape=[
            jax.ShapeDtypeStruct(normed.shape, F32),
            jax.ShapeDtypeStruct(normed.shape, F32),
            jax.ShapeDtypeStruct(up.shape, BF16),
            jax.ShapeDtypeStruct(down.shape, BF16),
            jax.ShapeDtypeStruct((1, units), F32),
        ],
        compiler_params=params(),
        name="mlp",
    )(normed, dy, up, down, bias)


def turn_kernel(hidden, y, bias, dn, dy, gain, weight, o, out, dh_out, do_out, dw_out, vec_out, dw_sum):
    first = pl.program_id(0) == 0
    last = pl.program_id(0) == pl.num_programs(0) - 1
    out[...] = (hidden[...] + (y[...] + bias[...])).astype(BF16)
    back, unit = norm_back(hidden[...], gain[...], dn[...])
    dyf = dy[...].astype(F32)
    dh = dyf + back
    dh_out[...] = dh
    da = dh.astype(BF16)
    do_out[...] = dot_nt(da, weight[...]).astype(BF16)
    dw = dot_tn(o[...], da)
    sums = jnp.concatenate(
        [
            jnp.sum(dn[...] * unit, axis=0, keepdims=True),
            jnp.sum(dn[...], axis=0, keepdims=True),
            jnp.sum(da.astype(F32), axis=0, keepdims=True),
            jnp.sum(dyf, axis=0, keepdims=True),
        ],
        axis=0,
    )

    @pl.when(first)
    def _():
        dw_sum[...] = dw
        vec_out[...] = sums

    @pl.when(jnp.logical_not(first))
    def _():
        dw_sum[...] += dw
        vec_out[...] += sums

    @pl.when(last)
    def _():
        dw_out[...] = dw_sum[...].astype(BF16)


def turn(hidden, y, bias, dn, dy, gain, weight, o):
    rows, width = hidden.shape
    block = min(256, rows)
    by_rows = lambda cols: pl.BlockSpec((block, cols), lambda i: (i, 0))
    wide = weight.shape[0]
    return pl.pallas_call(
        turn_kernel,
        grid=(rows // block,),
        in_specs=[
            by_rows(width),
            by_rows(width),
            resident((1, width)),
            by_rows(width),
            by_rows(width),
            resident((1, width)),
            resident(weight.shape),
            by_rows(wide),
        ],
        out_specs=[by_rows(width), by_rows(width), by_rows(wide), resident(weight.shape), resident((4, width))],
        out_shape=[
            jax.ShapeDtypeStruct(hidden.shape, BF16),
            jax.ShapeDtypeStruct(hidden.shape, F32),
            jax.ShapeDtypeStruct((rows, wide), BF16),
            jax.ShapeDtypeStruct(weight.shape, BF16),
            jax.ShapeDtypeStruct((4, width), F32),
        ],
        scratch_shapes=[pltpu.VMEM(weight.shape, F32)],
        compiler_params=params(),
        name="turn",
    )(hidden, y, bias, dn, dy, gain, weight, o)


def end_kernel(tokens, dqkv, weight, gain, dh, out, vec_out):
    first = pl.program_id(0) == 0
    dn = dot_nn(dqkv[...], weight[...])
    back, unit = norm_back(tokens[...].astype(F32), gain[...], dn)
    out[...] = (dh[...] + back).astype(BF16)
    sums = jnp.concatenate(
        [jnp.sum(dn * unit, axis=0, keepdims=True), jnp.sum(dn, axis=0, keepdims=True)], axis=0
    )

    @pl.when(first)
    def _():
        vec_out[...] = sums

    @pl.when(jnp.logical_not(first))
    def _():
        vec_out[...] += sums


def end(tokens, dqkv, weight, gain, dh):
    rows, width = tokens.shape
    block = min(256, rows)
    by_rows = lambda cols: pl.BlockSpec((block, cols), lambda i: (i, 0))
    return pl.pallas_call(
        end_kernel,
        grid=(rows // block,),
        in_specs=[
            by_rows(width), by_rows(dqkv.shape[1]), resident(weight.shape), resident((1, width)), by_rows(width)
        ],
        out_specs=[by_rows(width), resident((2, width))],
        out_shape=[jax.ShapeDtypeStruct(tokens.shape, BF16), jax.ShapeDtypeStruct((2, width), F32)],
        compiler_params=params(),
        name="end",
    )(tokens, dqkv, weight, gain, dh)


def time_embed(stamps, feat_width):
    half_width = feat_width // 2
    frequency = jnp.exp(-math.log(10000.0) * jnp.arange(half_width, dtype=F32) / half_width)
    angles = stamps.astype(F32)[:, None] * frequency[None, :]
    return jnp.concatenate([jnp.cos(angles), jnp.sin(angles)], axis=1)


def local(
    tokens,
    image_lengths,
    timesteps,
    patch_cells,
    norm1_gain,
    norm1_bias,
    qkv_weight,
    time_weight,
    out_weight,
    out_bias,
    norm2_gain,
    norm2_bias,
    fc1_weight,
    fc1_bias,
    fc2_weight,
    fc2_bias,
    row_table,
    col_table,
    cotangent,
):
    rows, width = tokens.shape
    head_dim = width // HEADS
    slot_rows = SMALL * SMALL
    per = image_lengths.shape[0]
    assert rows == GRID * GRID and per * slot_rows == rows
    fsdp = lax.axis_size("fsdp")
    devices = lax.axis_size("dp") * fsdp
    dims = split_dp(lax.axis_size("dp"))
    spread = (dims[0], 2, dims[1], 2, 2)

    qkv_share, out_share = qkv_weight.shape[1], out_weight.shape[0]
    unit_share = fc1_weight.shape[1]
    mixed_shard = pad_rows(jnp.concatenate([qkv_weight.T, out_weight], axis=0))
    (mixed,) = gather([mixed_shard], dims, 1)
    up, down = gather([pad_rows(fc1_weight.T), pad_rows(fc2_weight)], dims, 2)
    mixed = mixed.reshape((devices,) + mixed_shard.shape)
    units = devices * unit_share
    up = up.reshape(devices, -1, width)[:, :unit_share].reshape(units, width)
    down = down.reshape(devices, -1, width)[:, :unit_share].reshape(units, width)
    qkv_rows = mixed[:, :qkv_share].reshape(3, HEADS, head_dim, width)
    qkv_rows = jnp.pad(qkv_rows, ((0, 0), (0, 0), (0, LANES - head_dim), (0, 0)))
    qkv_full = qkv_rows.transpose(1, 0, 2, 3).reshape(HEADS, 3 * LANES, width)
    out_full = mixed[:, qkv_share : qkv_share + out_share].reshape(HEADS, head_dim, width)
    out_full = jnp.pad(out_full, ((0, 0), (0, LANES - head_dim), (0, 0))).reshape(HEADS * LANES, width)

    embedded = time_embed(timesteps, width).astype(BF16)
    vectors = (norm1_gain, norm1_bias, out_bias, norm2_gain, norm2_bias, fc2_bias, fc1_bias)
    small = jnp.concatenate([*vectors, embedded.reshape(-1), row_table.reshape(-1), col_table.reshape(-1)])
    small = lax.all_gather(small[None], AXES, axis=0, tiled=True)
    found, start = [], 0
    for vector in vectors:
        share = vector.shape[0]
        found.append(small[:, start : start + share].reshape(1, -1).astype(F32))
        start += share
    gain_one, shift_one, b_out, gain_two, shift_two, b_down, b_up = found
    embedded_all = small[:, start : start + per * width].reshape(devices * per, width)
    start += per * width
    table_size = row_table.size
    row_full = small[:fsdp, start : start + table_size].reshape(HEADS, -1)
    col_full = small[:fsdp, start + table_size : start + 2 * table_size].reshape(HEADS, -1)

    lengths = image_lengths
    large = lengths[0] > slot_rows
    local_rows = jnp.arange(rows, dtype=jnp.int32)
    slot = jnp.where(large, 0, local_rows // slot_rows)
    spots = jnp.arange(per, dtype=jnp.int32)
    slot_pick = slot[:, None] == spots[None, :]
    slot_length = jnp.sum(jnp.where(slot_pick, lengths[None, :], 0), axis=1)
    valid = local_rows - slot * slot_rows < slot_length
    grid_index = jnp.arange(GRID, dtype=jnp.int32)
    row_hot = ((patch_cells // GRID)[:, None] == grid_index[None, :]).astype(BF16)
    col_hot = ((patch_cells % GRID)[:, None] == grid_index[None, :]).astype(BF16)
    onehot = jnp.concatenate([row_hot, col_hot, row_hot, col_hot], axis=1)
    lanes_left = ((0, 0), (head_dim, LANES - head_dim - per - 1))
    mask_q = jnp.concatenate(
        [jnp.where(slot_pick, 0.0, BIG), jnp.full((rows, 1), BIG, F32)], axis=1
    ).astype(BF16)
    mask_k = jnp.concatenate([slot_pick, jnp.logical_not(valid)[:, None]], axis=1).astype(BF16)
    mask_q, mask_k = jnp.pad(mask_q, lanes_left), jnp.pad(mask_k, lanes_left)

    offsets = grid_index[:, None] - grid_index[None, :] + GRID - 1
    diagonal = offsets[:, :, None] == jnp.arange(2 * GRID - 1, dtype=jnp.int32)[None, None, :]
    diagonal = diagonal.reshape(GRID * GRID, 2 * GRID - 1)
    both_tables = jnp.concatenate([row_full, col_full], axis=0)
    toeplitz = dot_nt(both_tables, diagonal.astype(BF16)).reshape(2, HEADS, GRID, GRID) * math.sqrt(head_dim)
    high = lax.reduce_precision(toeplitz, 8, 7)
    low = toeplitz - high
    zero = jnp.zeros((HEADS, GRID, GRID), F32)
    table = jnp.concatenate(
        [
            jnp.concatenate([high[0], zero, low[0], zero], axis=2),
            jnp.concatenate([zero, high[1], zero, low[1]], axis=2),
            jnp.zeros((HEADS, 2 * GRID, LANES), F32),
        ],
        axis=1,
    ).astype(BF16)

    share = time_weight.shape[1]
    time_part = jnp.dot(embedded_all, time_weight, preferred_element_type=F32)
    time_proj = lax.all_to_all(time_part.reshape(devices, per, share), AXES, 0, 0, tiled=True)
    time_proj = time_proj.transpose(1, 0, 2).reshape(per, 2, HEADS, head_dim)
    time_proj = jnp.where(large, time_proj[0:1], time_proj)
    time_proj = jnp.pad(time_proj, ((0, 0), (0, 0), (0, 0), (0, LANES - head_dim)))
    time_rows = time_proj.transpose(2, 1, 0, 3).reshape(HEADS, 2 * per, LANES)

    scale = 1.0 / math.sqrt(head_dim)
    normed_one, q, k, v, o, p = attend(
        tokens, gain_one, shift_one, qkv_full, time_rows, table, onehot, mask_q, mask_k, scale * math.log2(math.e)
    )
    hidden, normed_two = project(tokens, o, out_full, b_out, gain_two, shift_two)
    dy = jnp.where(valid[:, None], cotangent, jnp.zeros_like(cotangent))
    y, dn_two, d_up, d_down, db_up = mlp(normed_two, dy, up, down, b_up)
    layer_out, dh, do, d_out, vec_two = turn(hidden, y, b_down, dn_two, dy, gain_two, out_full, o)

    def shares(full, share):
        full = full.reshape(devices, share, width)
        full = jnp.pad(full, ((0, 0), (0, -share % PIECE), (0, 0)))
        return full.reshape(spread + full.shape[1:])

    up_sum, down_sum = scatter([shares(d_up, unit_share), shares(d_down, unit_share)], dims, 3)
    dqkv, d_qkv, slot_sums, pair = attend_back(normed_one, p, q, k, v, do, o, onehot, scale, per)
    d_qkv = d_qkv.reshape(HEADS, 3, LANES, width)[:, :, :head_dim].transpose(1, 0, 2, 3)
    d_out = d_out.reshape(HEADS, LANES, width)[:, :head_dim]
    d_mixed = jnp.concatenate(
        [d_qkv.reshape(devices, qkv_share, width), d_out.reshape(devices, out_share, width)], axis=1
    )
    (mixed_sum,) = scatter([shares(d_mixed, qkv_share + out_share)], dims, 4)
    input_grad, vec_one = end(tokens, dqkv, qkv_full.reshape(HEADS * 3 * LANES, width), gain_one, dh)

    slot_sums = slot_sums.reshape(HEADS, per, 3, LANES)[:, :, ::2, :head_dim]
    slot_sums = slot_sums.transpose(1, 2, 0, 3).reshape(per, 2 * width)
    merged = jnp.where(spots[:, None] == 0, jnp.sum(slot_sums, axis=0, keepdims=True), 0.0)
    slot_sums = jnp.where(large, merged, slot_sums)
    slot_sums = slot_sums.reshape(per, devices, share).transpose(1, 0, 2)
    slot_sums = lax.all_to_all(slot_sums, AXES, 0, 0, tiled=True).reshape(devices * per, share)
    time_grad = lax.dot_general(
        embedded_all.astype(F32), slot_sums, (((0,), (0,)), ((), ())), precision=HIGHEST
    )

    picked = pair[:, : 2 * GRID, : 2 * GRID]
    pairs = jnp.stack([picked[:, :GRID, :GRID], picked[:, GRID:, GRID:]]).reshape(2 * HEADS, GRID * GRID)
    tables = jnp.dot(pairs, diagonal.astype(F32), precision=HIGHEST)
    packed = [vec_one.reshape(-1), vec_two.reshape(-1), db_up.reshape(-1), tables.reshape(-1)]
    sizes = [part.shape[0] for part in packed]
    packed = lax.psum(jnp.concatenate(packed), AXES)
    place = lax.axis_index("dp") * fsdp + lax.axis_index("fsdp")
    small_share = width // devices
    vec_sum = packed[: 6 * width].reshape(6, devices, small_share)
    vec_sum = lax.dynamic_index_in_dim(vec_sum, place, 1, keepdims=False)
    up_bias = lax.dynamic_slice_in_dim(packed, 6 * width + place * unit_share, unit_share)
    tables = packed[6 * width + units :].reshape(2, fsdp, HEADS // fsdp, 2 * GRID - 1)
    tables = lax.dynamic_index_in_dim(tables, lax.axis_index("fsdp"), 1, keepdims=False)

    return (
        layer_out,
        input_grad,
        vec_sum[0],
        vec_sum[1],
        mixed_sum[:qkv_share].T,
        time_grad,
        mixed_sum[qkv_share : qkv_share + out_share],
        vec_sum[4],
        vec_sum[2],
        vec_sum[3],
        up_sum[:unit_share].T,
        up_bias,
        down_sum[:unit_share],
        vec_sum[5],
        tables[0],
        tables[1],
    )


def solution(mesh):
    rows = P(AXES, None)
    cols = P(None, AXES)
    vector = P(AXES)
    heads = P("fsdp", None)
    in_specs = (
        rows, vector, vector, vector, vector, vector, cols, cols, rows, vector, vector, vector,
        cols, vector, rows, vector, heads, heads, rows,
    )
    out_specs = (
        rows, rows, vector, vector, cols, cols, rows, vector, vector, vector, cols, vector, rows, vector,
        heads, heads,
    )
    return jax.shard_map(local, mesh=mesh, in_specs=in_specs, out_specs=out_specs, check_vma=False)
```

time: 2440 us -> 894 us (0.37)
  local copies, waits for them, and re-layouts: 1100 us -> 88.9 us
  Pallas kernels: 0 us -> 706 us
  blocking collectives: 690 us -> 40.9 us
  matrix products: 464 us -> 2.27 us
  other arithmetic: 109 us -> 20 us
  starting transfers between devices: 45.8 us -> 13.1 us
    gather x32 -> x0, local copies, waits for them, and re-layouts: 1010 us -> none  [the longest x16 504 us: scores(): jnp.take(col_full[head_start:head_start + head_group], col_choice, axis=1)]
    pallas_call x0 -> x10, Pallas kernels: none -> 706 us  [the longest x2 189 us: scatter(): pl.pallas_call(kernel, out_shape=[jax.ShapeDtypeStruct(part.shape[5:], F3...]
    unnamed x3 -> x0, blocking collectives: 680 us -> none
    dot_general x91 -> x4, matrix products: 464 us -> 2.27 us  [the longest x1 1.09 us: local(): lax.dot_general(embedded_all.astype(F32), slot_sums, (((0,), (0,)), ((),...]
    unnamed x416 -> x22, local copies, waits for them, and re-layouts: 69.3 us -> 5.15 us
    convert_element_type x18 -> x3, other arithmetic: 57.8 us -> 0.82 us  [the longest x1 0.66 us: time_embed(): angles = stamps.astype(F32)[:, None] * frequency[None, :]]
    unnamed x11 -> x1, starting transfers between devices: 45.6 us -> 0.04 us
    psum x0 -> x1, blocking collectives: none -> 40.9 us  [local(): packed = lax.psum(jnp.concatenate(packed), AXES)]
  transfers between devices with their start and end apart: 18 -> 3, of which waited for: 0 -> 1; matrix products, arithmetic and copies ran while one was open for 83% -> 6% of each run, Pallas kernels for 0% -> 35%
where the time goes in v1:
time: 894 us; the launch traced here: 886 us
  Pallas kernels  706 us (79%)
  local copies, waits for them, and re-layouts  88.9 us (10%)
  blocking collectives  40.9 us (5%)
  other arithmetic  20 us (2%)
  between operations  15.4 us (2%)
  starting transfers between devices  13.1 us (1%)
    pallas_call x2, Pallas kernels, scatter(): pl.pallas_call(kernel, out_shape=[jax.ShapeDtypeStruct(part.shape[5:], F3...  189 us
    pallas_call x2, Pallas kernels, gather(): pl.pallas_call(kernel, out_shape=[jax.ShapeDtypeStruct((G1, 2, G2, 2, 2)...  188 us
    pallas_call x1, Pallas kernels, mlp(): pl.pallas_call(mlp_kernel, grid=(units // block,), in_specs=[resident(nor...  94.2 us
    pallas_call x1, Pallas kernels, attend_back(): pl.pallas_call(functools.partial(attend_back_kernel, block, scale), grid=...  89.3 us
    pallas_call x1, Pallas kernels, attend(): pl.pallas_call(functools.partial(attend_kernel, factor, block), grid=(HEA...  77.9 us
    psum x1, blocking collectives, local(): packed = lax.psum(jnp.concatenate(packed), AXES)  40.9 us
    pallas_call x1, Pallas kernels, turn(): pl.pallas_call(turn_kernel, grid=(rows // block,), in_specs=[by_rows(widt...  28.4 us
    pallas_call x1, Pallas kernels, end(): pl.pallas_call(end_kernel, grid=(rows // block,), in_specs=[by_rows(width...  27.2 us
  transfers between devices with their start and end apart: 3, of which 1 were waited for; matrix products, arithmetic and copies ran while one was open for 6% of the time, Pallas kernels for 35%

profile of v1, /device:TPU:0, one launch (start us, length us, event | category | flops | bytes accessed | tf_op | source)
XLA Modules:
  0.0 886.4 jit_solution(11057503535482398158)
XLA Ops:
  7.9 0.8 reshape.389
  8.7 0.8 reshape.390
  9.7 4.8 concatenate.48
  14.9 0.7 copy-done.3
  16.4 0.7 select_reduce_fusion
  17.2 1.8 pad_maximum_fusion.2.refs_0_
  18.9 69.7 %shard_map.306 = bf16[4,2,1,2,2,144,1152]{6,5,4,3,2,1,0:T(8,128)(2,1)} custom-call(bf16[144,1152]{1,0:T(8,128)(2,1)} %pad_maximum_fusion.2.refs_0_), custom_call_target="tpu_custom_call" | custom-call | tf_op jit(solution)/shard_map/pallas_call | solution.py:302
  88.6 3.2 slice.167
  91.8 7.2 slice.158
  99.5 0.9 pad_convert_fusion.mask_k
  100.6 0.9 fusion.6.mask_q
  101.4 9.2 %reshape.392 = bf16[3,16,72,1152]{3,2,1,0:T(8,128)(2,1)} reshape(bf16[32,108,1152]{2,1,0:T(8,128)(2,1)} %slice.158) | data formatting | bytes 15925248 | tf_op jit(solution)/shard_map/reshape | solution.py:738
  110.6 2.3 reshape.398
  112.9 4.5 pad.28
  117.5 5.5 pad_bitcast_fusion
  123.0 5.7 copy.98
  129.1 1.8 broadcast_select_fusion.dy
  130.9 118.4 %shard_map.307 = (bf16[4,2,1,2,2,144,1152]{6,5,4,3,2,1,0:T(8,128)(2,1)}, bf16[4,2,1,2,2,144,1152]{6,5,4,3,2,1,0:T(8,128)(2,1)}) custom-call(bf16[144,1152]{1,0:T(8,128)(2,1)} %bitcast.109, bf16[144,1152]{1,0:T(8,128)(2,1)} %refs_1_.1), custom_call_target="tpu_custom_call" | custom-call | tf_op jit(solution)/shard_map/pallas_call | solution.py:302
  249.2 1.2 add_convert_fusion.onehot
  250.4 1.6 reshape.422
  253.4 7.3 all-to-all-start
  261.6 1.2 maximum_maximum_fusion.table
  263.1 0.7 reshape.420.bias
  264.5 0.7 reshape.418.gain
  265.2 0.7 reshape.415.gain
  265.9 0.7 reshape.419.shift
  267.3 0.7 reshape.416.shift
  269.0 77.9 %attend.1 = (bf16[1024,1152]{1,0:T(8,128)(2,1)}, bf16[16,1024,128]{2,1,0:T(8,128)(2,1)}, bf16[16,1024,128]{2,1,0:T(8,128)(2,1)}, bf16[16,1024,128]{2,1,0:T(8,128...) custom-call(bf16[1024,1152]{1,0:T(8,128)(2,1)} %tokens.5, f32[1,1152]{1,0:T(1,128)} %reshape.415.gain, ...), custom_call_target="tpu_custom_call" | custom-call | tf_op jit(solution)/shard_map/attend/pallas_call | solution.py:385
  346.9 11.3 %project.1 = (f32[1024,1152]{1,0:T(8,128)}, bf16[1024,1152]{1,0:T(8,128)(2,1)}) custom-call(bf16[1024,1152]{1,0:T(8,128)(2,1)} %tokens.5, bf16[1024,2048]{1,0:T(8,128)(2,1)} %get-tuple-element.44.o, bf16[2048,1152]{1,0:T(8,128)(2,1)} %bitcast.96, f32[1,1152]{1,0:T(1,128)} %reshape.417.bias, f32[1,1152]{1,0:T(1,128)} %reshape.418.gain, f32[1,1152]{1,0:T(1,128)} %reshape.419.shift), custom_call_target="tpu_custom_call" | custom-call | tf_op jit(solution)/shard_map/project/pallas_call | solution.py:516
  358.1 94.2 %mlp.1 = (f32[1024,1152]{1,0:T(8,128)}, f32[1024,1152]{1,0:T(8,128)}, bf16[4608,1152]{1,0:T(8,128)(2,1)}, bf16[4608,1152]{1,0:T(8,128)(2,1)}, f32[1,4608]{1,0:T(1,128)}) custom-call(bf16[1024,1152]{1,0:T(8,128)(2,1)} %get-tuple-element.46.normed, bf16[1024,1152]{1,0:T(8,128)(2,1)} %broadcast_select_fusion.dy, bf16[4608,1152]{1,0:T(8,128)(2,1)} %bitcast.102, ...), custom_call_target="tpu_custom_call" | custom-call | tf_op jit(solution)/shard_map/mlp/pallas_call | solution.py:571
  452.3 28.4 %turn.1 = (bf16[1024,1152]{1,0:T(8,128)(2,1)}, f32[1024,1152]{1,0:T(8,128)}, bf16[1024,2048]{1,0:T(8,128)(2,1)}, bf16[2048,1152]{1,0:T(8,128)(2,1)}, f32[4,1152]{1,0:T(4,128)}) custom-call(f32[1024,1152]{1,0:T(8,128)} %get-tuple-element.45.hidden, f32[1024,1152]{1,0:T(8,128)} %get-tuple-element.49.y, f32[1,1152]{1,0:T(1,128)} %reshape.421.bias, ...), custom_call_target="tpu_custom_call" | custom-call | tf_op jit(solution)/shard_map/turn/pallas_call | solution.py:629
  480.7 89.3 %attend_back.1 = (bf16[1024,6144]{1,0:T(8,128)(2,1)}, bf16[16,384,1152]{2,1,0:T(8,128)(2,1)}, f32[16,4,384]{2,1,0:T(4,128)}, f32[16,128,128]{2,1,0:T(8,128)}) custom-call(bf16[1024,1152]{1,0:T(8,128)(2,1)} %get-tuple-element.52.normed, bf16[16,1024,1024]{2,1,0:T(8,128)(2,1)} %get-tuple-element.53.p, bf16[16,1024,128]{2,1,0:T(8,128)(2,1)} %get-tuple-element.54.q, ...), custom_call_target="tpu_custom_call" | custom-call | tf_op jit(solution)/shard_map/attend_back/pallas_call | solution.py:469
  570.0 27.2 %end.1 = (bf16[1024,1152]{1,0:T(8,128)(2,1)}, f32[2,1152]{1,0:T(2,128)}) custom-call(bf16[1024,1152]{1,0:T(8,128)(2,1)} %tokens.5, bf16[1024,6144]{1,0:T(8,128)(2,1)} %get-tuple-element.58.dqkv, bf16[6144,1152]{1,0:T(8,128)(2,1)} %bitcast.93, f32[1,1152]{1,0:T(1,128)} %reshape.415.gain, f32[1024,1152]{1,0:T(8,128)} %get-tuple-element.59.dh), custom_call_target="tpu_custom_call" | custom-call | tf_op jit(solution)/shard_map/end/pallas_call | solution.py:678
  597.2 0.7 reshape.400
  599.0 40.9 %psum.7 = f32[13536]{0:T(1024)S(1)} all-reduce(f32[13536]{0:T(1024)S(1)} %pad_maximum_fusion.3), channel_id=1, replica_groups=mesh['dp'=16,'fsdp'=2] {'dp','fsdp'}, use_global_device_ids=true, to_apply=%region_1.2 | all-reduce | flops 13536 | bytes 108288 | tf_op jit(solution)/shard_map/psum | solution.py:843
  639.9 3.4 slice.175
  643.3 3.5 reshape.429
  646.8 7.0 copy_bitcast_fusion
  653.8 9.2 %concatenate.59 = bf16[4,2,1,2,2,108,1152]{6,5,4,3,1,0,2:T(8,128)(2,1)} reshape(bf16[3,16,72,1152]{3,2,1,0:T(8,128)(2,1)} %copy_bitcast_fusion) | data formatting | bytes 15925248 | tf_op jit(solution)/shard_map/concatenate | solution.py:822
  663.0 9.6 %pad_maximum_fusion.refs_0_ = bf16[4,2,1,2,2,144,1152]{6,5,4,3,2,1,0:T(8,128)(2,1)} fusion(bf16[4,2,1,2,2,36,1152]{6,5,4,3,2,1,0:T(8,128)(2,1)S(1)} %bitcast.99, bf16[4,2,1,2,2,108,1152]{6,5,4,3,2,1,0:T(8,128)(2,1)} %bitcast.98), kind=kLoop, calls=%fused_computation.1 | loop fusion | flops 21233664 | bytes 21233664 | tf_op jit(solution)/shard_map/concatenate | solution.py:822
  672.6 68.6 %shard_map.308 = f32[144,1152]{1,0:T(8,128)} custom-call(bf16[4,2,1,2,2,144,1152]{6,5,4,3,2,1,0:T(8,128)(2,1)} %pad_maximum_fusion.refs_0_), custom_call_target="tpu_custom_call" | custom-call | tf_op jit(solution)/shard_map/pallas_call | solution.py:323
  741.1 1.6 slice.148
  742.7 1.9 slice_bitcast_fusion
  745.7 5.8 all-to-all-start.1
  752.4 120.8 %shard_map.309 = (f32[144,1152]{1,0:T(8,128)}, f32[144,1152]{1,0:T(8,128)}) custom-call(bf16[4,2,1,2,2,144,1152]{6,5,4,3,2,1,0:T(8,128)(2,1)} %bitcast.100, bf16[4,2,1,2,2,144,1152]{6,5,4,3,2,1,0:T(8,128)(2,1)} %bitcast.101), custom_call_target="tpu_custom_call" | custom-call | tf_op jit(solution)/shard_map/pallas_call | solution.py:323
  874.4 1.1 fusion.30
  875.5 2.0 copy.136
  877.4 2.0 copy.137
  (87 shorter events, 11.5 us)
Async XLA Ops:
  7.2 245.3 %copy-start = (bf16[1152,72]{0,1:T(8,128)(2,1)S(1)}, bf16[1152,72]{0,1:T(8,128)(2,1)}, u32[]{:S(2)}) copy-start(bf16[1152,72]{0,1:T(8,128)(2,1)} %param.26) | copy-start | bytes 497668
  7.2 243.2 %all-reduce.9.cloned.1.call-start = ((), (), s32[]{:S(2)}) async-start(), calls=%async_computation.2 | async-start | bytes 765952
  14.9 0.7 copy-start.3
  91.8 7.3 copy-start.8
  123.0 6.1 copy-start.2
  253.4 14.9 %all-to-all-start = ((f32[32,4,72]{2,1,0:T(4,128)}), f32[32,4,72]{2,1,0:T(4,128)S(1)}, u32[]{:S(2)}, u32[]{:S(2)}) async-start(f32[32,4,72]{2,1,0:T(4,128)} %copy.100), calls=%async_computation | async-start | bytes 131072 | tf_op jit(solution)/shard_map/all_to_all | solution.py:798
  570.0 28.0 %copy-start.7 = (f32[4,1152]{1,0:T(4,128)S(1)}, f32[4,1152]{1,0:T(4,128)}, u32[]{:S(2)}) copy-start(f32[4,1152]{1,0:T(4,128)} %get-tuple-element.62) | copy-start | bytes 55300
  570.0 28.0 %copy-start.4 = (f32[16,128,128]{2,1,0:T(8,128)S(1)}, f32[16,128,128]{2,1,0:T(8,128)}, u32[]{:S(2)}) copy-start(f32[16,128,128]{2,1,0:T(8,128)} %get-tuple-element.64) | copy-start | bytes 3145732
  570.0 28.9 %copy-start.6 = (f32[1,4608]{1,0:T(1,128)S(1)}, f32[1,4608]{1,0:T(1,128)}, u32[]{:S(2)}) copy-start(f32[1,4608]{1,0:T(1,128)} %get-tuple-element.63) | copy-start | bytes 55300
  672.6 72.0 %copy-start.5 = (f32[16,4,384]{2,1,0:T(4,128)S(1)}, f32[16,4,384]{2,1,0:T(4,128)}, u32[]{:S(2)}) copy-start(f32[16,4,384]{2,1,0:T(4,128)} %get-tuple-element.67) | copy-start | bytes 294916
  745.7 128.7 %all-to-all-start.1 = ((f32[32,4,72]{2,1,0:T(4,128)}), f32[32,4,72]{2,1,0:T(4,128)S(1)}, u32[]{:S(2)}, u32[]{:S(2)}) async-start(f32[32,4,72]{2,1,0:T(4,128)} %copy.114), calls=%async_computation.1 | async-start | bytes 131072 | tf_op jit(solution)/shard_map/all_to_all | solution.py:833
  752.4 127.0 %copy-start.1 = (bf16[1152,72]{0,1:T(8,128)(2,1)S(1)}, bf16[1152,72]{0,1:T(8,128)(2,1)}, u32[]{:S(2)}) copy-start(bf16[1152,72]{0,1:T(8,128)(2,1)} %param.26) | copy-start | bytes 497668
Sparse Core Ops, SparseCore 0:
  15.8 147.6 all-reduce.8

commit v2 on v1

--- a/solution.py
+++ b/solution.py
@@ -19,7 +19,7 @@
 BF16 = jnp.bfloat16
 HIGHEST = lax.Precision.HIGHEST
 MESH_ID = pl.DeviceIdType.MESH
-VMEM_LIMIT = 60 * 1024 * 1024
+VMEM_LIMIT = 62 * 1024 * 1024
 
 
 def dot_nn(a, b):
@@ -84,6 +84,27 @@
     def sibling(self):
         return self.device(self.g1, self.p, self.g2, 1 - self.c, self.q)
 
+    def barrier_all(self):
+        semaphore = pltpu.get_barrier_semaphore()
+        count = self.count()
+
+        def body(i, carry):
+            pl.semaphore_signal(semaphore, inc=1, device_id=self.other(i), device_id_type=MESH_ID)
+            return carry
+
+        lax.fori_loop(1, count, body, 0)
+        pl.semaphore_wait(semaphore, count - 1)
+
+    def count(self):
+        return self.G1 * self.G2 * 8
+
+    def index(self):
+        return lax.axis_index("dp") * 2 + self.q
+
+    def other(self, i):
+        to = (self.index() + i) % self.count()
+        return (to // 2, to % 2)
+
     def barrier(self):
         partners = [self.on_line(spot) for spot in self.line()] + [self.first(), self.second(), self.sibling()]
         semaphore = pltpu.get_barrier_semaphore()
@@ -127,8 +148,8 @@
 
     def stage(self, k, number):
         at = self.at
-        array, start = self.pieces[k]
-        rows = pl.ds(start, PIECE)
+        array, start, count = self.pieces[k]
+        rows = pl.ds(start, count)
         result = self.results[array]
         every, every2 = at.whole
         source = self.sources[array].at[rows]
@@ -181,11 +202,11 @@
         self.from_first, self.from_line, self.sems = from_first, from_line, sems
 
     @staticmethod
-    def scratch(dims, pieces, width):
+    def scratch(dims, pieces, width, in_place=False):
         G1, G2 = dims
         n = len(pieces)
         return [
-            pltpu.VMEM((n, G1, 2, G2, 2, PIECE, width), BF16),
+            pltpu.VMEM((8, LANES) if in_place else (n, G1, 2, G2, 2, PIECE, width), BF16),
             pltpu.VMEM((n, G1, 2, G2, 2, PIECE, width), BF16),
             pltpu.VMEM((n, 2, G1, G2, PIECE, width), BF16),
             pltpu.VMEM((n, G1, G2, PIECE, width), BF16),
@@ -216,24 +237,28 @@
 
     def stage(self, k, number):
         at = self.at
-        array, start = self.pieces[k]
-        rows = pl.ds(start, PIECE)
+        array, start, count = self.pieces[k]
+        rows = pl.ds(start, count)
         source = self.sources[array]
         every, every2 = at.whole
         both = pl.ds(0, 2)
-        held = self.held.at[k]
+        in_place = len(self.held.shape) == 2
 
         def plane(p, q):
-            return held.at[every, p, every2, q]
+            if in_place:
+                return source.at[every, p, every2, at.c, q, rows]
+            return self.held.at[k, every, p, every2, q]
 
         local_copy = lambda: pltpu.make_async_copy(
-            source.at[every, both, every2, at.c, both, rows], held, self.sems.at[k, 4, 0]
+            source.at[every, both, every2, at.c, both, rows], self.held.at[k], self.sems.at[k, 4, 0]
         )
         if number == 0:
             self.send(k, 0, source.at[every, both, every2, 1 - at.c, both, rows], self.from_core.at[k], at.sibling())
-            local_copy().start()
+            if not in_place:
+                local_copy().start()
         if number == 1:
-            local_copy().wait()
+            if not in_place:
+                local_copy().wait()
             wait_for(self.from_core.at[k], self.sems.at[k, 0, 1])
             core = self.from_core.at[k]
             for p, q in ((at.bp, at.bq), (1 - at.p, 1 - at.q)):
@@ -251,12 +276,11 @@
         if number == 3:
             wait_for(self.from_first.at[k], self.sems.at[k, 3, 1])
             self.add(plane(at.p, at.q), self.from_first.at[k])
+            mine = plane(at.p, at.q)
             for i, spot in enumerate(at.line()):
-                self.send(
-                    k, 5 + i, held.at[spot[0], at.p, spot[1], at.q], self.from_line.at[k, i], at.on_line(spot)
-                )
+                self.send(k, 5 + i, mine.at[spot[0], spot[1]], self.from_line.at[k, i], at.on_line(spot))
         if number == 4:
-            total = held[at.g1, at.p, at.g2, at.q].astype(F32)
+            total = plane(at.p, at.q)[at.g1, at.g2].astype(F32)
             for i in range(at.G1 * at.G2 - 1):
                 wait_for(self.from_line.at[k, i], self.sems.at[k, 5 + i, 1])
                 total = total + self.from_line[k, i].astype(F32)
@@ -278,7 +302,7 @@
 
 
 def pieces_of(shards):
-    per = [(array, start) for array, shard in enumerate(shards) for start in range(0, shard, PIECE)]
+    per = [(array, start, PIECE) for array, shard in enumerate(shards) for start in range(0, shard, PIECE)]
     return sorted(per, key=lambda piece: piece[1])
 
 
@@ -287,47 +311,102 @@
     return jnp.pad(shard, ((0, -rows % PIECE), (0, 0)))
 
 
-def gather(shards, dims, collective):
-    pieces = pieces_of([shard.shape[0] for shard in shards])
-    count = len(shards)
-
-    def kernel(*refs):
-        work = Gather(dims, pieces, refs[:count], refs[count : 2 * count], *refs[2 * count :])
-        work.at.barrier()
-        for number in range(work.rounds()):
-            work.round(number)
-
-    G1, G2 = dims
+def spread_of(dims):
+    return (dims[0], 2, dims[1], 2, 2)
+
+
+def exchange(at, source, target, sems):
+    me = at.index()
+
+    def body(i, carry):
+        to = (me + i) % at.count()
+        pltpu.make_async_remote_copy(
+            src_ref=source.at[to, pl.ds(0, 8)],
+            dst_ref=target.at[me, pl.ds(0, 8)],
+            send_sem=sems.at[0],
+            recv_sem=sems.at[1],
+            device_id=at.other(i),
+            device_id_type=MESH_ID,
+        ).start()
+        return carry
+
+    lax.fori_loop(1, at.count(), body, 0)
+
+
+def exchanged(at, target, sems):
+    view = target.at[pl.ds(0, at.count() - 1), pl.ds(0, 8)]
+    wait_for(view, sems.at[1])
+    wait_for(view, sems.at[0])
+
+
+def begin_kernel(dims, pieces, shares, head_dim, mixed_shard, small_shard, time_weight, qkv_out, out_out, small_out,
+                 time_out, mixed, small, time_all, time_got, sems, own_sems, time_sems):
+    work = Gather(dims, pieces, (small_shard, mixed_shard), (small, mixed), sems, own_sems)
+    at = work.at
+    devices = at.count()
+    width = mixed.shape[-1]
+    at.barrier_all()
+    for number in range(work.rounds()):
+        work.round(number)
+        if number == Gather.STAGES - 1:
+            small_out[...] = small[...].reshape(small_out.shape)
+            for start in range(0, devices, 32):
+                span = pl.ds(start, 32)
+                rows = small_out[span].reshape(32 * small_out.shape[1], width)
+                time_all[span] = dot_nn(rows, time_weight[...]).reshape(32, small_out.shape[1], LANES)
+            exchange(at, time_all, time_got, time_sems)
+    exchanged(at, time_got, time_sems)
+    time_got[at.index()] = time_all[at.index(), 0:8]
+    time_out[...] = time_got[...]
+
+    def rows_of(first, share, base):
+        parts, left = [], head_dim
+        while left:
+            device, offset = divmod(first, share)
+            count = min(left, share - offset)
+            place = []
+            for size in reversed(spread_of(dims)):
+                device, digit = divmod(device, size)
+                place.insert(0, digit)
+            parts.append(mixed[(*place, slice(base + offset, base + offset + count))])
+            first, left = first + count, left - count
+        parts.append(jnp.zeros((LANES - head_dim, width), BF16))
+        return jnp.concatenate(parts, axis=0)
+
+    for head in range(HEADS):
+        for kind in range(3):
+            qkv_out[head, kind * LANES : (kind + 1) * LANES] = rows_of((kind * HEADS + head) * head_dim, shares[0], 0)
+        out_out[head * LANES : (head + 1) * LANES] = rows_of(head * head_dim, shares[1], shares[0])
+
+
+def begin(mixed_shard, small_shard, time_weight, dims, shares, head_dim):
+    width = mixed_shard.shape[1]
+    small_rows = small_shard.shape[0]
+    devices = dims[0] * dims[1] * 8
+    pieces = [(0, 0, small_rows)] + [(1, start, PIECE) for start in range(0, mixed_shard.shape[0], PIECE)]
     anywhere = pl.BlockSpec(memory_space=pl.ANY)
+    vmem = pl.BlockSpec(memory_space=pltpu.VMEM)
     return pl.pallas_call(
-        kernel,
-        out_shape=[jax.ShapeDtypeStruct((G1, 2, G2, 2, 2) + s.shape, s.dtype) for s in shards],
-        in_specs=[anywhere] * count,
-        out_specs=[anywhere] * count,
-        scratch_shapes=Gather.scratch(dims, pieces),
-        compiler_params=params(collective_id=collective, has_side_effects=True),
-    )(*shards)
-
-
-def scatter(parts, dims, collective):
-    pieces = pieces_of([part.shape[5] for part in parts])
-    count = len(parts)
-    width = parts[0].shape[6]
-
-    def kernel(*refs):
-        work = Scatter(dims, pieces, refs[:count], refs[count : 2 * count], *refs[2 * count :])
-        work.at.barrier()
-        for number in range(work.rounds()):
-            work.round(number)
-
-    return pl.pallas_call(
-        kernel,
-        out_shape=[jax.ShapeDtypeStruct(part.shape[5:], F32) for part in parts],
-        in_specs=[pl.BlockSpec(memory_space=pl.ANY)] * count,
-        out_specs=[pl.BlockSpec(memory_space=pltpu.VMEM)] * count,
-        scratch_shapes=Scatter.scratch(dims, pieces, width),
-        compiler_params=params(collective_id=collective, has_side_effects=True),
-    )(*parts)
+        functools.partial(begin_kernel, dims, pieces, shares, head_dim),
+        in_specs=[anywhere, anywhere, vmem],
+        out_specs=[vmem] * 4,
+        out_shape=[
+            jax.ShapeDtypeStruct((HEADS, 3 * LANES, width), BF16),
+            jax.ShapeDtypeStruct((HEADS * LANES, width), BF16),
+            jax.ShapeDtypeStruct((devices, small_rows, width), BF16),
+            jax.ShapeDtypeStruct((devices, 8, LANES), F32),
+        ],
+        scratch_shapes=[
+            pltpu.VMEM(spread_of(dims) + mixed_shard.shape, BF16),
+            pltpu.VMEM(spread_of(dims) + small_shard.shape, BF16),
+            pltpu.VMEM((devices, small_rows, LANES), F32),
+            pltpu.VMEM((devices, 8, LANES), F32),
+            *Gather.scratch(dims, pieces),
+            pltpu.SemaphoreType.DMA((2,)),
+        ],
+        compiler_params=params(collective_id=1, has_side_effects=True),
+        name="begin",
+    )(mixed_shard, small_shard, time_weight)
 
 
 def normalise(values):
@@ -343,9 +422,28 @@
     return inverse * (scaled - inner), unit
 
 
-def attend_kernel(factor, block, tokens, gain, shift, weight, time_rows, table, onehot, mask_q, mask_k,
-                  normed_out, q_out, k_out, v_out, o_out, p_out, keys):
+def spaced(work, step, steps):
+    last = work.rounds() - 1
+    for number in range(last):
+        at_step = number * steps // last
+
+        @pl.when(step == at_step)
+        def _(number=number):
+            work.round(number)
+
+
+def attend_kernel(factor, block, dims, pieces, tokens, gain, shift, weight, time_q, time_v, large, table, onehot,
+                  mask_q, mask_k, up_shard, down_shard,
+                  normed_out, q_out, k_out, v_out, o_out, p_out, up_out, down_out, keys, sems, own_sems):
     rows = tokens.shape[0]
+    work = Gather(dims, pieces, (up_shard, down_shard), (up_out, down_out), sems, own_sems)
+    step = pl.program_id(0)
+
+    @pl.when(step == 0)
+    def _():
+        work.at.barrier()
+
+    spaced(work, step, HEADS)
 
     @pl.when(pl.program_id(0) == 0)
     def _():
@@ -354,14 +452,17 @@
             unit, _ = normalise(tokens[span].astype(F32))
             normed_out[span] = (unit * gain[...] + shift[...]).astype(BF16)
 
-    per = time_rows.shape[1] // 2
+    per = rows // (SMALL * SMALL)
     slot = rows // per
+    one = large[...] > 0.0
     for i in range(per):
         span = pl.ds(i * slot, slot)
         qkv = dot_nt(normed_out[span], weight[0])
-        q_out[0, span] = (qkv[:, :LANES] + time_rows[0, i : i + 1]).astype(BF16)
+        add_q = jnp.where(one, time_q[0, 0:1], time_q[0, i : i + 1])
+        add_v = jnp.where(one, time_v[0, 0:1], time_v[0, i : i + 1])
+        q_out[0, span] = (qkv[:, :LANES] + add_q).astype(BF16)
         k_out[0, span] = qkv[:, LANES : 2 * LANES].astype(BF16)
-        v_out[0, span] = (qkv[:, 2 * LANES :] + time_rows[0, per + i : per + i + 1]).astype(BF16)
+        v_out[0, span] = (qkv[:, 2 * LANES :] + add_v).astype(BF16)
     keys[:, :LANES] = k_out[0] + mask_k[...]
     keys[:, LANES:] = onehot[...]
     for start in range(0, rows, block):
@@ -376,25 +477,35 @@
         p_out[0, span] = low
         o_out[span] = dot_nn(low, v_out[0]).astype(BF16)
 
-
-def attend(tokens, gain, shift, weight, time_rows, table, onehot, mask_q, mask_k, factor):
+    @pl.when(step == HEADS - 1)
+    def _():
+        work.round(work.rounds() - 1)
+
+
+def attend(tokens, gain, shift, weight, times, large, table, onehot, mask_q, mask_k, factor, shards, dims):
     rows, width = tokens.shape
     block = min(256, rows)
+    pieces = pieces_of([shard.shape[0] for shard in shards])
+    anywhere = pl.BlockSpec(memory_space=pl.ANY)
     per_head = lambda *shape: pl.BlockSpec((1,) + shape, lambda h: (h, 0, 0))
     head_rows = jax.ShapeDtypeStruct((HEADS, rows, LANES), BF16)
     return pl.pallas_call(
-        functools.partial(attend_kernel, factor, block),
+        functools.partial(attend_kernel, factor, block, dims, pieces),
         grid=(HEADS,),
         in_specs=[
             resident(tokens.shape),
             resident(gain.shape),
             resident(shift.shape),
             per_head(3 * LANES, width),
-            per_head(*time_rows.shape[1:]),
+            pl.BlockSpec((1, 8, LANES), lambda h: (h, 0, 0)),
+            pl.BlockSpec((1, 8, LANES), lambda h: (HEADS + h, 0, 0)),
+            resident(large.shape),
             per_head(LANES, LANES),
             resident(onehot.shape),
             resident(mask_q.shape),
             resident(mask_k.shape),
+            anywhere,
+            anywhere,
         ],
         out_specs=[
             resident(tokens.shape),
@@ -403,6 +514,8 @@
             per_head(rows, LANES),
             pl.BlockSpec((rows, LANES), lambda h: (0, h)),
             per_head(rows, rows),
+            anywhere,
+            anywhere,
         ],
         out_shape=[
             jax.ShapeDtypeStruct(tokens.shape, BF16),
@@ -411,16 +524,26 @@
             head_rows,
             jax.ShapeDtypeStruct((rows, HEADS * LANES), BF16),
             jax.ShapeDtypeStruct((HEADS, rows, rows), BF16),
-        ],
-        scratch_shapes=[pltpu.VMEM((rows, 2 * LANES), BF16)],
-        compiler_params=params(),
+            *[jax.ShapeDtypeStruct(spread_of(dims) + s.shape, BF16) for s in shards],
+        ],
+        scratch_shapes=[pltpu.VMEM((rows, 2 * LANES), BF16), *Gather.scratch(dims, pieces)],
+        compiler_params=params(collective_id=2, has_side_effects=True),
         name="attend",
-    )(tokens, gain, shift, weight, time_rows, table, onehot, mask_q, mask_k)
-
-
-def attend_back_kernel(block, scale, normed, p, q, k, v, do, o, onehot,
-                       dqkv_out, dw_out, sums_out, pair_out, keys, grads, dk_sum, dv_sum):
+    )(tokens, gain, shift, weight, times, times, large, table, onehot, mask_q, mask_k, *shards)
+
+
+def attend_back_kernel(block, scale, dims, pieces, normed, p, q, k, v, do, o, onehot, large, d_up, d_down,
+                       dqkv_out, dw_out, sums_q, sums_v, pair_out, up_out, down_out,
+                       keys, grads, dk_sum, dv_sum, *buffers):
     rows = normed.shape[0]
+    work = Scatter(dims, pieces, (d_up, d_down), (up_out, down_out), *buffers)
+    step = pl.program_id(0)
+
+    @pl.when(step == 0)
+    def _():
+        work.at.barrier()
+
+    spaced(work, step, HEADS)
     lane = lax.broadcasted_iota(jnp.int32, (rows, LANES), 1)
     head = 72
     delta = jnp.sum(do[...].astype(F32) * o[...].astype(F32), axis=1, keepdims=True)
@@ -452,22 +575,33 @@
     dqkv_out[:, LANES : 2 * LANES] = (dk_sum[...] * scale).astype(BF16)
     dqkv_out[:, 2 * LANES :] = dv_sum[...].astype(BF16)
     pair_out[0] = pair
-    per = sums_out.shape[1]
-    slot = rows // per
-    for i in range(per):
-        sums_out[0, i : i + 1] = jnp.sum(
-            dqkv_out[pl.ds(i * slot, slot)].astype(F32), axis=0, keepdims=True
-        )
+    slot = SMALL * SMALL
+    one = large[...] > 0.0
+    for target, base in ((sums_q, 0), (sums_v, 2 * LANES)):
+        sums = []
+        for start in range(0, rows, slot):
+            part = dqkv_out[pl.ds(start, slot), base : base + LANES]
+            sums.append(jnp.sum(part.astype(F32), axis=0, keepdims=True))
+        total = functools.reduce(jnp.add, sums)
+        sums = [jnp.where(one, total if i == 0 else jnp.zeros_like(total), part) for i, part in enumerate(sums)]
+        sums.append(jnp.zeros((8 - len(sums), LANES), F32))
+        target[0] = jnp.concatenate(sums, axis=0)
     dw_out[0] = dot_tn(dqkv_out[...], normed[...]).astype(BF16)
 
-
-def attend_back(normed, p, q, k, v, do, o, onehot, scale, per):
+    @pl.when(step == HEADS - 1)
+    def _():
+        work.round(work.rounds() - 1)
+
+
+def attend_back(normed, p, q, k, v, do, o, onehot, large, scale, parts, dims):
     rows, width = normed.shape
     block = min(256, rows)
+    pieces = pieces_of([part.shape[5] for part in parts])
+    anywhere = pl.BlockSpec(memory_space=pl.ANY)
     per_head = lambda *shape: pl.BlockSpec((1,) + shape, lambda h: (h, 0, 0))
     head_cols = pl.BlockSpec((rows, LANES), lambda h: (0, h))
     return pl.pallas_call(
-        functools.partial(attend_back_kernel, block, scale),
+        functools.partial(attend_back_kernel, block, scale, dims, pieces),
         grid=(HEADS,),
         in_specs=[
             resident(normed.shape),
@@ -478,28 +612,36 @@
             head_cols,
             head_cols,
             resident(onehot.shape),
+            resident(large.shape),
+            anywhere,
+            anywhere,
         ],
         out_specs=[
             pl.BlockSpec((rows, 3 * LANES), lambda h: (0, h)),
             per_head(3 * LANES, width),
-            per_head(per, 3 * LANES),
+            per_head(8, LANES),
+            per_head(8, LANES),
             per_head(LANES, LANES),
+            *[resident(part.shape[5:]) for part in parts],
         ],
         out_shape=[
             jax.ShapeDtypeStruct((rows, HEADS * 3 * LANES), BF16),
             jax.ShapeDtypeStruct((HEADS, 3 * LANES, width), BF16),
-            jax.ShapeDtypeStruct((HEADS, per, 3 * LANES), F32),
+            jax.ShapeDtypeStruct((HEADS, 8, LANES), F32),
+            jax.ShapeDtypeStruct((HEADS, 8, LANES), F32),
             jax.ShapeDtypeStruct((HEADS, LANES, LANES), F32),
+            *[jax.ShapeDtypeStruct(part.shape[5:], F32) for part in parts],
         ],
         scratch_shapes=[
             pltpu.VMEM((rows, 2 * LANES), BF16),
             pltpu.VMEM((rows, LANES), BF16),
             pltpu.VMEM((rows, LANES), F32),
             pltpu.VMEM((rows, LANES), F32),
-        ],
-        compiler_params=params(),
+            *Scatter.scratch(dims, pieces, width),
+        ],
+        compiler_params=params(collective_id=3, has_side_effects=True),
         name="attend_back",
-    )(normed, p, q, k, v, do, o, onehot)
+    )(normed, p, q, k, v, do, o, onehot, large, *parts)
 
 
 def project_kernel(tokens, o, weight, bias, gain, shift, hidden_out, normed_out):
@@ -653,39 +795,203 @@
     )(hidden, y, bias, dn, dy, gain, weight, o)
 
 
-def end_kernel(tokens, dqkv, weight, gain, dh, out, vec_out):
-    first = pl.program_id(0) == 0
+class SumAll:
+    STAGES = 5
+
+    def __init__(self, at, total, send, got, sems):
+        self.at, self.total, self.send, self.got, self.sems = at, total, send, got, sems
+
+    @staticmethod
+    def scratch(dims, shape):
+        copies = 2 + dims[0] * dims[1]
+        return [
+            pltpu.VMEM(shape, F32),
+            pltpu.VMEM((4,) + shape, F32),
+            pltpu.VMEM((copies,) + shape, F32),
+            pltpu.SemaphoreType.DMA((copies, 2)),
+        ]
+
+    def start(self, stage, kind, to):
+        pltpu.make_async_remote_copy(
+            src_ref=self.send.at[stage],
+            dst_ref=self.got.at[kind],
+            send_sem=self.sems.at[kind, 0],
+            recv_sem=self.sems.at[kind, 1],
+            device_id=to,
+            device_id_type=MESH_ID,
+        ).start()
+
+    def take(self, kind):
+        wait_for(self.got.at[kind], self.sems.at[kind, 1])
+        wait_for(self.got.at[kind], self.sems.at[kind, 0])
+
+    def stage(self, number):
+        at = self.at
+        p_next = at.device(at.g1, 1 - at.p, at.g2, at.c, at.q)
+        q_next = at.device(at.g1, at.p, at.g2, at.c, 1 - at.q)
+        if 0 < number < 4:
+            self.take(number - 1)
+            self.total[...] += self.got[number - 1]
+        if number < 4:
+            self.send[number] = self.total[...]
+        if number < 3:
+            self.start(number, number, (at.sibling(), p_next, q_next)[number])
+        if number == 3:
+            line = at.G1 * at.G2
+            mine = at.g1 * at.G2 + at.g2
+            for i, spot in enumerate(at.line()):
+                self.start(3, 3 + i, at.on_line(spot))
+        if number == 4:
+            line = at.G1 * at.G2
+            mine = at.g1 * at.G2 + at.g2
+            for i in range(line - 1):
+                self.take(3 + i)
+            spots = [spot[0] * at.G2 + spot[1] for spot in at.line()]
+            parts = [self.got[3 + i] for i in range(line - 1)] + [self.send[3]]
+            spots.append(mine)
+            total = jnp.zeros_like(parts[0])
+            for place in range(line):
+                chosen = jnp.zeros_like(parts[0])
+                for spot, part in zip(spots, parts):
+                    chosen = jnp.where(spot == place, part, chosen)
+                total = total + chosen
+            self.total[...] = total
+
+
+def end_kernel(dims, pieces, shares, head_dim, tokens, dqkv, weight, gain, dh, small, time_send, vec_in, dw, dw_out,
+               out, vec_out, time_out, mixed_out, mixed, dw_buffer, dw_sems, time_got, time_sems,
+               vec_total, vec_send, vec_got, vec_sems, *buffers):
+    step = pl.program_id(0)
+    steps = pl.num_programs(0)
+    work = Scatter(dims, pieces, (mixed,), (mixed_out,), *buffers)
+    at = work.at
+    sums = SumAll(at, vec_total, vec_send, vec_got, vec_sems)
+    width = tokens.shape[1]
+    fetches = HEADS + HEADS // 2
+    pair = 2 * LANES
+
+    def fetch(number):
+        slot = number % 2
+        if number < HEADS:
+            return pltpu.make_async_copy(dw.at[number], dw_buffer.at[slot], dw_sems.at[slot])
+        source = dw_out.at[pl.ds((number - HEADS) * pair, pair)]
+        return pltpu.make_async_copy(source, dw_buffer.at[slot, pl.ds(0, pair)], dw_sems.at[slot])
+
+    def place_of(device):
+        place = []
+        for size in reversed(spread_of(dims)):
+            device, digit = divmod(device, size)
+            place.insert(0, digit)
+        return tuple(place)
+
+    def put(first, share, base, value):
+        done = 0
+        while done < head_dim:
+            device, offset = divmod(first + done, share)
+            count = min(head_dim - done, share - offset)
+            mixed[(*place_of(device), slice(base + offset, base + offset + count))] = value[done : done + count]
+            done += count
+
+    @pl.when(step == 0)
+    def _():
+        fetch(0).start()
+        time_got[...] = jnp.zeros_like(time_got)
+        at.barrier_all()
+        exchange(at, time_send, time_got, time_sems)
+        vec_total[...] = vec_in[...]
+        for number in range(fetches):
+            if number + 1 < fetches:
+                fetch(number + 1).start()
+            fetch(number).wait()
+            if number < HEADS:
+                for kind in range(3):
+                    value = dw_buffer[number % 2, kind * LANES : kind * LANES + head_dim]
+                    put((kind * HEADS + number) * head_dim, shares[0], 0, value)
+            else:
+                for i in range(2):
+                    head = (number - HEADS) * 2 + i
+                    value = dw_buffer[number % 2, i * LANES : i * LANES + head_dim]
+                    put(head * head_dim, shares[1], shares[0], value)
+        work.round(0)
+
+    @pl.when(step == 3)
+    def _():
+        work.round(1)
+
+    @pl.when(step == 6)
+    def _():
+        work.round(2)
+
     dn = dot_nn(dqkv[...], weight[...])
     back, unit = norm_back(tokens[...].astype(F32), gain[...], dn)
     out[...] = (dh[...] + back).astype(BF16)
-    sums = jnp.concatenate(
-        [jnp.sum(dn * unit, axis=0, keepdims=True), jnp.sum(dn, axis=0, keepdims=True)], axis=0
-    )
-
-    @pl.when(first)
-    def _():
-        vec_out[...] = sums
-
-    @pl.when(jnp.logical_not(first))
-    def _():
-        vec_out[...] += sums
-
-
-def end(tokens, dqkv, weight, gain, dh):
+    vec_total[0:1] += jnp.sum(dn * unit, axis=0, keepdims=True)
+    vec_total[1:2] += jnp.sum(dn, axis=0, keepdims=True)
+
+    @pl.when(step == steps - 1)
+    def _():
+        sums.stage(0)
+        exchanged(at, time_got, time_sems)
+        time_got[at.index(), 0:8] = time_send[at.index()]
+        for number in range(3, max(work.rounds(), 7)):
+            if number < work.rounds():
+                work.round(number)
+            if number < 7:
+                sums.stage(number - 2)
+        vec_out[...] = vec_total[...]
+        times = time_got[...].reshape(small.shape[0], LANES)
+        high = times.astype(BF16)
+        low = (times - high.astype(F32)).astype(BF16)
+        time_out[...] = dot_tn(small[...], high) + dot_tn(small[...], low)
+
+
+def end(tokens, dqkv, weight, gain, dh, small, time_send, vec_in, dw, dw_out, dims, shares, head_dim):
     rows, width = tokens.shape
-    block = min(256, rows)
+    block = rows // 8
     by_rows = lambda cols: pl.BlockSpec((block, cols), lambda i: (i, 0))
+    shard_rows = -(-sum(shares) // PIECE) * PIECE
+    pieces = pieces_of([shard_rows])
+    anywhere = pl.BlockSpec(memory_space=pl.ANY)
+    devices = time_send.shape[0]
     return pl.pallas_call(
-        end_kernel,
+        functools.partial(end_kernel, dims, pieces, shares, head_dim),
         grid=(rows // block,),
         in_specs=[
-            by_rows(width), by_rows(dqkv.shape[1]), resident(weight.shape), resident((1, width)), by_rows(width)
-        ],
-        out_specs=[by_rows(width), resident((2, width))],
-        out_shape=[jax.ShapeDtypeStruct(tokens.shape, BF16), jax.ShapeDtypeStruct((2, width), F32)],
-        compiler_params=params(),
+            by_rows(width),
+            by_rows(dqkv.shape[1]),
+            resident(weight.shape),
+            resident((1, width)),
+            by_rows(width),
+            resident(small.shape),
+            resident(time_send.shape),
+            resident(vec_in.shape),
+            anywhere,
+            anywhere,
+        ],
+        out_specs=[
+            by_rows(width),
+            resident(vec_in.shape),
+            resident((width, LANES)),
+            resident((shard_rows, width)),
+        ],
+        out_shape=[
+            jax.ShapeDtypeStruct(tokens.shape, BF16),
+            jax.ShapeDtypeStruct(vec_in.shape, F32),
+            jax.ShapeDtypeStruct((width, LANES), F32),
+            jax.ShapeDtypeStruct((shard_rows, width), F32),
+        ],
+        scratch_shapes=[
+            pltpu.VMEM(spread_of(dims) + (shard_rows, width), BF16),
+            pltpu.VMEM((2,) + dw.shape[1:], BF16),
+            pltpu.SemaphoreType.DMA((2,)),
+            pltpu.VMEM((devices, small.shape[0] // devices, LANES), F32),
+            pltpu.SemaphoreType.DMA((2,)),
+            *SumAll.scratch(dims, vec_in.shape),
+            *Scatter.scratch(dims, pieces, width, in_place=True),
+        ],
+        compiler_params=params(collective_id=4, has_side_effects=True),
         name="end",
-    )(tokens, dqkv, weight, gain, dh)
+    )(tokens, dqkv, weight, gain, dh, small, time_send, vec_in, dw, dw_out)
 
 
 def time_embed(stamps, feat_width):
@@ -724,38 +1030,29 @@
     fsdp = lax.axis_size("fsdp")
     devices = lax.axis_size("dp") * fsdp
     dims = split_dp(lax.axis_size("dp"))
-    spread = (dims[0], 2, dims[1], 2, 2)
 
     qkv_share, out_share = qkv_weight.shape[1], out_weight.shape[0]
-    unit_share = fc1_weight.shape[1]
+    unit_share, time_share = fc1_weight.shape[1], time_weight.shape[1]
+    units = devices * unit_share
     mixed_shard = pad_rows(jnp.concatenate([qkv_weight.T, out_weight], axis=0))
-    (mixed,) = gather([mixed_shard], dims, 1)
-    up, down = gather([pad_rows(fc1_weight.T), pad_rows(fc2_weight)], dims, 2)
-    mixed = mixed.reshape((devices,) + mixed_shard.shape)
-    units = devices * unit_share
-    up = up.reshape(devices, -1, width)[:, :unit_share].reshape(units, width)
-    down = down.reshape(devices, -1, width)[:, :unit_share].reshape(units, width)
-    qkv_rows = mixed[:, :qkv_share].reshape(3, HEADS, head_dim, width)
-    qkv_rows = jnp.pad(qkv_rows, ((0, 0), (0, 0), (0, LANES - head_dim), (0, 0)))
-    qkv_full = qkv_rows.transpose(1, 0, 2, 3).reshape(HEADS, 3 * LANES, width)
-    out_full = mixed[:, qkv_share : qkv_share + out_share].reshape(HEADS, head_dim, width)
-    out_full = jnp.pad(out_full, ((0, 0), (0, LANES - head_dim), (0, 0))).reshape(HEADS * LANES, width)
-
     embedded = time_embed(timesteps, width).astype(BF16)
-    vectors = (norm1_gain, norm1_bias, out_bias, norm2_gain, norm2_bias, fc2_bias, fc1_bias)
-    small = jnp.concatenate([*vectors, embedded.reshape(-1), row_table.reshape(-1), col_table.reshape(-1)])
-    small = lax.all_gather(small[None], AXES, axis=0, tiled=True)
-    found, start = [], 0
-    for vector in vectors:
-        share = vector.shape[0]
-        found.append(small[:, start : start + share].reshape(1, -1).astype(F32))
-        start += share
-    gain_one, shift_one, b_out, gain_two, shift_two, b_down, b_up = found
-    embedded_all = small[:, start : start + per * width].reshape(devices * per, width)
-    start += per * width
+    vectors = jnp.concatenate([norm1_gain, norm1_bias, out_bias, norm2_gain, norm2_bias, fc2_bias, fc1_bias])
     table_size = row_table.size
-    row_full = small[:fsdp, start : start + table_size].reshape(HEADS, -1)
-    col_full = small[:fsdp, start + table_size : start + 2 * table_size].reshape(HEADS, -1)
+    to_row = lambda flat: jnp.pad(flat, (0, width - flat.shape[0]))[None]
+    both_tables = jnp.concatenate([row_table.reshape(-1), col_table.reshape(-1)])
+    small_shard = jnp.concatenate([embedded, to_row(vectors), to_row(both_tables)], axis=0)
+    small_shard = jnp.pad(small_shard, ((0, -small_shard.shape[0] % 16), (0, 0)))
+    time_padded = jnp.pad(time_weight, ((0, 0), (0, LANES - time_share)))
+    shares = (qkv_share, out_share)
+    qkv_full, out_full, small, times = begin(mixed_shard, small_shard, time_padded, dims, shares, head_dim)
+    gathered = small[:, per]
+    vector_share = norm1_gain.shape[0]
+    vectors = gathered[:, : 6 * vector_share].reshape(devices, 6, vector_share).transpose(1, 0, 2)
+    vectors = vectors.reshape(6, width).astype(F32)
+    gain_one, shift_one, b_out, gain_two, shift_two, b_down = (vectors[i : i + 1] for i in range(6))
+    b_up = gathered[:, 6 * vector_share : 6 * vector_share + unit_share].reshape(1, units).astype(F32)
+    tables = small[:fsdp, per + 1, : 2 * table_size].reshape(fsdp, 2, HEADS // fsdp, 2 * GRID - 1)
+    tables = tables.transpose(1, 0, 2, 3).reshape(2 * HEADS, 2 * GRID - 1)
 
     lengths = image_lengths
     large = lengths[0] > slot_rows
@@ -779,8 +1076,7 @@
     offsets = grid_index[:, None] - grid_index[None, :] + GRID - 1
     diagonal = offsets[:, :, None] == jnp.arange(2 * GRID - 1, dtype=jnp.int32)[None, None, :]
     diagonal = diagonal.reshape(GRID * GRID, 2 * GRID - 1)
-    both_tables = jnp.concatenate([row_full, col_full], axis=0)
-    toeplitz = dot_nt(both_tables, diagonal.astype(BF16)).reshape(2, HEADS, GRID, GRID) * math.sqrt(head_dim)
+    toeplitz = dot_nt(tables, diagonal.astype(BF16)).reshape(2, HEADS, GRID, GRID) * math.sqrt(head_dim)
     high = lax.reduce_precision(toeplitz, 8, 7)
     low = toeplitz - high
     zero = jnp.zeros((HEADS, GRID, GRID), F32)
@@ -793,60 +1089,59 @@
         axis=1,
     ).astype(BF16)
 
-    share = time_weight.shape[1]
-    time_part = jnp.dot(embedded_all, time_weight, preferred_element_type=F32)
-    time_proj = lax.all_to_all(time_part.reshape(devices, per, share), AXES, 0, 0, tiled=True)
-    time_proj = time_proj.transpose(1, 0, 2).reshape(per, 2, HEADS, head_dim)
-    time_proj = jnp.where(large, time_proj[0:1], time_proj)
-    time_proj = jnp.pad(time_proj, ((0, 0), (0, 0), (0, 0), (0, LANES - head_dim)))
-    time_rows = time_proj.transpose(2, 1, 0, 3).reshape(HEADS, 2 * per, LANES)
+    if time_share != head_dim:
+        times = times[:, :per, :time_share].transpose(1, 0, 2).reshape(per, 2 * HEADS, head_dim)
+        times = jnp.pad(times.transpose(1, 0, 2), ((0, 0), (0, 8 - per), (0, LANES - head_dim)))
 
     scale = 1.0 / math.sqrt(head_dim)
-    normed_one, q, k, v, o, p = attend(
-        tokens, gain_one, shift_one, qkv_full, time_rows, table, onehot, mask_q, mask_k, scale * math.log2(math.e)
+    large_lanes = jnp.broadcast_to(large.astype(F32), (1, LANES))
+    normed_one, q, k, v, o, p, up, down = attend(
+        tokens, gain_one, shift_one, qkv_full, times, large_lanes, table, onehot, mask_q, mask_k,
+        scale * math.log2(math.e), (pad_rows(fc1_weight.T), pad_rows(fc2_weight)), dims,
     )
+    up = up.reshape(devices, -1, width)[:, :unit_share].reshape(units, width)
+    down = down.reshape(devices, -1, width)[:, :unit_share].reshape(units, width)
     hidden, normed_two = project(tokens, o, out_full, b_out, gain_two, shift_two)
     dy = jnp.where(valid[:, None], cotangent, jnp.zeros_like(cotangent))
     y, dn_two, d_up, d_down, db_up = mlp(normed_two, dy, up, down, b_up)
     layer_out, dh, do, d_out, vec_two = turn(hidden, y, b_down, dn_two, dy, gain_two, out_full, o)
 
-    def shares(full, share):
+    def by_device(full, share):
         full = full.reshape(devices, share, width)
         full = jnp.pad(full, ((0, 0), (0, -share % PIECE), (0, 0)))
-        return full.reshape(spread + full.shape[1:])
-
-    up_sum, down_sum = scatter([shares(d_up, unit_share), shares(d_down, unit_share)], dims, 3)
-    dqkv, d_qkv, slot_sums, pair = attend_back(normed_one, p, q, k, v, do, o, onehot, scale, per)
-    d_qkv = d_qkv.reshape(HEADS, 3, LANES, width)[:, :, :head_dim].transpose(1, 0, 2, 3)
-    d_out = d_out.reshape(HEADS, LANES, width)[:, :head_dim]
-    d_mixed = jnp.concatenate(
-        [d_qkv.reshape(devices, qkv_share, width), d_out.reshape(devices, out_share, width)], axis=1
+        return full.reshape(spread_of(dims) + full.shape[1:])
+
+    dqkv, d_qkv, sums_q, sums_v, pair, up_sum, down_sum = attend_back(
+        normed_one, p, q, k, v, do, o, onehot, large_lanes, scale,
+        (by_device(d_up, unit_share), by_device(d_down, unit_share)), dims,
     )
-    (mixed_sum,) = scatter([shares(d_mixed, qkv_share + out_share)], dims, 4)
-    input_grad, vec_one = end(tokens, dqkv, qkv_full.reshape(HEADS * 3 * LANES, width), gain_one, dh)
-
-    slot_sums = slot_sums.reshape(HEADS, per, 3, LANES)[:, :, ::2, :head_dim]
-    slot_sums = slot_sums.transpose(1, 2, 0, 3).reshape(per, 2 * width)
-    merged = jnp.where(spots[:, None] == 0, jnp.sum(slot_sums, axis=0, keepdims=True), 0.0)
-    slot_sums = jnp.where(large, merged, slot_sums)
-    slot_sums = slot_sums.reshape(per, devices, share).transpose(1, 0, 2)
-    slot_sums = lax.all_to_all(slot_sums, AXES, 0, 0, tiled=True).reshape(devices * per, share)
-    time_grad = lax.dot_general(
-        embedded_all.astype(F32), slot_sums, (((0,), (0,)), ((), ())), precision=HIGHEST
+    time_send = jnp.concatenate([sums_q, sums_v], axis=0)
+    if time_share != head_dim:
+        time_send = time_send[:, :per, :head_dim].transpose(1, 0, 2).reshape(per, devices, time_share)
+        time_send = jnp.pad(time_send.transpose(1, 0, 2), ((0, 0), (0, 8 - per), (0, LANES - time_share)))
+    pairs = jnp.concatenate([pair[:, :GRID, :GRID], pair[:, GRID : 2 * GRID, GRID : 2 * GRID]])
+    tables = jnp.dot(pairs.reshape(2 * HEADS, GRID * GRID), diagonal.astype(F32), precision=HIGHEST)
+    tables = tables.reshape(2, HEADS * (2 * GRID - 1))
+    vec_in = jnp.concatenate(
+        [
+            jnp.zeros((2, width), F32),
+            vec_two,
+            db_up.reshape(units // width, width),
+            jnp.pad(tables, ((0, 0), (0, width - tables.shape[1]))),
+        ],
+        axis=0,
     )
-
-    picked = pair[:, : 2 * GRID, : 2 * GRID]
-    pairs = jnp.stack([picked[:, :GRID, :GRID], picked[:, GRID:, GRID:]]).reshape(2 * HEADS, GRID * GRID)
-    tables = jnp.dot(pairs, diagonal.astype(F32), precision=HIGHEST)
-    packed = [vec_one.reshape(-1), vec_two.reshape(-1), db_up.reshape(-1), tables.reshape(-1)]
-    sizes = [part.shape[0] for part in packed]
-    packed = lax.psum(jnp.concatenate(packed), AXES)
+    vec_in = jnp.pad(vec_in, ((0, -vec_in.shape[0] % 8), (0, 0)))
+    input_grad, vec_all, time_grad, mixed_sum = end(
+        tokens, dqkv, qkv_full.reshape(HEADS * 3 * LANES, width), gain_one, dh,
+        small.reshape(-1, width), time_send, vec_in, d_qkv, d_out, dims, shares, head_dim,
+    )
+
     place = lax.axis_index("dp") * fsdp + lax.axis_index("fsdp")
-    small_share = width // devices
-    vec_sum = packed[: 6 * width].reshape(6, devices, small_share)
-    vec_sum = lax.dynamic_index_in_dim(vec_sum, place, 1, keepdims=False)
-    up_bias = lax.dynamic_slice_in_dim(packed, 6 * width + place * unit_share, unit_share)
-    tables = packed[6 * width + units :].reshape(2, fsdp, HEADS // fsdp, 2 * GRID - 1)
+    vec_sum = lax.dynamic_slice_in_dim(vec_all[:6], place * vector_share, vector_share, 1)
+    up_bias = vec_all[6 : 6 + units // width].reshape(units)
+    up_bias = lax.dynamic_slice_in_dim(up_bias, place * unit_share, unit_share)
+    tables = vec_all[6 + units // width :][:2, : HEADS * (2 * GRID - 1)].reshape(2, fsdp, -1, 2 * GRID - 1)
     tables = lax.dynamic_index_in_dim(tables, lax.axis_index("fsdp"), 1, keepdims=False)
 
     return (
@@ -855,7 +1150,7 @@
         vec_sum[0],
         vec_sum[1],
         mixed_sum[:qkv_share].T,
-        time_grad,
+        time_grad[:, :time_share],
         mixed_sum[qkv_share : qkv_share + out_share],
         vec_sum[4],
         vec_sum[2],

time: 894 us -> 642 us (0.72)
  Pallas kernels: 706 us -> 587 us
  local copies, waits for them, and re-layouts: 88.9 us -> 31.8 us
  blocking collectives: 40.9 us -> 0 us
  between operations: 15.4 us -> 1.19 us
  starting transfers between devices: 13.1 us -> 0 us
    pallas_call x7 -> x4, Pallas kernels: 572 us -> 454 us  [the longest x1 133 us: attend_back(): pl.pallas_call(functools.partial(attend_back_kernel, block, scale, dims,...]
    psum x1 -> x0, blocking collectives: 40.9 us -> none  [local(): packed = lax.psum(jnp.concatenate(packed), AXES)]
    transpose x5 -> x0, local copies, waits for them, and re-layouts: 18.8 us -> none  [the longest x2 11.2 us: local(): qkv_full = qkv_rows.transpose(1, 0, 2, 3).reshape(HEADS, 3 * LANES, width)]
    all_to_all x2 -> x0, starting transfers between devices: 13.1 us -> none  [the longest x1 7.28 us: local(): lax.all_to_all(time_part.reshape(devices, per, share), AXES, 0, 0, tiled=...]
    reshape x12 -> x4, local copies, waits for them, and re-layouts: 13.2 us -> 0.21 us  [the longest x1 0.1 us: local(): tables = tables.reshape(2, HEADS * (2 * GRID - 1))]
    concatenate x3 -> x2, local copies, waits for them, and re-layouts: 17.5 us -> 4.78 us  [the longest x1 4.78 us: local(): jnp.concatenate([norm1_gain, norm1_bias, out_bias, norm2_gain, norm2_bias...]
  transfers between devices with their start and end apart: 3 -> 0, of which waited for: 1 -> 0; matrix products, arithmetic and copies ran while one was open for 6% -> 0% of each run, Pallas kernels for 35% -> 0%
where the time goes in v2:
time: 642 us; the launch traced here: 635 us
  Pallas kernels  587 us (91%)
  local copies, waits for them, and re-layouts  31.8 us (5%)
  other arithmetic  13.5 us (2%)
    pallas_call x1, Pallas kernels, attend_back(): pl.pallas_call(functools.partial(attend_back_kernel, block, scale, dims,...  133 us
    pallas_call x1, Pallas kernels, attend(): pl.pallas_call(functools.partial(attend_kernel, factor, block, dims, piec...  133 us
    pallas_call x1, Pallas kernels, end(): pl.pallas_call(functools.partial(end_kernel, dims, pieces, shares, head_d...  105 us
    pallas_call x1, Pallas kernels, mlp(): pl.pallas_call(mlp_kernel, grid=(units // block,), in_specs=[resident(nor...  94.1 us
    pallas_call x1, Pallas kernels, begin(): pl.pallas_call(functools.partial(begin_kernel, dims, pieces, shares, head...  82.9 us
    pallas_call x1, Pallas kernels, turn(): pl.pallas_call(turn_kernel, grid=(rows // block,), in_specs=[by_rows(widt...  28 us

profile of v2, /device:TPU:0, one launch (start us, length us, event | category | flops | bytes accessed | tf_op | source)
XLA Modules:
  0.0 635.3 jit_solution(7284180235048603829)
XLA Ops:
  0.7 0.7 convert_element_type.44
  1.5 0.8 reshape.213
  2.3 0.8 reshape.214
  3.1 4.8 concatenate.50
  7.9 0.7 fusion.15.small_shard
  8.6 1.1 copy.60
  9.7 0.8 pad.38.time_weight
  10.5 1.8 pad_maximum_fusion.1.mixed_shard
  12.3 82.9 %begin.1 = (bf16[16,384,1152]{2,1,0:T(8,128)(2,1)}, bf16[2048,1152]{1,0:T(8,128)(2,1)}, bf16[32,16,1152]{2,1,0:T(8,128)(2,1)}, f32[32,8,128]{2,1,0:T(8,128)}) custom-call(bf16[144,1152]{1,0:T(8,128)(2,1)} %pad_maximum_fusion.1.mixed_shard, bf16[16,1152]{1,0:T(8,128)(2,1)} %fusion.15.small_shard, bf16[1152,128]{1,0:T(8,128)(2,1)} %pad.38.time_weight), custom_call_target="tpu_custom_call" | custom-call | tf_op jit(solution)/shard_map/begin/pallas_call | solution.py:389
  95.2 0.8 slice_reduce_fusion.6
  96.1 0.6 fusion.3
  97.1 1.2 maximum_maximum_fusion.table
  98.3 1.2 slice.119
  99.9 0.7 slice.122.gain
  101.1 0.9 pad_convert_fusion.mask_k
  102.0 0.7 slice.124.shift
  102.7 0.3 iota_compare_fusion.3
  103.1 1.2 add_convert_fusion.onehot
  104.5 0.9 fusion.6.mask_q
  105.3 0.5 broadcast_in_dim.69.large
  105.8 132.8 %attend.1 = (bf16[1024,1152]{1,0:T(8,128)(2,1)}, bf16[16,1024,128]{2,1,0:T(8,128)(2,1)}, bf16[16,1024,128]{2,1,0:T(8,128)(2,1)}, bf16[16,1024,128]{2,1,0:T(8,128...) custom-call(bf16[1024,1152]{1,0:T(8,128)(2,1)} %tokens.5, ...), custom_call_target="tpu_custom_call" | custom-call | tf_op jit(solution)/shard_map/attend/pallas_call | solution.py:492
  238.7 0.7 slice.134.gain
  239.4 0.7 slice.132.bias
  240.1 0.7 slice.136.shift
  240.8 11.2 %project.1 = (f32[1024,1152]{1,0:T(8,128)}, bf16[1024,1152]{1,0:T(8,128)(2,1)}) custom-call(bf16[1024,1152]{1,0:T(8,128)(2,1)} %tokens.5, bf16[1024,2048]{1,0:T(8,128)(2,1)} %get-tuple-element.54.o, bf16[2048,1152]{1,0:T(8,128)(2,1)} %get-tuple-element.55.weight, f32[1,1152]{1,0:T(1,128)} %slice.132.bias, f32[1,1152]{1,0:T(1,128)} %slice.134.gain, ...), custom_call_target="tpu_custom_call" | custom-call | tf_op jit(solution)/shard_map/project/pallas_call | solution.py:658
  252.0 3.5 broadcast_select_fusion.dy
  255.6 0.7 reshape.223.bias
  256.3 94.1 %mlp.1 = (f32[1024,1152]{1,0:T(8,128)}, f32[1024,1152]{1,0:T(8,128)}, bf16[4608,1152]{1,0:T(8,128)(2,1)}, bf16[4608,1152]{1,0:T(8,128)(2,1)}, f32[1,4608]{1,0:T(1,128)}) custom-call(bf16[1024,1152]{1,0:T(8,128)(2,1)} %get-tuple-element.57.normed, bf16[1024,1152]{1,0:T(8,128)(2,1)} %broadcast_select_fusion.dy, bf16[4608,1152]{1,0:T(8,128)(2,1)} %bitcast.61, ...), custom_call_target="tpu_custom_call" | custom-call | tf_op jit(solution)/shard_map/mlp/pallas_call | solution.py:713
  350.4 0.7 slice.139.bias
  351.1 28.0 %turn.1 = (bf16[1024,1152]{1,0:T(8,128)(2,1)}, f32[1024,1152]{1,0:T(8,128)}, bf16[1024,2048]{1,0:T(8,128)(2,1)}, bf16[2048,1152]{1,0:T(8,128)(2,1)}, f32[4,1152]{1,0:T(4,128)}) custom-call(f32[1024,1152]{1,0:T(8,128)} %get-tuple-element.56.hidden, f32[1024,1152]{1,0:T(8,128)} %get-tuple-element.60.y, f32[1,1152]{1,0:T(1,128)} %slice.139.bias, ...), custom_call_target="tpu_custom_call" | custom-call | tf_op jit(solution)/shard_map/turn/pallas_call | solution.py:771
  379.1 133.3 %attend_back.1 = (bf16[1024,6144]{1,0:T(8,128)(2,1)}, bf16[16,384,1152]{2,1,0:T(8,128)(2,1)}, f32[16,8,128]{2,1,0:T(8,128)}, f32[16,8,128]{2,1,0:T(8,128)}, f32[...) custom-call(bf16[1024,1152]{1,0:T(8,128)(2,1)} %get-tuple-element.63.normed, ...), custom_call_target="tpu_custom_call" | custom-call | tf_op jit(solution)/shard_map/attend_back/pallas_call | solution.py:603
  512.4 1.2 fusion.31
  513.6 0.7 convolution_bitcast_fusion
  514.6 0.6 pad.43.vec_in
  515.2 1.5 pad_maximum_fusion.2.time_send
  516.8 105.2 %end.1 = (bf16[1024,1152]{1,0:T(8,128)(2,1)}, f32[16,1152]{1,0:T(8,128)}, f32[1152,128]{1,0:T(8,128)}, f32[144,1152]{1,0:T(8,128)}) custom-call(bf16[1024,1152]{1,0:T(8,128)(2,1)} %tokens.5, bf16[1024,6144]{1,0:T(8,128)(2,1)} %get-tuple-element.71.dqkv, bf16[6144,1152]{1,0:T(8,128)(2,1)} %bitcast.60, f32[1,1152]{1,0:T(1,128)} %slice.122.gain, ...), custom_call_target="tpu_custom_call" | custom-call | tf_op jit(solution)/shard_map/end/pallas_call | solution.py:956
  621.9 2.0 slice_bitcast_fusion
  623.9 2.0 copy.66
  626.0 1.6 slice.147
  627.6 0.8 slice.142
  628.4 0.5 slice_bitcast_fusion.5
  628.9 0.9 slice.151
  629.9 0.6 dynamic_slice.11
  630.5 0.8 slice.153
  631.4 0.6 dynamic-slice_bitcast_fusion
  632.0 1.4 copy.85
  633.4 0.8 copy.86
  634.2 0.8 copy.87
  (52 shorter events, 2.4 us)
Async XLA Ops:
  0.6 100.0 %copy-start.6 = (s32[4]{0:T(128)S(1)}, s32[4]{0:T(128)}, u32[]{:S(2)}) copy-start(s32[4]{0:T(128)} %param.20) | copy-start | bytes 52
  0.7 102.1 %copy-start.5 = (s32[1024]{0:T(1024)S(1)}, s32[1024]{0:T(1024)}, u32[]{:S(2)}) copy-start(s32[1024]{0:T(1024)} %param.22) | copy-start | bytes 12292
  379.1 135.3 %copy-start.3 = (f32[1,4608]{1,0:T(1,128)S(1)}, f32[1,4608]{1,0:T(1,128)}, u32[]{:S(2)}) copy-start(f32[1,4608]{1,0:T(1,128)} %get-tuple-element.76) | copy-start | bytes 55300
  379.1 135.4 %copy-start.4 = (f32[4,1152]{1,0:T(4,128)S(1)}, f32[4,1152]{1,0:T(4,128)}, u32[]{:S(2)}) copy-start(f32[4,1152]{1,0:T(4,128)} %get-tuple-element.75) | copy-start | bytes 55300
  621.9 10.1 %copy-start = (bf16[1024,1152]{1,0:T(8,128)(2,1)S(1)}, bf16[1024,1152]{1,0:T(8,128)(2,1)}, u32[]{:S(2)}) copy-start(bf16[1024,1152]{1,0:T(8,128)(2,1)} %get-tuple-element.197) | copy-start | bytes 7077892
  621.9 12.3 %copy-start.1 = (f32[144,1152]{1,0:T(8,128)S(1)}, f32[144,1152]{1,0:T(8,128)}, u32[]{:S(2)}) copy-start(f32[144,1152]{1,0:T(8,128)} %get-tuple-element.208) | copy-start | bytes 1990660
  631.4 2.0 copy-start.2

commit v3 on v2

--- a/solution.py
+++ b/solution.py
@@ -20,6 +20,49 @@
 HIGHEST = lax.Precision.HIGHEST
 MESH_ID = pl.DeviceIdType.MESH
 VMEM_LIMIT = 62 * 1024 * 1024
+
+
+BEGIN_ROWS = (32, 32, 32, 16, 16, 16)
+BEGIN_ORDER = ((
+    10, 0, 1, 40, 11, 30, 60, 2, 41, 12, 20, 42, 31, 61, 21, 13, 62, 3, 43, 32, 4, 50, 44, 63, 22, 51, 52, 33, 34,
+    14, 64, 23, 53, 24, 54,
+),)
+ATTEND_ORDER = (
+    (0,), (30,), (), (), (10, 1), (31,), (2,), (11, 32, 20), (), (), (21,), (12, 33, 3), (22,), (), (),
+    (13, 23, 4), (14, 24, 34),
+)
+MLP_ORDER = (
+    (10,), (), (11, 0), (12,), (1,), (2, 30, 13, 20), (31, 14, 3), (21, 4), (32,), (22, 33), (23,), (), (34, 24),
+)
+BACK_ORDER = (
+    (0,), (30, 10, 20, 1), (), (11,), (2,), (21,), (), (12, 31, 3), (22,), (4,), (13,), (), (23, 32), (), (33, 14),
+    (), (34, 24),
+)
+END_ORDER = (
+    (0,), (), (20, 1), (10, 2), (21,), (30, 11, 22, 40), (12, 50, 31), (), (), (51, 32, 41, 23), (), (3,), (13, 42),
+    (), (24, 52, 33), (43, 4), (53, 34, 44, 14, 54),
+)
+BACK_ORDER = (
+    (0,), (1, 50), (51, 30), (31,), (), (2, 20), (21, 52, 10, 32), (3, 40), (41, 53), (), (22, 33, 54, 42), (11, 23),
+    (43,), (12, 34), (4, 24, 13), (44,), (14,),
+)
+END_ORDER = (
+    (20,), (0, 21, 10), (1, 50), (), (22, 11), (30, 2), (23,), (51, 3, 12),
+    (52, 31, 40, 13, 60, 41, 53, 24, 4, 32, 61, 42, 33, 54, 43, 62, 63, 14, 34, 44, 64),
+)
+STAGES = 5
+
+
+def rounds_order(count, places, extra=False):
+    order = [[] for _ in range(places)]
+    last = count + STAGES - 2
+    for number in range(last + 1):
+        for k in range(count):
+            if 0 <= number - k < STAGES:
+                order[number * (places - 1) // last].append(k * 10 + number - k)
+    if extra:
+        order[-1] += [count * 10 + number for number in range(STAGES)]
+    return order
 
 
 def dot_nn(a, b):
@@ -118,8 +161,6 @@
 
 
 class Gather:
-    STAGES = 5
-
     def __init__(self, dims, pieces, sources, results, sems, own_sems):
         self.at = Place(dims)
         self.pieces, self.sources, self.results = pieces, sources, results
@@ -183,20 +224,13 @@
             for kind in (3, 5, 6, 7):
                 self.finish(k, kind, plane(at.p, at.q))
 
-    def round(self, number):
-        for k in range(len(self.pieces)):
-            if 0 <= number - k < self.STAGES:
-                self.stage(k, number - k)
-
-    def rounds(self):
-        return len(self.pieces) + self.STAGES - 1
-
 
 class Scatter:
-    STAGES = 5
-
-    def __init__(self, dims, pieces, sources, results, held, from_core, from_second, from_first, from_line, sems):
+    def __init__(
+        self, dims, pieces, shift, sources, results, held, from_core, from_second, from_first, from_line, sems
+    ):
         self.at = Place(dims)
+        self.shift = shift
         self.pieces, self.sources, self.results = pieces, sources, results
         self.held, self.from_core, self.from_second = held, from_core, from_second
         self.from_first, self.from_line, self.sems = from_first, from_line, sems
@@ -205,12 +239,13 @@
     def scratch(dims, pieces, width, in_place=False):
         G1, G2 = dims
         n = len(pieces)
+        most = max(piece[2] for piece in pieces)
         return [
-            pltpu.VMEM((8, LANES) if in_place else (n, G1, 2, G2, 2, PIECE, width), BF16),
-            pltpu.VMEM((n, G1, 2, G2, 2, PIECE, width), BF16),
-            pltpu.VMEM((n, 2, G1, G2, PIECE, width), BF16),
-            pltpu.VMEM((n, G1, G2, PIECE, width), BF16),
-            pltpu.VMEM((n, G1 * G2 - 1, PIECE, width), BF16),
+            pltpu.VMEM((8, LANES) if in_place else (n, G1, 2, G2, 2, most, width), BF16),
+            pltpu.VMEM((n, G1, 2, G2, 2, most, width), BF16),
+            pltpu.VMEM((n, 2, G1, G2, most, width), BF16),
+            pltpu.VMEM((n, G1, G2, most, width), BF16),
+            pltpu.VMEM((n, G1 * G2 - 1, most, width), BF16),
             pltpu.SemaphoreType.DMA((n, 5 + G1 * G2, 2)),
         ]
 
@@ -243,67 +278,85 @@
         every, every2 = at.whole
         both = pl.ds(0, 2)
         in_place = len(self.held.shape) == 2
+        some = pl.ds(0, count)
+        from_core = self.from_core.at[k, every, both, every2, both, some]
+        from_second = [self.from_second.at[k, i, every, every2, some] for i in range(2)]
+        from_first = self.from_first.at[k, every, every2, some]
+        from_line = [self.from_line.at[k, i, some] for i in range(at.G1 * at.G2 - 1)]
 
         def plane(p, q):
             if in_place:
                 return source.at[every, p, every2, at.c, q, rows]
-            return self.held.at[k, every, p, every2, q]
+            return self.held.at[k, every, p, every2, q, some]
 
         local_copy = lambda: pltpu.make_async_copy(
-            source.at[every, both, every2, at.c, both, rows], self.held.at[k], self.sems.at[k, 4, 0]
+            source.at[every, both, every2, at.c, both, rows],
+            self.held.at[k, every, both, every2, both, some],
+            self.sems.at[k, 4, 0],
         )
         if number == 0:
-            self.send(k, 0, source.at[every, both, every2, 1 - at.c, both, rows], self.from_core.at[k], at.sibling())
+            self.send(k, 0, source.at[every, both, every2, 1 - at.c, both, rows], from_core, at.sibling())
             if not in_place:
                 local_copy().start()
         if number == 1:
             if not in_place:
                 local_copy().wait()
-            wait_for(self.from_core.at[k], self.sems.at[k, 0, 1])
-            core = self.from_core.at[k]
+            wait_for(from_core, self.sems.at[k, 0, 1])
             for p, q in ((at.bp, at.bq), (1 - at.p, 1 - at.q)):
-                self.add(plane(p, q), core.at[every, p, every2, q])
-            self.send(k, 1, plane(at.bp, at.bq), self.from_second.at[k, 0], at.second())
-            self.send(k, 2, plane(1 - at.p, 1 - at.q), self.from_second.at[k, 1], at.second())
+                self.add(plane(p, q), from_core.at[every, p, every2, q])
+            self.send(k, 1, plane(at.bp, at.bq), from_second[0], at.second())
+            self.send(k, 2, plane(1 - at.p, 1 - at.q), from_second[1], at.second())
             for p, q in ((at.p, at.q), (at.ap, at.aq)):
-                self.add(plane(p, q), core.at[every, p, every2, q])
+                self.add(plane(p, q), from_core.at[every, p, every2, q])
         if number == 2:
             for kind in (1, 2):
-                wait_for(self.from_second.at[k, kind - 1], self.sems.at[k, kind, 1])
-            self.add(plane(at.ap, at.aq), self.from_second.at[k, 1])
-            self.send(k, 3, plane(at.ap, at.aq), self.from_first.at[k], at.first())
-            self.add(plane(at.p, at.q), self.from_second.at[k, 0])
+                wait_for(from_second[kind - 1], self.sems.at[k, kind, 1])
+            self.add(plane(at.ap, at.aq), from_second[1])
+            self.send(k, 3, plane(at.ap, at.aq), from_first, at.first())
+            self.add(plane(at.p, at.q), from_second[0])
         if number == 3:
-            wait_for(self.from_first.at[k], self.sems.at[k, 3, 1])
-            self.add(plane(at.p, at.q), self.from_first.at[k])
+            wait_for(from_first, self.sems.at[k, 3, 1])
+            self.add(plane(at.p, at.q), from_first)
             mine = plane(at.p, at.q)
             for i, spot in enumerate(at.line()):
-                self.send(k, 5 + i, mine.at[spot[0], spot[1]], self.from_line.at[k, i], at.on_line(spot))
+                self.send(k, 5 + i, mine.at[spot[0], spot[1]], from_line[i], at.on_line(spot))
         if number == 4:
             total = plane(at.p, at.q)[at.g1, at.g2].astype(F32)
             for i in range(at.G1 * at.G2 - 1):
-                wait_for(self.from_line.at[k, i], self.sems.at[k, 5 + i, 1])
-                total = total + self.from_line[k, i].astype(F32)
-            self.results[array][rows] = total
-            wait_for(self.from_core.at[k], self.sems.at[k, 0, 0])
+                wait_for(from_line[i], self.sems.at[k, 5 + i, 1])
+                total = total + from_line[i][...].astype(F32)
+            self.results[array][pl.ds(start - self.shift, count)] = total
+            wait_for(from_core, self.sems.at[k, 0, 0])
             for kind in (1, 2):
-                wait_for(self.from_second.at[k, kind - 1], self.sems.at[k, kind, 0])
-            wait_for(self.from_first.at[k], self.sems.at[k, 3, 0])
+                wait_for(from_second[kind - 1], self.sems.at[k, kind, 0])
+            wait_for(from_first, self.sems.at[k, 3, 0])
             for i in range(at.G1 * at.G2 - 1):
-                wait_for(self.from_line.at[k, i], self.sems.at[k, 5 + i, 0])
-
-    def round(self, number):
-        for k in range(len(self.pieces)):
-            if 0 <= number - k < self.STAGES:
-                self.stage(k, number - k)
-
-    def rounds(self):
-        return len(self.pieces) + self.STAGES - 1
-
-
-def pieces_of(shards):
-    per = [(array, start, PIECE) for array, shard in enumerate(shards) for start in range(0, shard, PIECE)]
-    return sorted(per, key=lambda piece: piece[1])
+                wait_for(from_line[i], self.sems.at[k, 5 + i, 0])
+
+
+def pieces_of(first, last):
+    return [(array, start, PIECE) for start in range(first, last, PIECE) for array in range(2)]
+
+
+def early_rows(rows):
+    return max(PIECE, rows - PIECE)
+
+
+def summed_rows(rows):
+    return PIECE if rows > PIECE else 0
+
+
+def cut(array, rows, sizes):
+    if sum(sizes) != rows:
+        sizes = (PIECE,) * (rows // PIECE)
+    return [(array, sum(sizes[:i]), size) for i, size in enumerate(sizes)]
+
+
+def order_for(order, pieces, places, extra=False):
+    count = len(pieces) + extra
+    if sum(len(place) for place in order) == count * STAGES:
+        return order
+    return rounds_order(len(pieces), places, extra)
 
 
 def pad_rows(shard):
@@ -339,16 +392,16 @@
     wait_for(view, sems.at[0])
 
 
-def begin_kernel(dims, pieces, shares, head_dim, mixed_shard, small_shard, time_weight, qkv_out, out_out, small_out,
+def begin_kernel(dims, pieces, order, shares, head_dim, mixed_shard, small_shard, time_weight, qkv_out, out_out, small_out,
                  time_out, mixed, small, time_all, time_got, sems, own_sems, time_sems):
     work = Gather(dims, pieces, (small_shard, mixed_shard), (small, mixed), sems, own_sems)
     at = work.at
     devices = at.count()
     width = mixed.shape[-1]
     at.barrier_all()
-    for number in range(work.rounds()):
-        work.round(number)
-        if number == Gather.STAGES - 1:
+    for event in order:
+        work.stage(*divmod(event, 10))
+        if event == STAGES - 1:
             small_out[...] = small[...].reshape(small_out.shape)
             for start in range(0, devices, 32):
                 span = pl.ds(start, 32)
@@ -383,11 +436,12 @@
     width = mixed_shard.shape[1]
     small_rows = small_shard.shape[0]
     devices = dims[0] * dims[1] * 8
-    pieces = [(0, 0, small_rows)] + [(1, start, PIECE) for start in range(0, mixed_shard.shape[0], PIECE)]
+    pieces = [(0, 0, small_rows)] + cut(1, mixed_shard.shape[0], BEGIN_ROWS)
+    (order,) = order_for(BEGIN_ORDER, pieces, 1)
     anywhere = pl.BlockSpec(memory_space=pl.ANY)
     vmem = pl.BlockSpec(memory_space=pltpu.VMEM)
     return pl.pallas_call(
-        functools.partial(begin_kernel, dims, pieces, shares, head_dim),
+        functools.partial(begin_kernel, dims, pieces, order, shares, head_dim),
         in_specs=[anywhere, anywhere, vmem],
         out_specs=[vmem] * 4,
         out_shape=[
@@ -422,17 +476,16 @@
     return inverse * (scaled - inner), unit
 
 
-def spaced(work, step, steps):
-    last = work.rounds() - 1
-    for number in range(last):
-        at_step = number * steps // last
-
-        @pl.when(step == at_step)
-        def _(number=number):
-            work.round(number)
-
-
-def attend_kernel(factor, block, dims, pieces, tokens, gain, shift, weight, time_q, time_v, large, table, onehot,
+def events(order, step, work, place):
+    if order[place]:
+
+        @pl.when(step == place)
+        def _():
+            for event in order[place]:
+                work.stage(*divmod(event, 10))
+
+
+def attend_kernel(factor, block, dims, pieces, order, tokens, gain, shift, weight, time_q, time_v, large, table, onehot,
                   mask_q, mask_k, up_shard, down_shard,
                   normed_out, q_out, k_out, v_out, o_out, p_out, up_out, down_out, keys, sems, own_sems):
     rows = tokens.shape[0]
@@ -443,7 +496,8 @@
     def _():
         work.at.barrier()
 
-    spaced(work, step, HEADS)
+    for place in range(HEADS):
+        events(order, step, work, place)
 
     @pl.when(pl.program_id(0) == 0)
     def _():
@@ -479,18 +533,19 @@
 
     @pl.when(step == HEADS - 1)
     def _():
-        work.round(work.rounds() - 1)
+        for event in order[HEADS]:
+            work.stage(*divmod(event, 10))
 
 
 def attend(tokens, gain, shift, weight, times, large, table, onehot, mask_q, mask_k, factor, shards, dims):
     rows, width = tokens.shape
     block = min(256, rows)
-    pieces = pieces_of([shard.shape[0] for shard in shards])
+    pieces = pieces_of(0, early_rows(shards[0].shape[0]))
     anywhere = pl.BlockSpec(memory_space=pl.ANY)
     per_head = lambda *shape: pl.BlockSpec((1,) + shape, lambda h: (h, 0, 0))
     head_rows = jax.ShapeDtypeStruct((HEADS, rows, LANES), BF16)
     return pl.pallas_call(
-        functools.partial(attend_kernel, factor, block, dims, pieces),
+        functools.partial(attend_kernel, factor, block, dims, pieces, order_for(ATTEND_ORDER, pieces, HEADS + 1)),
         grid=(HEADS,),
         in_specs=[
             resident(tokens.shape),
@@ -532,18 +587,19 @@
     )(tokens, gain, shift, weight, times, times, large, table, onehot, mask_q, mask_k, *shards)
 
 
-def attend_back_kernel(block, scale, dims, pieces, normed, p, q, k, v, do, o, onehot, large, d_up, d_down,
+def attend_back_kernel(block, scale, dims, pieces, shift, order, normed, p, q, k, v, do, o, onehot, large, d_up, d_down,
                        dqkv_out, dw_out, sums_q, sums_v, pair_out, up_out, down_out,
                        keys, grads, dk_sum, dv_sum, *buffers):
     rows = normed.shape[0]
-    work = Scatter(dims, pieces, (d_up, d_down), (up_out, down_out), *buffers)
+    work = Scatter(dims, pieces, shift, (d_up, d_down), (up_out, down_out), *buffers)
     step = pl.program_id(0)
 
     @pl.when(step == 0)
     def _():
         work.at.barrier()
 
-    spaced(work, step, HEADS)
+    for place in range(HEADS):
+        events(order, step, work, place)
     lane = lax.broadcasted_iota(jnp.int32, (rows, LANES), 1)
     head = 72
     delta = jnp.sum(do[...].astype(F32) * o[...].astype(F32), axis=1, keepdims=True)
@@ -590,18 +646,23 @@
 
     @pl.when(step == HEADS - 1)
     def _():
-        work.round(work.rounds() - 1)
+        for event in order[HEADS]:
+            work.stage(*divmod(event, 10))
 
 
 def attend_back(normed, p, q, k, v, do, o, onehot, large, scale, parts, dims):
     rows, width = normed.shape
     block = min(256, rows)
-    pieces = pieces_of([part.shape[5] for part in parts])
+    shift = summed_rows(parts[0].shape[5])
+    pieces = pieces_of(shift, parts[0].shape[5])
+    sum_shape = (parts[0].shape[5] - shift, width)
     anywhere = pl.BlockSpec(memory_space=pl.ANY)
     per_head = lambda *shape: pl.BlockSpec((1,) + shape, lambda h: (h, 0, 0))
     head_cols = pl.BlockSpec((rows, LANES), lambda h: (0, h))
     return pl.pallas_call(
-        functools.partial(attend_back_kernel, block, scale, dims, pieces),
+        functools.partial(
+            attend_back_kernel, block, scale, dims, pieces, shift, order_for(BACK_ORDER, pieces, HEADS + 1)
+        ),
         grid=(HEADS,),
         in_specs=[
             resident(normed.shape),
@@ -622,7 +683,7 @@
             per_head(8, LANES),
             per_head(8, LANES),
             per_head(LANES, LANES),
-            *[resident(part.shape[5:]) for part in parts],
+            *[resident(sum_shape) for _ in parts],
         ],
         out_shape=[
             jax.ShapeDtypeStruct((rows, HEADS * 3 * LANES), BF16),
@@ -630,7 +691,7 @@
             jax.ShapeDtypeStruct((HEADS, 8, LANES), F32),
             jax.ShapeDtypeStruct((HEADS, 8, LANES), F32),
             jax.ShapeDtypeStruct((HEADS, LANES, LANES), F32),
-            *[jax.ShapeDtypeStruct(part.shape[5:], F32) for part in parts],
+            *[jax.ShapeDtypeStruct(sum_shape, F32) for _ in parts],
         ],
         scratch_shapes=[
             pltpu.VMEM((rows, 2 * LANES), BF16),
@@ -678,53 +739,196 @@
     return jnp.where(u >= 0.0, 1.0 - tail, tail), bell * (1.0 / math.sqrt(2.0 * math.pi))
 
 
-def mlp_kernel(normed, dy, up, down, bias, y_out, dn_out, dup_out, ddown_out, dbias_out):
+BLOCK = (2, 2, 1, 2, 2)
+BLOCK_DEVICES = 16
+
+
+def block_of(ref, i, rows):
+    whole = [pl.ds(0, size) for size in BLOCK]
+    if len(ref.shape) == 7:
+        return ref.at[(pl.ds(2 * i, 2), *whole[1:], rows)]
+    return ref.at[(i, *whole, rows)]
+
+
+def mlp_kernel(dims, block, blocks, gathers, sums, order, *refs):
+    refs = list(refs)
+    take = lambda count: [refs.pop(0) for _ in range(count)]
+    normed, dy, bias, *early = take(5)
+    shards = take(2) if gathers else None
+    y_out, dn_out, dbias_out, *grads_out = take(5)
+    late = take(2) if gathers else None
+    totals = take(2) if sums else None
+    weights, grads, act_all, du_all, weight_sems, grad_sems = take(6)
+    if gathers:
+        first_late = early[0].shape[-2] - PIECE
+        shards = [shard.at[pl.ds(first_late, PIECE)] for shard in shards]
+        gather = Gather(dims, gathers, shards, late, *take(2))
+    if sums:
+        scatter = Scatter(dims, sums, 0, grads_out, totals, *refs)
     rows = normed.shape[0]
-    first = pl.program_id(0) == 0
-    u = dot_nt(normed[...], up[...]) + bias[...]
-    phi, density = normal_parts(u)
-    act = (u * phi).astype(BF16)
-    slope = phi + u * density
-    du = (slope * dot_nt(dy[...], down[...])).astype(BF16)
-    dbias_out[...] = jnp.sum(du.astype(F32), axis=0, keepdims=True)
-    y = dot_nn(act, down[...])
-    dn = dot_nn(du, up[...])
-
-    @pl.when(first)
+    units = act_all.shape[1]
+    step = pl.program_id(0)
+    steps = pl.num_programs(0)
+    late_step = steps - blocks if gathers else steps
+
+    def copies(target_step, source):
+        slot = target_step % 2
+        i = target_step % blocks
+        rows_of = pl.ds(pl.multiple_of(target_step // blocks * PIECE, PIECE), PIECE)
+        return [
+            pltpu.make_async_copy(block_of(source[array], i, rows_of), weights.at[slot, array], weight_sems.at[slot, array])
+            for array in range(2)
+        ]
+
+    def late_copies(target_step):
+        slot = target_step % 2
+        i = target_step % blocks
+        return [
+            pltpu.make_async_copy(
+                block_of(late[array], i, pl.ds(0, PIECE)), weights.at[slot, array], weight_sems.at[slot, array]
+            )
+            for array in range(2)
+        ]
+
+    def write_copies(target_step):
+        slot = target_step % 2
+        i = target_step % blocks
+        rows_of = pl.ds(pl.multiple_of(target_step // blocks * PIECE, PIECE), PIECE)
+        return [
+            pltpu.make_async_copy(grads.at[slot, array], block_of(grads_out[array], i, rows_of), grad_sems.at[slot, array])
+            for array in range(2)
+        ]
+
+    def happen(place, at_step):
+        if gathers and order[place]:
+
+            @pl.when(step == at_step)
+            def _():
+                for event in order[place]:
+                    k, number = divmod(event, 10)
+                    if k < len(gathers):
+                        gather.stage(k, number)
+                    else:
+                        scatter.stage(k - len(gathers), number)
+
+    @pl.when(step == 0)
     def _():
-        y_out[...] = y
-        dn_out[...] = dn
-
-    @pl.when(jnp.logical_not(first))
+        if gathers:
+            gather.at.barrier()
+        for copy in copies(0, early):
+            copy.start()
+        y_out[...] = jnp.zeros_like(y_out)
+        dn_out[...] = jnp.zeros_like(dn_out)
+
+    for place in range(0, len(order) - 1, 2):
+        happen(place, place // 2)
+    for copy in copies(step, early):
+        copy.wait()
+
+    @pl.when(step + 1 < late_step)
     def _():
-        y_out[...] += y
-        dn_out[...] += dn
-
-    ddown_out[...] = dot_tn(act, dy[...]).astype(BF16)
-    dup_out[...] = dot_tn(du, normed[...]).astype(BF16)
-
-
-def mlp(normed, dy, up, down, bias):
+        for copy in copies(step + 1, early):
+            copy.start()
+
+    if gathers:
+
+        @pl.when((step + 1 > late_step) & (step + 1 < steps))
+        def _():
+            for copy in late_copies(step + 1):
+                copy.start()
+
+    slot = step % 2
+    up = weights[slot, 0].reshape(units, -1)
+    down = weights[slot, 1].reshape(units, -1)
+    total = jnp.zeros((1, units), F32)
+    for start in range(0, rows, block):
+        span = pl.ds(start, block)
+        if start == rows // 2:
+
+            @pl.when(step >= 1)
+            def _():
+                for copy in write_copies(step - 1):
+                    copy.wait()
+
+            for place in range(1, len(order) - 1, 2):
+                happen(place, place // 2)
+            if gathers:
+
+                @pl.when(step + 1 == late_step)
+                def _():
+                    for copy in late_copies(step + 1):
+                        copy.start()
+
+        u = dot_nt(normed[span], up) + bias[0]
+        phi, density = normal_parts(u)
+        act = (u * phi).astype(BF16)
+        slope = phi + u * density
+        du = (slope * dot_nt(dy[span], down)).astype(BF16)
+        total = total + jnp.sum(du.astype(F32), axis=0, keepdims=True)
+        act_all[span] = act
+        du_all[span] = du
+        y_out[span] += dot_nn(act, down)
+        dn_out[span] += dot_nn(du, up)
+    dbias_out[0] = total
+    grads[slot, 0] = dot_tn(du_all[...], normed[...]).astype(BF16).reshape(grads.shape[2:])
+    grads[slot, 1] = dot_tn(act_all[...], dy[...]).astype(BF16).reshape(grads.shape[2:])
+    for copy in write_copies(step):
+        copy.start()
+
+    @pl.when(step == steps - 1)
+    def _():
+        for copy in write_copies(step):
+            copy.wait()
+
+    happen(len(order) - 1, steps - 1)
+
+
+def mlp(normed, dy, bias, weights, shards, dims):
     rows, width = normed.shape
-    units = up.shape[0]
-    block = 512
-    by_units = pl.BlockSpec((block, width), lambda i: (i, 0))
-    by_bias = pl.BlockSpec((1, block), lambda i: (0, i))
-    return pl.pallas_call(
-        mlp_kernel,
-        grid=(units // block,),
-        in_specs=[resident(normed.shape), resident(dy.shape), by_units, by_units, by_bias],
-        out_specs=[resident(normed.shape), resident(normed.shape), by_units, by_units, by_bias],
+    shard_rows = shards[0].shape[0]
+    devices = dims[0] * dims[1] * 8
+    blocks = devices // BLOCK_DEVICES
+    steps = blocks * shard_rows // PIECE
+    units = BLOCK_DEVICES * PIECE
+    overlap = shard_rows > PIECE
+    gathers = pieces_of(0, PIECE) if overlap else []
+    sums = pieces_of(0, PIECE) if overlap else []
+    anywhere = pl.BlockSpec(memory_space=pl.ANY)
+    by_step = pl.BlockSpec((1, 1, units), lambda i: (i, 0, 0))
+    spread = spread_of(dims)
+    if dims[1] > 1:
+        weights = [weight.reshape((blocks,) + BLOCK + (shard_rows, width)) for weight in weights]
+    landing = jax.ShapeDtypeStruct(spread + (PIECE, width), BF16)
+    total = jax.ShapeDtypeStruct((PIECE, width), F32)
+    order = order_for(MLP_ORDER, gathers + sums, 2 * steps + 1)
+    y, dn, dbias, d_up, d_down, *rest = pl.pallas_call(
+        functools.partial(mlp_kernel, dims, min(256, rows), blocks, gathers, sums, order),
+        grid=(steps,),
+        in_specs=[resident(normed.shape), resident(dy.shape), by_step, anywhere, anywhere]
+        + [anywhere, anywhere] * overlap,
+        out_specs=[resident(normed.shape), resident(normed.shape), by_step, anywhere, anywhere]
+        + ([anywhere] * 2 + [resident((PIECE, width))] * 2) * overlap,
         out_shape=[
             jax.ShapeDtypeStruct(normed.shape, F32),
             jax.ShapeDtypeStruct(normed.shape, F32),
-            jax.ShapeDtypeStruct(up.shape, BF16),
-            jax.ShapeDtypeStruct(down.shape, BF16),
-            jax.ShapeDtypeStruct((1, units), F32),
-        ],
-        compiler_params=params(),
+            jax.ShapeDtypeStruct(bias.shape, F32),
+            *[jax.ShapeDtypeStruct(weight.shape, BF16) for weight in weights],
+            *([landing] * 2 + [total] * 2) * overlap,
+        ],
+        scratch_shapes=[
+            pltpu.VMEM((2, 2) + BLOCK + (PIECE, width), BF16),
+            pltpu.VMEM((2, 2) + BLOCK + (PIECE, width), BF16),
+            pltpu.VMEM((rows, units), BF16),
+            pltpu.VMEM((rows, units), BF16),
+            pltpu.SemaphoreType.DMA((2, 2)),
+            pltpu.SemaphoreType.DMA((2, 2)),
+            *(Gather.scratch(dims, gathers) + Scatter.scratch(dims, sums, width) if overlap else []),
+        ],
+        compiler_params=params(collective_id=5, has_side_effects=True) if overlap else params(),
         name="mlp",
-    )(normed, dy, up, down, bias)
+    )(normed, dy, bias, *weights, *(shards if overlap else []))
+    whole = spread + (shard_rows, width)
+    return y, dn, dbias, d_up.reshape(whole), d_down.reshape(whole), rest[2:]
 
 
 def turn_kernel(hidden, y, bias, dn, dy, gain, weight, o, out, dh_out, do_out, dw_out, vec_out, dw_sum):
@@ -796,8 +1000,6 @@
 
 
 class SumAll:
-    STAGES = 5
-
     def __init__(self, at, total, send, got, sems):
         self.at, self.total, self.send, self.got, self.sems = at, total, send, got, sems
 
@@ -858,12 +1060,12 @@
             self.total[...] = total
 
 
-def end_kernel(dims, pieces, shares, head_dim, tokens, dqkv, weight, gain, dh, small, time_send, vec_in, dw, dw_out,
+def end_kernel(dims, pieces, order, shares, head_dim, tokens, dqkv, weight, gain, dh, small, time_send, vec_in, dw, dw_out,
                out, vec_out, time_out, mixed_out, mixed, dw_buffer, dw_sems, time_got, time_sems,
                vec_total, vec_send, vec_got, vec_sems, *buffers):
     step = pl.program_id(0)
     steps = pl.num_programs(0)
-    work = Scatter(dims, pieces, (mixed,), (mixed_out,), *buffers)
+    work = Scatter(dims, pieces, 0, (mixed,), (mixed_out,), *buffers)
     at = work.at
     sums = SumAll(at, vec_total, vec_send, vec_got, vec_sems)
     width = tokens.shape[1]
@@ -912,15 +1114,9 @@
                     head = (number - HEADS) * 2 + i
                     value = dw_buffer[number % 2, i * LANES : i * LANES + head_dim]
                     put(head * head_dim, shares[1], shares[0], value)
-        work.round(0)
-
-    @pl.when(step == 3)
-    def _():
-        work.round(1)
-
-    @pl.when(step == 6)
-    def _():
-        work.round(2)
+
+    for place in range(len(order) - 1):
+        events(order, step, work, place)
 
     dn = dot_nn(dqkv[...], weight[...])
     back, unit = norm_back(tokens[...].astype(F32), gain[...], dn)
@@ -930,14 +1126,14 @@
 
     @pl.when(step == steps - 1)
     def _():
-        sums.stage(0)
+        for event in order[-1]:
+            k, number = divmod(event, 10)
+            if k == len(pieces):
+                sums.stage(number)
+            else:
+                work.stage(k, number)
         exchanged(at, time_got, time_sems)
         time_got[at.index(), 0:8] = time_send[at.index()]
-        for number in range(3, max(work.rounds(), 7)):
-            if number < work.rounds():
-                work.round(number)
-            if number < 7:
-                sums.stage(number - 2)
         vec_out[...] = vec_total[...]
         times = time_got[...].reshape(small.shape[0], LANES)
         high = times.astype(BF16)
@@ -950,11 +1146,12 @@
     block = rows // 8
     by_rows = lambda cols: pl.BlockSpec((block, cols), lambda i: (i, 0))
     shard_rows = -(-sum(shares) // PIECE) * PIECE
-    pieces = pieces_of([shard_rows])
+    pieces = cut(0, shard_rows, BEGIN_ROWS)
+    order = order_for(END_ORDER, pieces, rows // block + 1, True)
     anywhere = pl.BlockSpec(memory_space=pl.ANY)
     devices = time_send.shape[0]
     return pl.pallas_call(
-        functools.partial(end_kernel, dims, pieces, shares, head_dim),
+        functools.partial(end_kernel, dims, pieces, order, shares, head_dim),
         grid=(rows // block,),
         in_specs=[
             by_rows(width),
@@ -1050,7 +1247,11 @@
     vectors = gathered[:, : 6 * vector_share].reshape(devices, 6, vector_share).transpose(1, 0, 2)
     vectors = vectors.reshape(6, width).astype(F32)
     gain_one, shift_one, b_out, gain_two, shift_two, b_down = (vectors[i : i + 1] for i in range(6))
-    b_up = gathered[:, 6 * vector_share : 6 * vector_share + unit_share].reshape(1, units).astype(F32)
+    b_up = gathered[:, 6 * vector_share : 6 * vector_share + unit_share].astype(F32)
+    b_up = jnp.pad(b_up, ((0, 0), (0, -unit_share % PIECE)))
+    b_up = b_up.reshape(devices // BLOCK_DEVICES, BLOCK_DEVICES, b_up.shape[1] // PIECE, PIECE)
+    b_up = b_up.transpose(2, 0, 1, 3).reshape(-1, 1, BLOCK_DEVICES * PIECE)
+    unit_shards = (pad_rows(fc1_weight.T), pad_rows(fc2_weight))
     tables = small[:fsdp, per + 1, : 2 * table_size].reshape(fsdp, 2, HEADS // fsdp, 2 * GRID - 1)
     tables = tables.transpose(1, 0, 2, 3).reshape(2 * HEADS, 2 * GRID - 1)
 
@@ -1097,24 +1298,22 @@
     large_lanes = jnp.broadcast_to(large.astype(F32), (1, LANES))
     normed_one, q, k, v, o, p, up, down = attend(
         tokens, gain_one, shift_one, qkv_full, times, large_lanes, table, onehot, mask_q, mask_k,
-        scale * math.log2(math.e), (pad_rows(fc1_weight.T), pad_rows(fc2_weight)), dims,
+        scale * math.log2(math.e), unit_shards, dims,
     )
-    up = up.reshape(devices, -1, width)[:, :unit_share].reshape(units, width)
-    down = down.reshape(devices, -1, width)[:, :unit_share].reshape(units, width)
     hidden, normed_two = project(tokens, o, out_full, b_out, gain_two, shift_two)
     dy = jnp.where(valid[:, None], cotangent, jnp.zeros_like(cotangent))
-    y, dn_two, d_up, d_down, db_up = mlp(normed_two, dy, up, down, b_up)
+    y, dn_two, db_up, d_up, d_down, first_sums = mlp(normed_two, dy, b_up, (up, down), unit_shards, dims)
+    db_up = db_up.reshape(-1, devices // BLOCK_DEVICES, BLOCK_DEVICES, PIECE).transpose(1, 2, 0, 3)
+    db_up = db_up.reshape(devices, -1)[:, :unit_share]
     layer_out, dh, do, d_out, vec_two = turn(hidden, y, b_down, dn_two, dy, gain_two, out_full, o)
-
-    def by_device(full, share):
-        full = full.reshape(devices, share, width)
-        full = jnp.pad(full, ((0, 0), (0, -share % PIECE), (0, 0)))
-        return full.reshape(spread_of(dims) + full.shape[1:])
 
     dqkv, d_qkv, sums_q, sums_v, pair, up_sum, down_sum = attend_back(
         normed_one, p, q, k, v, do, o, onehot, large_lanes, scale,
-        (by_device(d_up, unit_share), by_device(d_down, unit_share)), dims,
+        (d_up, d_down), dims,
     )
+    if first_sums:
+        up_sum = jnp.concatenate([first_sums[0], up_sum], axis=0)
+        down_sum = jnp.concatenate([first_sums[1], down_sum], axis=0)
     time_send = jnp.concatenate([sums_q, sums_v], axis=0)
     if time_share != head_dim:
         time_send = time_send[:, :per, :head_dim].transpose(1, 0, 2).reshape(per, devices, time_share)

time: 642 us -> 576 us (0.90)
  Pallas kernels: 587 us -> 521 us
    pallas_call x1, Pallas kernels: 133 us -> 95.9 us  [attend(): pl.pallas_call(functools.partial(attend_kernel, factor, block, dims, piec...]
    pallas_call x1, Pallas kernels: 133 us -> 108 us  [attend_back(): pl.pallas_call(functools.partial(attend_back_kernel, block, scale, dims,...]
where the time goes in v3:
time: 576 us; the launch traced here: 572 us
  Pallas kernels  521 us (90%)
  local copies, waits for them, and re-layouts  30.4 us (5%)
  other arithmetic  17 us (3%)
    pallas_call x1, Pallas kernels, mlp(): pl.pallas_call(functools.partial(mlp_kernel, dims, min(256, rows), blocks...  109 us
    pallas_call x1, Pallas kernels, attend_back(): pl.pallas_call(functools.partial(attend_back_kernel, block, scale, dims,...  108 us
    pallas_call x1, Pallas kernels, attend(): pl.pallas_call(functools.partial(attend_kernel, factor, block, dims, piec...  95.9 us
    pallas_call x1, Pallas kernels, end(): pl.pallas_call(functools.partial(end_kernel, dims, pieces, order, shares,...  88.6 us
    pallas_call x1, Pallas kernels, begin(): pl.pallas_call(functools.partial(begin_kernel, dims, pieces, order, share...  79.9 us
    pallas_call x1, Pallas kernels, turn(): pl.pallas_call(turn_kernel, grid=(rows // block,), in_specs=[by_rows(widt...  27.8 us

profile of v3, /device:TPU:0, one launch (start us, length us, event | category | flops | bytes accessed | tf_op | source)
XLA Modules:
  0.0 571.7 jit_solution(13171132634977092765)
XLA Ops:
  2.0 0.7 convert_element_type.40
  2.7 4.8 concatenate.56
  7.5 0.8 reshape.197
  8.3 0.8 reshape.198
  9.2 0.7 select_reduce_fusion
  10.2 0.7 add_select_fusion.2
  10.9 0.7 fusion.15.small_shard
  11.9 0.9 pad_convert_fusion.mask_k
  13.0 0.9 fusion.6.mask_q
  14.2 1.2 add_convert_fusion.onehot
  15.4 1.1 copy.66
  16.5 0.8 pad.38.time_weight
  17.3 1.8 pad_maximum_fusion.2.mixed_shard
  19.0 1.8 broadcast_select_fusion.refs_1_.dy
  20.8 79.9 %begin.1 = (bf16[16,384,1152]{2,1,0:T(8,128)(2,1)}, bf16[2048,1152]{1,0:T(8,128)(2,1)}, bf16[32,16,1152]{2,1,0:T(8,128)(2,1)}, f32[32,8,128]{2,1,0:T(8,128)}) custom-call(bf16[144,1152]{1,0:T(8,128)(2,1)} %pad_maximum_fusion.2.mixed_shard, bf16[16,1152]{1,0:T(8,128)(2,1)} %fusion.15.small_shard, bf16[1152,128]{1,0:T(8,128)(2,1)} %pad.38.time_weight), custom_call_target="tpu_custom_call" | custom-call | tf_op jit(solution)/shard_map/begin/pallas_call | solution.py:443
  100.7 0.8 slice_reduce_fusion.6
  101.6 1.2 slice.119
  103.1 0.7 reshape.209.refs_2_
  104.1 0.7 slice.139.bias
  104.8 0.7 slice.134.gain
  105.5 0.7 slice.122.gain
  106.2 0.7 slice.136.shift
  106.9 0.7 slice.132.bias
  107.7 0.7 slice.124.shift
  108.4 0.6 fusion.3
  109.3 1.2 maximum_maximum_fusion.table
  110.4 95.9 %attend.1 = (bf16[1024,1152]{1,0:T(8,128)(2,1)}, bf16[16,1024,128]{2,1,0:T(8,128)(2,1)}, bf16[16,1024,128]{2,1,0:T(8,128)(2,1)}, bf16[16,1024,128]{2,1,0:T(8,128...) custom-call(bf16[1024,1152]{1,0:T(8,128)(2,1)} %tokens.5, ...), custom_call_target="tpu_custom_call" | custom-call | tf_op jit(solution)/shard_map/attend/pallas_call | solution.py:547
  206.4 11.3 %project.1 = (f32[1024,1152]{1,0:T(8,128)}, bf16[1024,1152]{1,0:T(8,128)(2,1)}) custom-call(bf16[1024,1152]{1,0:T(8,128)(2,1)} %tokens.5, bf16[1024,2048]{1,0:T(8,128)(2,1)} %get-tuple-element.56.o, bf16[2048,1152]{1,0:T(8,128)(2,1)} %get-tuple-element.57.weight, f32[1,1152]{1,0:T(1,128)} %slice.132.bias, f32[1,1152]{1,0:T(1,128)} %slice.134.gain, ...), custom_call_target="tpu_custom_call" | custom-call | tf_op jit(solution)/shard_map/project/pallas_call | solution.py:719
  217.7 109.1 %mlp.1 = (f32[1024,1152]{1,0:T(8,128)}, f32[1024,1152]{1,0:T(8,128)}, f32[6,1,768]{2,1,0:T(1,128)}, bf16[4,2,1,2,2,144,1152]{6,5,4,3,2,1,0:T(8,128)(2,1)}, bf16[...) custom-call(bf16[1024,1152]{1,0:T(8,128)(2,1)} %get-tuple-element.59, ...), custom_call_target="tpu_custom_call" | custom-call | tf_op jit(solution)/shard_map/mlp/pallas_call | solution.py:904
  326.8 27.8 %turn.1 = (bf16[1024,1152]{1,0:T(8,128)(2,1)}, f32[1024,1152]{1,0:T(8,128)}, bf16[1024,2048]{1,0:T(8,128)(2,1)}, bf16[2048,1152]{1,0:T(8,128)(2,1)}, f32[4,1152]{1,0:T(4,128)}) custom-call(f32[1024,1152]{1,0:T(8,128)} %get-tuple-element.58.hidden, f32[1024,1152]{1,0:T(8,128)} %get-tuple-element.62.y, f32[1,1152]{1,0:T(1,128)} %slice.139.bias, ...), custom_call_target="tpu_custom_call" | custom-call | tf_op jit(solution)/shard_map/turn/pallas_call | solution.py:975
  354.6 108.4 %attend_back.1 = (bf16[1024,6144]{1,0:T(8,128)(2,1)}, bf16[16,384,1152]{2,1,0:T(8,128)(2,1)}, f32[16,8,128]{2,1,0:T(8,128)}, f32[16,8,128]{2,1,0:T(8,128)}, f32[...) custom-call(bf16[1024,1152]{1,0:T(8,128)(2,1)} %get-tuple-element.65.normed, ...), custom_call_target="tpu_custom_call" | custom-call | tf_op jit(solution)/shard_map/attend_back/pallas_call | solution.py:662
  463.4 1.5 pad_maximum_fusion.3.time_send
  464.9 1.9 maximum_bitcast_fusion
  466.8 1.9 pad_maximum_fusion
  468.7 1.2 fusion.31
  469.9 0.7 convolution_bitcast_fusion
  470.8 0.6 pad.43.vec_in
  471.4 88.6 %end.1 = (bf16[1024,1152]{1,0:T(8,128)(2,1)}, f32[16,1152]{1,0:T(8,128)}, f32[1152,128]{1,0:T(8,128)}, f32[144,1152]{1,0:T(8,128)}) custom-call(bf16[1024,1152]{1,0:T(8,128)(2,1)} %tokens.5, bf16[1024,6144]{1,0:T(8,128)(2,1)} %get-tuple-element.73.dqkv, bf16[6144,1152]{1,0:T(8,128)(2,1)} %bitcast.63, f32[1,1152]{1,0:T(1,128)} %slice.122.gain, ...), custom_call_target="tpu_custom_call" | custom-call | tf_op jit(solution)/shard_map/end/pallas_call | solution.py:1153
  560.0 2.2 copy.74
  562.2 0.8 slice.153
  563.0 0.6 dynamic-slice_bitcast_fusion
  563.6 0.9 slice.151
  564.5 0.8 slice.142
  565.4 0.5 slice_bitcast_fusion.5
  565.9 0.6 dynamic_slice.11
  566.6 1.6 slice.147
  568.2 1.9 slice_bitcast_fusion
  570.0 1.4 copy.93
  (54 shorter events, 3.4 us)
Async XLA Ops:
  0.6 18.4 %copy-start = (bf16[1024,1152]{1,0:T(8,128)(2,1)S(1)}, bf16[1024,1152]{1,0:T(8,128)(2,1)}, u32[]{:S(2)}) copy-start(bf16[1024,1152]{1,0:T(8,128)(2,1)} %param.37) | copy-start | bytes 7077892
  354.5 108.5 %copy-start.4 = (f32[6,1,768]{2,1,0:T(1,128)S(1)}, f32[6,1,768]{2,1,0:T(1,128)}, u32[]{:S(2)}) copy-start(f32[6,1,768]{2,1,0:T(1,128)} %get-tuple-element.78) | copy-start | bytes 55300
  354.6 110.3 %copy-start.3 = (f32[48,1152]{1,0:T(8,128)S(1)}, f32[48,1152]{1,0:T(8,128)}, u32[]{:S(2)}) copy-start(f32[48,1152]{1,0:T(8,128)} %get-tuple-element.86) | copy-start | bytes 663556
  354.6 112.2 %copy-start.2 = (f32[48,1152]{1,0:T(8,128)S(1)}, f32[48,1152]{1,0:T(8,128)}, u32[]{:S(2)}) copy-start(f32[48,1152]{1,0:T(8,128)} %get-tuple-element.88) | copy-start | bytes 663556
  463.0 7.7 %copy-start.5 = (f32[4,1152]{1,0:T(4,128)S(1)}, f32[4,1152]{1,0:T(4,128)}, u32[]{:S(2)}) copy-start(f32[4,1152]{1,0:T(4,128)} %get-tuple-element.77) | copy-start | bytes 55300
  560.0 10.0 %copy-start.1 = (bf16[1024,1152]{1,0:T(8,128)(2,1)S(1)}, bf16[1024,1152]{1,0:T(8,128)(2,1)}, u32[]{:S(2)}) copy-start(bf16[1024,1152]{1,0:T(8,128)(2,1)} %get-tuple-element.201) | copy-start | bytes 7077892

commit v4 on v3

--- a/solution.py
+++ b/solution.py
@@ -28,29 +28,24 @@
     14, 64, 23, 53, 24, 54,
 ),)
 ATTEND_ORDER = (
-    (0,), (30,), (), (), (10, 1), (31,), (2,), (11, 32, 20), (), (), (21,), (12, 33, 3), (22,), (), (),
-    (13, 23, 4), (14, 24, 34),
+    (20,), (), (0,), (21,), (10, 1, 22), (), (11, 30, 2), (), (), (31,), (12,), (3,), (4, 32), (23,), (13,),
+    (33,), (34, 24, 14),
 )
 MLP_ORDER = (
-    (10,), (), (11, 0), (12,), (1,), (2, 30, 13, 20), (31, 14, 3), (21, 4), (32,), (22, 33), (23,), (), (34, 24),
+    (0,), (), (), (), (1, 10), (2,), (), (11, 3), (12,), (30, 20), (13, 21), (4, 14, 31), (22,), (23, 32),
+    (33,), (), (34, 24),
 )
 BACK_ORDER = (
-    (0,), (30, 10, 20, 1), (), (11,), (2,), (21,), (), (12, 31, 3), (22,), (4,), (13,), (), (23, 32), (), (33, 14),
-    (), (34, 24),
-)
-END_ORDER = (
-    (0,), (), (20, 1), (10, 2), (21,), (30, 11, 22, 40), (12, 50, 31), (), (), (51, 32, 41, 23), (), (3,), (13, 42),
-    (), (24, 52, 33), (43, 4), (53, 34, 44, 14, 54),
-)
-BACK_ORDER = (
-    (0,), (1, 50), (51, 30), (31,), (), (2, 20), (21, 52, 10, 32), (3, 40), (41, 53), (), (22, 33, 54, 42), (11, 23),
-    (43,), (12, 34), (4, 24, 13), (44,), (14,),
+    (30, 10), (0,), (11,), (), (20,), (12,), (), (13, 31), (), (1,), (), (14,), (32,), (), (21, 33, 2), (), (),
+    (), (22, 3), (), (23, 34), (), (), (4, 24), (),
 )
 END_ORDER = (
     (20,), (0, 21, 10), (1, 50), (), (22, 11), (30, 2), (23,), (51, 3, 12),
     (52, 31, 40, 13, 60, 41, 53, 24, 4, 32, 61, 42, 33, 54, 43, 62, 63, 14, 34, 44, 64),
 )
 STAGES = 5
+PROJECTS = 4
+TURNS = 8
 
 
 def rounds_order(count, places, extra=False):
@@ -227,11 +222,10 @@
 
 class Scatter:
     def __init__(
-        self, dims, pieces, shift, sources, results, held, from_core, from_second, from_first, from_line, sems
+        self, dims, pieces, sources, put, held, from_core, from_second, from_first, from_line, sems
     ):
         self.at = Place(dims)
-        self.shift = shift
-        self.pieces, self.sources, self.results = pieces, sources, results
+        self.pieces, self.sources, self.put = pieces, sources, put
         self.held, self.from_core, self.from_second = held, from_core, from_second
         self.from_first, self.from_line, self.sems = from_first, from_line, sems
 
@@ -325,7 +319,7 @@
             for i in range(at.G1 * at.G2 - 1):
                 wait_for(from_line[i], self.sems.at[k, 5 + i, 1])
                 total = total + from_line[i][...].astype(F32)
-            self.results[array][pl.ds(start - self.shift, count)] = total
+            self.put(array, start, count, total)
             wait_for(from_core, self.sems.at[k, 0, 0])
             for kind in (1, 2):
                 wait_for(from_second[kind - 1], self.sems.at[k, kind, 0])
@@ -354,7 +348,7 @@
 
 def order_for(order, pieces, places, extra=False):
     count = len(pieces) + extra
-    if sum(len(place) for place in order) == count * STAGES:
+    if len(order) == places and sum(len(place) for place in order) == count * STAGES:
         return order
     return rounds_order(len(pieces), places, extra)
 
@@ -463,6 +457,34 @@
     )(mixed_shard, small_shard, time_weight)
 
 
+def store_rows(results):
+    def put(array, start, count, total):
+        results[array][pl.ds(start, count)] = total
+
+    return put
+
+
+def scatter(part, dims, collective):
+    shard = part.shape[5:]
+    pieces = cut(0, shard[0], ())
+    (order,) = rounds_order(len(pieces), 1)
+
+    def kernel(source, result, *buffers):
+        work = Scatter(dims, pieces, (source,), store_rows((result,)), *buffers)
+        work.at.barrier()
+        for event in order:
+            work.stage(*divmod(event, 10))
+
+    return pl.pallas_call(
+        kernel,
+        out_shape=jax.ShapeDtypeStruct(shard, F32),
+        in_specs=[pl.BlockSpec(memory_space=pl.ANY)],
+        out_specs=pl.BlockSpec(memory_space=pltpu.VMEM),
+        scratch_shapes=Scatter.scratch(dims, pieces, shard[1]),
+        compiler_params=params(collective_id=collective, has_side_effects=True),
+    )(part)
+
+
 def normalise(values):
     centre = values - jnp.mean(values, axis=-1, keepdims=True)
     inverse = lax.rsqrt(jnp.mean(centre * centre, axis=-1, keepdims=True) + 1e-06)
@@ -485,10 +507,11 @@
                 work.stage(*divmod(event, 10))
 
 
-def attend_kernel(factor, block, dims, pieces, order, tokens, gain, shift, weight, time_q, time_v, large, table, onehot,
+def attend_kernel(factor, block, dims, pieces, order, tokens, vectors, weight, time_q, time_v, large, table, onehot,
                   mask_q, mask_k, up_shard, down_shard,
                   normed_out, q_out, k_out, v_out, o_out, p_out, up_out, down_out, keys, sems, own_sems):
     rows = tokens.shape[0]
+    gain, shift = vectors.at[0:1], vectors.at[1:2]
     work = Gather(dims, pieces, (up_shard, down_shard), (up_out, down_out), sems, own_sems)
     step = pl.program_id(0)
 
@@ -537,9 +560,9 @@
             work.stage(*divmod(event, 10))
 
 
-def attend(tokens, gain, shift, weight, times, large, table, onehot, mask_q, mask_k, factor, shards, dims):
+def attend(tokens, vectors, weight, times, large, table, onehot, mask_q, mask_k, factor, shards, dims):
     rows, width = tokens.shape
-    block = min(256, rows)
+    block = min(512, rows)
     pieces = pieces_of(0, early_rows(shards[0].shape[0]))
     anywhere = pl.BlockSpec(memory_space=pl.ANY)
     per_head = lambda *shape: pl.BlockSpec((1,) + shape, lambda h: (h, 0, 0))
@@ -549,8 +572,7 @@
         grid=(HEADS,),
         in_specs=[
             resident(tokens.shape),
-            resident(gain.shape),
-            resident(shift.shape),
+            resident(vectors.shape),
             per_head(3 * LANES, width),
             pl.BlockSpec((1, 8, LANES), lambda h: (h, 0, 0)),
             pl.BlockSpec((1, 8, LANES), lambda h: (HEADS + h, 0, 0)),
@@ -584,147 +606,196 @@
         scratch_shapes=[pltpu.VMEM((rows, 2 * LANES), BF16), *Gather.scratch(dims, pieces)],
         compiler_params=params(collective_id=2, has_side_effects=True),
         name="attend",
-    )(tokens, gain, shift, weight, times, times, large, table, onehot, mask_q, mask_k, *shards)
-
-
-def attend_back_kernel(block, scale, dims, pieces, shift, order, normed, p, q, k, v, do, o, onehot, large, d_up, d_down,
-                       dqkv_out, dw_out, sums_q, sums_v, pair_out, up_out, down_out,
-                       keys, grads, dk_sum, dv_sum, *buffers):
+    )(tokens, vectors, weight, times, times, large, table, onehot, mask_q, mask_k, *shards)
+
+
+def turn_rows(hidden, y, dn, cotangent, mask, vectors, weight, span, out, dh_out, vec_out, da_all, do_all):
+    out[...] = (hidden[...] + (y[...] + vectors[5:6])).astype(BF16)
+    back, unit = norm_back(hidden[...], vectors[3:4], dn[...])
+    dyf = only_valid(cotangent, mask).astype(F32)
+    dh = dyf + back
+    dh_out[...] = dh
+    da = dh.astype(BF16)
+    da_all[span] = da
+    do = dot_nt(da, weight[...]).astype(BF16)
+    for head in range(HEADS):
+        do_all[head, span] = do[:, head * LANES : (head + 1) * LANES]
+    vec_out[0:1] += jnp.sum(dn[...] * unit, axis=0, keepdims=True)
+    vec_out[1:2] += jnp.sum(dn[...], axis=0, keepdims=True)
+    vec_out[2:3] += jnp.sum(da.astype(F32), axis=0, keepdims=True)
+    vec_out[3:4] += jnp.sum(dyf, axis=0, keepdims=True)
+
+
+def attend_back_kernel(block, turns, scale, dims, pieces, ready, order, hidden, y, dn, cotangent, mask, vectors, weight,
+                       normed, p, q, k, v, o, onehot, onehot_t, large, *refs):
+    refs = list(refs)
+    take = lambda count: [refs.pop(0) for _ in range(count)]
+    parts = take(2 if pieces else 0)
+    ready = take(ready)
+    out, dh_out, vec_out, dqkv_out, dw_out, dwo_out, sums_out, pair_out = take(8)
+    results = take(2 if pieces else 0)
+    da_all, do_all, keys, grads, offsets, dk_sum, dv_sum = take(7)
+
+    def put(array, start, count, total):
+        if array == 0:
+            results[0][:, start : start + count] = total.T
+        else:
+            results[1][start : start + count] = total
+
+    work = Scatter(dims, pieces, parts, put, *refs) if pieces else None
     rows = normed.shape[0]
-    work = Scatter(dims, pieces, shift, (d_up, d_down), (up_out, down_out), *buffers)
     step = pl.program_id(0)
 
     @pl.when(step == 0)
     def _():
-        work.at.barrier()
-
-    for place in range(HEADS):
+        if pieces:
+            work.at.barrier()
+        vec_out[...] = jnp.zeros_like(vec_out)
+        for array, part in enumerate(ready):
+            put(array, 0, part.shape[0], part[...])
+
+    for place in range(len(order) - 1):
         events(order, step, work, place)
-    lane = lax.broadcasted_iota(jnp.int32, (rows, LANES), 1)
-    head = 72
-    delta = jnp.sum(do[...].astype(F32) * o[...].astype(F32), axis=1, keepdims=True)
-    high = delta.astype(BF16).astype(F32)
-    more = jnp.where(lane == head, -high, jnp.where(lane == head + 1, high - delta, 0.0))
-    grads[...] = (do[...].astype(F32) + more).astype(BF16)
-    values = v[0] + jnp.where((lane == head) | (lane == head + 1), 1.0, 0.0).astype(BF16)
-    keys[:, :LANES] = k[0]
-    keys[:, LANES:] = onehot[...]
-    pair = jnp.zeros((LANES, LANES), F32)
-    for start in range(0, rows, block):
-        span = pl.ds(start, block)
-        centred = dot_nt(grads[span], values)
-        ds = (p[0, span].astype(F32) * centred).astype(BF16)
-        both = dot_nn(ds, keys[...])
-        dqkv_out[span, :LANES] = (both[:, :LANES] * scale).astype(BF16)
-        pair = pair + lax.dot_general(
-            onehot[span].astype(F32), both[:, LANES:], (((0,), (0,)), ((), ())),
-            preferred_element_type=F32, precision=HIGHEST,
-        )
-        dk = dot_tn(ds, q[0, span])
-        dv = dot_tn(p[0, span], do[span])
-        if start == 0:
-            dk_sum[...] = dk
-            dv_sum[...] = dv
-        else:
-            dk_sum[...] += dk
-            dv_sum[...] += dv
-    dqkv_out[:, LANES : 2 * LANES] = (dk_sum[...] * scale).astype(BF16)
-    dqkv_out[:, 2 * LANES :] = dv_sum[...].astype(BF16)
-    pair_out[0] = pair
-    slot = SMALL * SMALL
-    one = large[...] > 0.0
-    for target, base in ((sums_q, 0), (sums_v, 2 * LANES)):
-        sums = []
-        for start in range(0, rows, slot):
-            part = dqkv_out[pl.ds(start, slot), base : base + LANES]
-            sums.append(jnp.sum(part.astype(F32), axis=0, keepdims=True))
-        total = functools.reduce(jnp.add, sums)
-        sums = [jnp.where(one, total if i == 0 else jnp.zeros_like(total), part) for i, part in enumerate(sums)]
-        sums.append(jnp.zeros((8 - len(sums), LANES), F32))
-        target[0] = jnp.concatenate(sums, axis=0)
-    dw_out[0] = dot_tn(dqkv_out[...], normed[...]).astype(BF16)
-
-    @pl.when(step == HEADS - 1)
+
+    @pl.when(step < turns)
     def _():
-        for event in order[HEADS]:
-            work.stage(*divmod(event, 10))
-
-
-def attend_back(normed, p, q, k, v, do, o, onehot, large, scale, parts, dims):
+        some = hidden.shape[0]
+        span = pl.ds(pl.multiple_of(step * some, some), some)
+        turn_rows(hidden, y, dn, cotangent, mask, vectors, weight, span, out, dh_out, vec_out, da_all, do_all)
+
+    @pl.when(step >= turns)
+    def _():
+        do = do_all.at[step - turns]
+        lane = lax.broadcasted_iota(jnp.int32, (rows, LANES), 1)
+        head = 72
+        delta = jnp.sum(do[...].astype(F32) * o[...].astype(F32), axis=1, keepdims=True)
+        high = delta.astype(BF16).astype(F32)
+        more = jnp.where(lane == head, -high, jnp.where(lane == head + 1, high - delta, 0.0))
+        grads[...] = (do[...].astype(F32) + more).astype(BF16)
+        values = v[0] + jnp.where((lane == head) | (lane == head + 1), 1.0, 0.0).astype(BF16)
+        keys[:, :LANES] = k[0]
+        keys[:, LANES:] = onehot[...]
+        for start in range(0, rows, block):
+            span = pl.ds(start, block)
+            centred = dot_nt(grads[span], values)
+            ds = (p[0, span].astype(F32) * centred).astype(BF16)
+            both = dot_nn(ds, keys[...])
+            dqkv_out[span, :LANES] = (both[:, :LANES] * scale).astype(BF16)
+            by_place = both[:, LANES:]
+            upper = by_place.astype(BF16)
+            offsets[span, :LANES] = upper
+            offsets[span, LANES:] = (by_place - upper.astype(F32)).astype(BF16)
+            dk = dot_tn(q[0, span], ds)
+            dv = dot_tn(do[span], p[0, span])
+            if start == 0:
+                dk_sum[...] = dk
+                dv_sum[...] = dv
+            else:
+                dk_sum[...] += dk
+                dv_sum[...] += dv
+        dqkv_out[:, LANES : 2 * LANES] = (dk_sum[...] * scale).T.astype(BF16)
+        dqkv_out[:, 2 * LANES :] = dv_sum[...].T.astype(BF16)
+        pair = dot_nn(onehot_t[...], offsets[...])
+        pair_out[0] = pair[:, :LANES] + pair[:, LANES:]
+        slot = SMALL * SMALL
+        one = large[...] > 0.0
+        for kind, base in enumerate((0, 2 * LANES)):
+            sums = []
+            for start in range(0, rows, slot):
+                part = dqkv_out[pl.ds(start, slot), base : base + LANES]
+                sums.append(jnp.sum(part.astype(F32), axis=0, keepdims=True))
+            total = functools.reduce(jnp.add, sums)
+            sums = [jnp.where(one, total if i == 0 else jnp.zeros_like(total), part) for i, part in enumerate(sums)]
+            sums.append(jnp.zeros((8 - len(sums), LANES), F32))
+            sums_out[kind, 0] = jnp.concatenate(sums, axis=0)
+        dw_out[0] = dot_tn(dqkv_out[...], normed[...]).astype(BF16)
+        dwo_out[...] = dot_tn(o[...], da_all[...]).astype(BF16)
+
+    if pieces:
+
+        @pl.when(step == pl.num_programs(0) - 1)
+        def _():
+            for event in order[-1]:
+                work.stage(*divmod(event, 10))
+
+
+def attend_back(
+    hidden, y, dn, cotangent, mask, vectors, weight, normed, p, q, k, v, o, onehot, onehot_t, large, scale, parts, ready, dims
+):
     rows, width = normed.shape
-    block = min(256, rows)
-    shift = summed_rows(parts[0].shape[5])
-    pieces = pieces_of(shift, parts[0].shape[5])
-    sum_shape = (parts[0].shape[5] - shift, width)
+    block = min(512, rows)
+    turns = TURNS
+    some = rows // turns
+    pieces, sum_shapes = [], []
+    if parts:
+        shard_rows = parts[0].shape[5]
+        pieces = pieces_of(summed_rows(shard_rows), shard_rows)
+        sum_shapes = [(width, shard_rows), (shard_rows, width)]
     anywhere = pl.BlockSpec(memory_space=pl.ANY)
-    per_head = lambda *shape: pl.BlockSpec((1,) + shape, lambda h: (h, 0, 0))
-    head_cols = pl.BlockSpec((rows, LANES), lambda h: (0, h))
+    head_of = lambda s: jnp.maximum(s - turns, 0)
+    per_head = lambda *shape: pl.BlockSpec((1,) + shape, lambda s: (head_of(s), 0, 0))
+    by_rows = pl.BlockSpec((some, width), lambda s: (jnp.minimum(s, turns - 1), 0))
     return pl.pallas_call(
         functools.partial(
-            attend_back_kernel, block, scale, dims, pieces, shift, order_for(BACK_ORDER, pieces, HEADS + 1)
+            attend_back_kernel, block, turns, scale, dims, pieces, len(ready),
+            order_for(BACK_ORDER, pieces, turns + HEADS + 1),
         ),
-        grid=(HEADS,),
+        grid=(turns + HEADS,),
         in_specs=[
+            by_rows,
+            by_rows,
+            by_rows,
+            by_rows,
+            pl.BlockSpec((some, LANES), lambda s: (jnp.minimum(s, turns - 1), 0)),
+            resident(vectors.shape),
+            resident(weight.shape),
             resident(normed.shape),
             per_head(rows, rows),
             per_head(rows, LANES),
             per_head(rows, LANES),
             per_head(rows, LANES),
-            head_cols,
-            head_cols,
+            pl.BlockSpec((rows, LANES), lambda s: (0, head_of(s))),
             resident(onehot.shape),
+            resident(onehot_t.shape),
             resident(large.shape),
-            anywhere,
-            anywhere,
+            *[anywhere for _ in parts],
+            *[resident(part.shape) for part in ready],
         ],
         out_specs=[
-            pl.BlockSpec((rows, 3 * LANES), lambda h: (0, h)),
+            by_rows,
+            by_rows,
+            resident((4, width)),
+            pl.BlockSpec((rows, 3 * LANES), lambda s: (0, head_of(s))),
             per_head(3 * LANES, width),
-            per_head(8, LANES),
-            per_head(8, LANES),
-            per_head(LANES, LANES),
-            *[resident(sum_shape) for _ in parts],
+            pl.BlockSpec((LANES, width), lambda s: (head_of(s), 0)),
+            pl.BlockSpec((2, 1, 8, LANES), lambda s: (0, head_of(s), 0, 0)),
+            per_head(onehot_t.shape[0], LANES),
+            *[resident(shape) for shape in sum_shapes],
         ],
         out_shape=[
+            jax.ShapeDtypeStruct(hidden.shape, BF16),
+            jax.ShapeDtypeStruct(hidden.shape, F32),
+            jax.ShapeDtypeStruct((4, width), F32),
             jax.ShapeDtypeStruct((rows, HEADS * 3 * LANES), BF16),
             jax.ShapeDtypeStruct((HEADS, 3 * LANES, width), BF16),
-            jax.ShapeDtypeStruct((HEADS, 8, LANES), F32),
-            jax.ShapeDtypeStruct((HEADS, 8, LANES), F32),
-            jax.ShapeDtypeStruct((HEADS, LANES, LANES), F32),
-            *[jax.ShapeDtypeStruct(sum_shape, F32) for _ in parts],
+            jax.ShapeDtypeStruct((HEADS * LANES, width), BF16),
+            jax.ShapeDtypeStruct((2, HEADS, 8, LANES), F32),
+            jax.ShapeDtypeStruct((HEADS, onehot_t.shape[0], LANES), F32),
+            *[jax.ShapeDtypeStruct(shape, F32) for shape in sum_shapes],
         ],
         scratch_shapes=[
+            pltpu.VMEM((rows, width), BF16),
+            pltpu.VMEM((HEADS, rows, LANES), BF16),
             pltpu.VMEM((rows, 2 * LANES), BF16),
             pltpu.VMEM((rows, LANES), BF16),
-            pltpu.VMEM((rows, LANES), F32),
-            pltpu.VMEM((rows, LANES), F32),
-            *Scatter.scratch(dims, pieces, width),
-        ],
-        compiler_params=params(collective_id=3, has_side_effects=True),
+            pltpu.VMEM((rows, 2 * LANES), BF16),
+            pltpu.VMEM((LANES, rows), F32),
+            pltpu.VMEM((LANES, rows), F32),
+            *(Scatter.scratch(dims, pieces, width) if pieces else []),
+        ],
+        compiler_params=params(collective_id=3, has_side_effects=True) if pieces else params(),
         name="attend_back",
-    )(normed, p, q, k, v, do, o, onehot, large, *parts)
-
-
-def project_kernel(tokens, o, weight, bias, gain, shift, hidden_out, normed_out):
-    hidden = tokens[...].astype(F32) + (dot_nn(o[...], weight[...]) + bias[...])
-    hidden_out[...] = hidden
-    unit, _ = normalise(hidden)
-    normed_out[...] = (unit * gain[...] + shift[...]).astype(BF16)
-
-
-def project(tokens, o, weight, bias, gain, shift):
-    rows, width = tokens.shape
-    block = min(256, rows)
-    by_rows = lambda cols: pl.BlockSpec((block, cols), lambda i: (i, 0))
-    return pl.pallas_call(
-        project_kernel,
-        grid=(rows // block,),
-        in_specs=[by_rows(width), by_rows(o.shape[1]), resident(weight.shape)] + [resident((1, width))] * 3,
-        out_specs=[by_rows(width), by_rows(width)],
-        out_shape=[jax.ShapeDtypeStruct(tokens.shape, F32), jax.ShapeDtypeStruct(tokens.shape, BF16)],
-        compiler_params=params(),
-        name="project",
-    )(tokens, o, weight, bias, gain, shift)
+    )(hidden, y, dn, cotangent, mask, vectors, weight, normed, p, q, k, v, o, onehot, onehot_t, large, *parts, *ready)
 
 
 def normal_parts(u):
@@ -750,25 +821,31 @@
     return ref.at[(i, *whole, rows)]
 
 
-def mlp_kernel(dims, block, blocks, gathers, sums, order, *refs):
+def only_valid(cotangent, mask):
+    lane = 72 + GRID * GRID // (SMALL * SMALL)
+    return jnp.where(mask[:, lane : lane + 1].astype(F32) > 0.5, 0.0, cotangent[...].astype(F32)).astype(BF16)
+
+
+def mlp_kernel(dims, block, projects, blocks, gathers, sums, order, *refs):
     refs = list(refs)
     take = lambda count: [refs.pop(0) for _ in range(count)]
-    normed, dy, bias, *early = take(5)
+    tokens, o, out_weight, vectors, cotangent, mask, bias, *early = take(9)
+    out_bias, gain, offset = (vectors.at[i : i + 1] for i in (2, 3, 4))
     shards = take(2) if gathers else None
-    y_out, dn_out, dbias_out, *grads_out = take(5)
+    hidden_out, y_out, dn_out, dbias_out, *grads_out = take(6)
     late = take(2) if gathers else None
     totals = take(2) if sums else None
-    weights, grads, act_all, du_all, weight_sems, grad_sems = take(6)
+    normed, dy, weights, grads, act_all, du_all, weight_sems, grad_sems = take(8)
     if gathers:
         first_late = early[0].shape[-2] - PIECE
         shards = [shard.at[pl.ds(first_late, PIECE)] for shard in shards]
         gather = Gather(dims, gathers, shards, late, *take(2))
     if sums:
-        scatter = Scatter(dims, sums, 0, grads_out, totals, *refs)
+        scatter = Scatter(dims, sums, grads_out, store_rows(totals), *refs)
     rows = normed.shape[0]
     units = act_all.shape[1]
-    step = pl.program_id(0)
-    steps = pl.num_programs(0)
+    step = pl.program_id(0) - projects
+    steps = pl.num_programs(0) - projects
     late_step = steps - blocks if gathers else steps
 
     def copies(target_step, source):
@@ -811,7 +888,68 @@
                     else:
                         scatter.stage(k - len(gathers), number)
 
-    @pl.when(step == 0)
+    def mlp_step():
+        for place in range(projects, len(order) - 1, 2):
+            happen(place, (place - projects) // 2)
+        for copy in copies(step, early):
+            copy.wait()
+
+        @pl.when(step + 1 < late_step)
+        def _():
+            for copy in copies(step + 1, early):
+                copy.start()
+
+        if gathers:
+
+            @pl.when((step + 1 > late_step) & (step + 1 < steps))
+            def _():
+                for copy in late_copies(step + 1):
+                    copy.start()
+
+        slot = step % 2
+        up = weights[slot, 0].reshape(units, -1)
+        down = weights[slot, 1].reshape(units, -1)
+        total = jnp.zeros((1, units), F32)
+        for start in range(0, rows, block):
+            span = pl.ds(start, block)
+            if start == rows // 2:
+
+                @pl.when(step >= 1)
+                def _():
+                    for copy in write_copies(step - 1):
+                        copy.wait()
+
+                for place in range(projects + 1, len(order) - 1, 2):
+                    happen(place, (place - projects) // 2)
+                if gathers:
+
+                    @pl.when(step + 1 == late_step)
+                    def _():
+                        for copy in late_copies(step + 1):
+                            copy.start()
+
+            u = dot_nt(normed[span], up) + bias[0]
+            phi, density = normal_parts(u)
+            act = (u * phi).astype(BF16)
+            slope = phi + u * density
+            du = (slope * dot_nt(dy[span], down)).astype(BF16)
+            total = total + jnp.sum(du.astype(F32), axis=0, keepdims=True)
+            act_all[span] = act
+            du_all[span] = du
+            y_out[span] += dot_nn(act, down)
+            dn_out[span] += dot_nn(du, up)
+        dbias_out[0] = total
+        grads[slot, 0] = dot_tn(du_all[...], normed[...]).astype(BF16).reshape(grads.shape[2:])
+        grads[slot, 1] = dot_tn(act_all[...], dy[...]).astype(BF16).reshape(grads.shape[2:])
+        for copy in write_copies(step):
+            copy.start()
+
+        @pl.when(step == steps - 1)
+        def _():
+            for copy in write_copies(step):
+                copy.wait()
+
+    @pl.when(step == -projects)
     def _():
         if gathers:
             gather.at.barrier()
@@ -820,71 +958,28 @@
         y_out[...] = jnp.zeros_like(y_out)
         dn_out[...] = jnp.zeros_like(dn_out)
 
-    for place in range(0, len(order) - 1, 2):
-        happen(place, place // 2)
-    for copy in copies(step, early):
-        copy.wait()
-
-    @pl.when(step + 1 < late_step)
+    for place in range(projects):
+        happen(place, place - projects)
+
+    @pl.when(step < 0)
     def _():
-        for copy in copies(step + 1, early):
-            copy.start()
-
-    if gathers:
-
-        @pl.when((step + 1 > late_step) & (step + 1 < steps))
-        def _():
-            for copy in late_copies(step + 1):
-                copy.start()
-
-    slot = step % 2
-    up = weights[slot, 0].reshape(units, -1)
-    down = weights[slot, 1].reshape(units, -1)
-    total = jnp.zeros((1, units), F32)
-    for start in range(0, rows, block):
-        span = pl.ds(start, block)
-        if start == rows // 2:
-
-            @pl.when(step >= 1)
-            def _():
-                for copy in write_copies(step - 1):
-                    copy.wait()
-
-            for place in range(1, len(order) - 1, 2):
-                happen(place, place // 2)
-            if gathers:
-
-                @pl.when(step + 1 == late_step)
-                def _():
-                    for copy in late_copies(step + 1):
-                        copy.start()
-
-        u = dot_nt(normed[span], up) + bias[0]
-        phi, density = normal_parts(u)
-        act = (u * phi).astype(BF16)
-        slope = phi + u * density
-        du = (slope * dot_nt(dy[span], down)).astype(BF16)
-        total = total + jnp.sum(du.astype(F32), axis=0, keepdims=True)
-        act_all[span] = act
-        du_all[span] = du
-        y_out[span] += dot_nn(act, down)
-        dn_out[span] += dot_nn(du, up)
-    dbias_out[0] = total
-    grads[slot, 0] = dot_tn(du_all[...], normed[...]).astype(BF16).reshape(grads.shape[2:])
-    grads[slot, 1] = dot_tn(act_all[...], dy[...]).astype(BF16).reshape(grads.shape[2:])
-    for copy in write_copies(step):
-        copy.start()
-
-    @pl.when(step == steps - 1)
+        some = tokens.shape[0]
+        span = pl.ds(pl.multiple_of(pl.program_id(0) * some, some), some)
+        hidden = tokens[...].astype(F32) + (dot_nn(o[...], out_weight[...]) + out_bias[...])
+        hidden_out[...] = hidden
+        unit, _ = normalise(hidden)
+        normed[span] = (unit * gain[...] + offset[...]).astype(BF16)
+        dy[span] = only_valid(cotangent, mask)
+
+    @pl.when(step >= 0)
     def _():
-        for copy in write_copies(step):
-            copy.wait()
+        mlp_step()
 
     happen(len(order) - 1, steps - 1)
 
 
-def mlp(normed, dy, bias, weights, shards, dims):
-    rows, width = normed.shape
+def mlp(tokens, o, out_weight, vectors, cotangent, mask, bias, weights, shards, dims):
+    rows, width = tokens.shape
     shard_rows = shards[0].shape[0]
     devices = dims[0] * dims[1] * 8
     blocks = devices // BLOCK_DEVICES
@@ -894,28 +989,36 @@
     gathers = pieces_of(0, PIECE) if overlap else []
     sums = pieces_of(0, PIECE) if overlap else []
     anywhere = pl.BlockSpec(memory_space=pl.ANY)
-    by_step = pl.BlockSpec((1, 1, units), lambda i: (i, 0, 0))
+    projects = PROJECTS
+    some = rows // projects
+    by_step = pl.BlockSpec((1, 1, units), lambda i: (jnp.maximum(i - projects, 0), 0, 0))
+    by_rows = lambda cols: pl.BlockSpec((some, cols), lambda i: (jnp.minimum(i, projects - 1), 0))
     spread = spread_of(dims)
     if dims[1] > 1:
         weights = [weight.reshape((blocks,) + BLOCK + (shard_rows, width)) for weight in weights]
     landing = jax.ShapeDtypeStruct(spread + (PIECE, width), BF16)
     total = jax.ShapeDtypeStruct((PIECE, width), F32)
-    order = order_for(MLP_ORDER, gathers + sums, 2 * steps + 1)
-    y, dn, dbias, d_up, d_down, *rest = pl.pallas_call(
-        functools.partial(mlp_kernel, dims, min(256, rows), blocks, gathers, sums, order),
-        grid=(steps,),
-        in_specs=[resident(normed.shape), resident(dy.shape), by_step, anywhere, anywhere]
+    full = jax.ShapeDtypeStruct(tokens.shape, F32)
+    order = order_for(MLP_ORDER, gathers + sums, projects + 2 * steps + 1)
+    hidden, y, dn, dbias, d_up, d_down, *rest = pl.pallas_call(
+        functools.partial(mlp_kernel, dims, min(256, rows), projects, blocks, gathers, sums, order),
+        grid=(projects + steps,),
+        in_specs=[by_rows(width), by_rows(o.shape[1]), resident(out_weight.shape)]
+        + [resident(vectors.shape), by_rows(width), by_rows(LANES), by_step, anywhere, anywhere]
         + [anywhere, anywhere] * overlap,
-        out_specs=[resident(normed.shape), resident(normed.shape), by_step, anywhere, anywhere]
+        out_specs=[by_rows(width), resident(tokens.shape), resident(tokens.shape), by_step, anywhere, anywhere]
         + ([anywhere] * 2 + [resident((PIECE, width))] * 2) * overlap,
         out_shape=[
-            jax.ShapeDtypeStruct(normed.shape, F32),
-            jax.ShapeDtypeStruct(normed.shape, F32),
+            full,
+            full,
+            full,
             jax.ShapeDtypeStruct(bias.shape, F32),
             *[jax.ShapeDtypeStruct(weight.shape, BF16) for weight in weights],
             *([landing] * 2 + [total] * 2) * overlap,
         ],
         scratch_shapes=[
+            pltpu.VMEM((rows, width), BF16),
+            pltpu.VMEM((rows, width), BF16),
             pltpu.VMEM((2, 2) + BLOCK + (PIECE, width), BF16),
             pltpu.VMEM((2, 2) + BLOCK + (PIECE, width), BF16),
             pltpu.VMEM((rows, units), BF16),
@@ -926,77 +1029,9 @@
         ],
         compiler_params=params(collective_id=5, has_side_effects=True) if overlap else params(),
         name="mlp",
-    )(normed, dy, bias, *weights, *(shards if overlap else []))
+    )(tokens, o, out_weight, vectors, cotangent, mask, bias, *weights, *(shards if overlap else []))
     whole = spread + (shard_rows, width)
-    return y, dn, dbias, d_up.reshape(whole), d_down.reshape(whole), rest[2:]
-
-
-def turn_kernel(hidden, y, bias, dn, dy, gain, weight, o, out, dh_out, do_out, dw_out, vec_out, dw_sum):
-    first = pl.program_id(0) == 0
-    last = pl.program_id(0) == pl.num_programs(0) - 1
-    out[...] = (hidden[...] + (y[...] + bias[...])).astype(BF16)
-    back, unit = norm_back(hidden[...], gain[...], dn[...])
-    dyf = dy[...].astype(F32)
-    dh = dyf + back
-    dh_out[...] = dh
-    da = dh.astype(BF16)
-    do_out[...] = dot_nt(da, weight[...]).astype(BF16)
-    dw = dot_tn(o[...], da)
-    sums = jnp.concatenate(
-        [
-            jnp.sum(dn[...] * unit, axis=0, keepdims=True),
-            jnp.sum(dn[...], axis=0, keepdims=True),
-            jnp.sum(da.astype(F32), axis=0, keepdims=True),
-            jnp.sum(dyf, axis=0, keepdims=True),
-        ],
-        axis=0,
-    )
-
-    @pl.when(first)
-    def _():
-        dw_sum[...] = dw
-        vec_out[...] = sums
-
-    @pl.when(jnp.logical_not(first))
-    def _():
-        dw_sum[...] += dw
-        vec_out[...] += sums
-
-    @pl.when(last)
-    def _():
-        dw_out[...] = dw_sum[...].astype(BF16)
-
-
-def turn(hidden, y, bias, dn, dy, gain, weight, o):
-    rows, width = hidden.shape
-    block = min(256, rows)
-    by_rows = lambda cols: pl.BlockSpec((block, cols), lambda i: (i, 0))
-    wide = weight.shape[0]
-    return pl.pallas_call(
-        turn_kernel,
-        grid=(rows // block,),
-        in_specs=[
-            by_rows(width),
-            by_rows(width),
-            resident((1, width)),
-            by_rows(width),
-            by_rows(width),
-            resident((1, width)),
-            resident(weight.shape),
-            by_rows(wide),
-        ],
-        out_specs=[by_rows(width), by_rows(width), by_rows(wide), resident(weight.shape), resident((4, width))],
-        out_shape=[
-            jax.ShapeDtypeStruct(hidden.shape, BF16),
-            jax.ShapeDtypeStruct(hidden.shape, F32),
-            jax.ShapeDtypeStruct((rows, wide), BF16),
-            jax.ShapeDtypeStruct(weight.shape, BF16),
-            jax.ShapeDtypeStruct((4, width), F32),
-        ],
-        scratch_shapes=[pltpu.VMEM(weight.shape, F32)],
-        compiler_params=params(),
-        name="turn",
-    )(hidden, y, bias, dn, dy, gain, weight, o)
+    return hidden, y, dn, dbias, d_up.reshape(whole), d_down.reshape(whole), rest[2:]
 
 
 class SumAll:
@@ -1060,12 +1095,21 @@
             self.total[...] = total
 
 
-def end_kernel(dims, pieces, order, shares, head_dim, tokens, dqkv, weight, gain, dh, small, time_send, vec_in, dw, dw_out,
-               out, vec_out, time_out, mixed_out, mixed, dw_buffer, dw_sems, time_got, time_sems,
+def end_kernel(dims, pieces, order, shares, head_dim, tokens, dqkv, weight, vectors, dh, small, time_send, vec_in, dw, dw_out,
+               out, vec_out, time_out, qkv_out, out_out, mixed, dw_buffer, dw_sems, time_got, time_sems,
                vec_total, vec_send, vec_got, vec_sems, *buffers):
     step = pl.program_id(0)
     steps = pl.num_programs(0)
-    work = Scatter(dims, pieces, 0, (mixed,), (mixed_out,), *buffers)
+
+    def put_sum(array, start, count, total):
+        stop, cut_at = start + count, shares[0]
+        if start < cut_at:
+            qkv_out[:, start : min(stop, cut_at)] = total[: min(stop, cut_at) - start].T
+        first, last = max(start, cut_at), min(stop, sum(shares))
+        if first < last:
+            out_out[first - cut_at : last - cut_at] = total[first - start : last - start]
+
+    work = Scatter(dims, pieces, (mixed,), put_sum, *buffers)
     at = work.at
     sums = SumAll(at, vec_total, vec_send, vec_got, vec_sems)
     width = tokens.shape[1]
@@ -1119,7 +1163,7 @@
         events(order, step, work, place)
 
     dn = dot_nn(dqkv[...], weight[...])
-    back, unit = norm_back(tokens[...].astype(F32), gain[...], dn)
+    back, unit = norm_back(tokens[...].astype(F32), vectors[0:1], dn)
     out[...] = (dh[...] + back).astype(BF16)
     vec_total[0:1] += jnp.sum(dn * unit, axis=0, keepdims=True)
     vec_total[1:2] += jnp.sum(dn, axis=0, keepdims=True)
@@ -1141,7 +1185,7 @@
         time_out[...] = dot_tn(small[...], high) + dot_tn(small[...], low)
 
 
-def end(tokens, dqkv, weight, gain, dh, small, time_send, vec_in, dw, dw_out, dims, shares, head_dim):
+def end(tokens, dqkv, weight, vectors, dh, small, time_send, vec_in, dw, dw_out, dims, shares, head_dim):
     rows, width = tokens.shape
     block = rows // 8
     by_rows = lambda cols: pl.BlockSpec((block, cols), lambda i: (i, 0))
@@ -1157,7 +1201,7 @@
             by_rows(width),
             by_rows(dqkv.shape[1]),
             resident(weight.shape),
-            resident((1, width)),
+            resident(vectors.shape),
             by_rows(width),
             resident(small.shape),
             resident(time_send.shape),
@@ -1169,13 +1213,15 @@
             by_rows(width),
             resident(vec_in.shape),
             resident((width, LANES)),
-            resident((shard_rows, width)),
+            resident((width, shares[0])),
+            resident((shares[1], width)),
         ],
         out_shape=[
             jax.ShapeDtypeStruct(tokens.shape, BF16),
             jax.ShapeDtypeStruct(vec_in.shape, F32),
             jax.ShapeDtypeStruct((width, LANES), F32),
-            jax.ShapeDtypeStruct((shard_rows, width), F32),
+            jax.ShapeDtypeStruct((width, shares[0]), F32),
+            jax.ShapeDtypeStruct((shares[1], width), F32),
         ],
         scratch_shapes=[
             pltpu.VMEM(spread_of(dims) + (shard_rows, width), BF16),
@@ -1188,7 +1234,7 @@
         ],
         compiler_params=params(collective_id=4, has_side_effects=True),
         name="end",
-    )(tokens, dqkv, weight, gain, dh, small, time_send, vec_in, dw, dw_out)
+    )(tokens, dqkv, weight, vectors, dh, small, time_send, vec_in, dw, dw_out)
 
 
 def time_embed(stamps, feat_width):
@@ -1233,27 +1279,27 @@
     units = devices * unit_share
     mixed_shard = pad_rows(jnp.concatenate([qkv_weight.T, out_weight], axis=0))
     embedded = time_embed(timesteps, width).astype(BF16)
-    vectors = jnp.concatenate([norm1_gain, norm1_bias, out_bias, norm2_gain, norm2_bias, fc2_bias, fc1_bias])
-    table_size = row_table.size
-    to_row = lambda flat: jnp.pad(flat, (0, width - flat.shape[0]))[None]
-    both_tables = jnp.concatenate([row_table.reshape(-1), col_table.reshape(-1)])
-    small_shard = jnp.concatenate([embedded, to_row(vectors), to_row(both_tables)], axis=0)
-    small_shard = jnp.pad(small_shard, ((0, -small_shard.shape[0] % 16), (0, 0)))
+    vectors = (norm1_gain, norm1_bias, out_bias, norm2_gain, norm2_bias, fc2_bias, fc1_bias)
+    table_rows, table_width = row_table.shape
+    small_rows, table_at = 16, 8
+    put_at = lambda part, row, lane: jnp.pad(
+        part, ((row, small_rows - row - part.shape[0]), (lane, width - lane - part.shape[1]))
+    )
+    spots_of = [put_at(embedded, 0, 0), put_at(row_table, table_at, 2 * LANES), put_at(col_table, table_at, 3 * LANES)]
+    spots_of += [put_at(vector[None], per + i, 0) for i, vector in enumerate(vectors)]
+    small_shard = functools.reduce(jnp.add, spots_of)
     time_padded = jnp.pad(time_weight, ((0, 0), (0, LANES - time_share)))
     shares = (qkv_share, out_share)
     qkv_full, out_full, small, times = begin(mixed_shard, small_shard, time_padded, dims, shares, head_dim)
-    gathered = small[:, per]
     vector_share = norm1_gain.shape[0]
-    vectors = gathered[:, : 6 * vector_share].reshape(devices, 6, vector_share).transpose(1, 0, 2)
-    vectors = vectors.reshape(6, width).astype(F32)
-    gain_one, shift_one, b_out, gain_two, shift_two, b_down = (vectors[i : i + 1] for i in range(6))
-    b_up = gathered[:, 6 * vector_share : 6 * vector_share + unit_share].astype(F32)
+    vectors = small[:, per : per + 6, :vector_share].transpose(1, 0, 2).reshape(6, width).astype(F32)
+    b_up = small[:, per + 6, :unit_share].astype(F32)
     b_up = jnp.pad(b_up, ((0, 0), (0, -unit_share % PIECE)))
     b_up = b_up.reshape(devices // BLOCK_DEVICES, BLOCK_DEVICES, b_up.shape[1] // PIECE, PIECE)
     b_up = b_up.transpose(2, 0, 1, 3).reshape(-1, 1, BLOCK_DEVICES * PIECE)
     unit_shards = (pad_rows(fc1_weight.T), pad_rows(fc2_weight))
-    tables = small[:fsdp, per + 1, : 2 * table_size].reshape(fsdp, 2, HEADS // fsdp, 2 * GRID - 1)
-    tables = tables.transpose(1, 0, 2, 3).reshape(2 * HEADS, 2 * GRID - 1)
+    tables = small[:fsdp, table_at : table_at + table_rows, 2 * LANES : 4 * LANES].reshape(HEADS, 2, LANES)
+    tables = tables.transpose(1, 0, 2).reshape(2 * HEADS, LANES)[:, :table_width]
 
     lengths = image_lengths
     large = lengths[0] > slot_rows
@@ -1267,6 +1313,9 @@
     row_hot = ((patch_cells // GRID)[:, None] == grid_index[None, :]).astype(BF16)
     col_hot = ((patch_cells % GRID)[:, None] == grid_index[None, :]).astype(BF16)
     onehot = jnp.concatenate([row_hot, col_hot, row_hot, col_hot], axis=1)
+    both_index = jnp.concatenate([grid_index, grid_index])[:, None]
+    both_cells = jnp.where(jnp.arange(2 * GRID)[:, None] < GRID, patch_cells // GRID, patch_cells % GRID)
+    onehot_t = (both_cells == both_index).astype(BF16)
     lanes_left = ((0, 0), (head_dim, LANES - head_dim - per - 1))
     mask_q = jnp.concatenate(
         [jnp.where(slot_pick, 0.0, BIG), jnp.full((rows, 1), BIG, F32)], axis=1
@@ -1297,24 +1346,25 @@
     scale = 1.0 / math.sqrt(head_dim)
     large_lanes = jnp.broadcast_to(large.astype(F32), (1, LANES))
     normed_one, q, k, v, o, p, up, down = attend(
-        tokens, gain_one, shift_one, qkv_full, times, large_lanes, table, onehot, mask_q, mask_k,
+        tokens, vectors, qkv_full, times, large_lanes, table, onehot, mask_q, mask_k,
         scale * math.log2(math.e), unit_shards, dims,
     )
-    hidden, normed_two = project(tokens, o, out_full, b_out, gain_two, shift_two)
-    dy = jnp.where(valid[:, None], cotangent, jnp.zeros_like(cotangent))
-    y, dn_two, db_up, d_up, d_down, first_sums = mlp(normed_two, dy, b_up, (up, down), unit_shards, dims)
+    hidden, y, dn_two, db_up, d_up, d_down, first_sums = mlp(
+        tokens, o, out_full, vectors, cotangent, mask_k, b_up, (up, down), unit_shards, dims
+    )
     db_up = db_up.reshape(-1, devices // BLOCK_DEVICES, BLOCK_DEVICES, PIECE).transpose(1, 2, 0, 3)
     db_up = db_up.reshape(devices, -1)[:, :unit_share]
-    layer_out, dh, do, d_out, vec_two = turn(hidden, y, b_down, dn_two, dy, gain_two, out_full, o)
-
-    dqkv, d_qkv, sums_q, sums_v, pair, up_sum, down_sum = attend_back(
-        normed_one, p, q, k, v, do, o, onehot, large_lanes, scale,
-        (d_up, d_down), dims,
+
+    beside = dims[1] == 1
+    layer_out, dh, vec_two, dqkv, d_qkv, d_out, slot_sums, pair, *unit_sums = attend_back(
+        hidden, y, dn_two, cotangent, mask_k, vectors, out_full,
+        normed_one, p, q, k, v, o, onehot, onehot_t, large_lanes, scale,
+        (d_up, d_down) if beside else (), first_sums, dims,
     )
-    if first_sums:
-        up_sum = jnp.concatenate([first_sums[0], up_sum], axis=0)
-        down_sum = jnp.concatenate([first_sums[1], down_sum], axis=0)
-    time_send = jnp.concatenate([sums_q, sums_v], axis=0)
+    if not beside:
+        unit_sums = scatter(d_up, dims, 6).T, scatter(d_down, dims, 7)
+    up_sum, down_sum = unit_sums
+    time_send = slot_sums.reshape(2 * HEADS, 8, LANES)
     if time_share != head_dim:
         time_send = time_send[:, :per, :head_dim].transpose(1, 0, 2).reshape(per, devices, time_share)
         time_send = jnp.pad(time_send.transpose(1, 0, 2), ((0, 0), (0, 8 - per), (0, LANES - time_share)))
@@ -1331,8 +1381,8 @@
         axis=0,
     )
     vec_in = jnp.pad(vec_in, ((0, -vec_in.shape[0] % 8), (0, 0)))
-    input_grad, vec_all, time_grad, mixed_sum = end(
-        tokens, dqkv, qkv_full.reshape(HEADS * 3 * LANES, width), gain_one, dh,
+    input_grad, vec_all, time_grad, qkv_sum, out_sum = end(
+        tokens, dqkv, qkv_full.reshape(HEADS * 3 * LANES, width), vectors, dh,
         small.reshape(-1, width), time_send, vec_in, d_qkv, d_out, dims, shares, head_dim,
     )
 
@@ -1348,13 +1398,13 @@
         input_grad,
         vec_sum[0],
         vec_sum[1],
-        mixed_sum[:qkv_share].T,
+        qkv_sum,
         time_grad[:, :time_share],
-        mixed_sum[qkv_share : qkv_share + out_share],
+        out_sum,
         vec_sum[4],
         vec_sum[2],
         vec_sum[3],
-        up_sum[:unit_share].T,
+        up_sum[:, :unit_share],
         up_bias,
         down_sum[:unit_share],
         vec_sum[5],

time: 576 us -> 543 us (0.943); the launches traced: 572 us -> 533 us
  Pallas kernels: 521 us -> 489 us
    pallas_call x4 -> x2, Pallas kernels: 257 us -> 233 us  [the longest x1 124 us: mlp(): pl.pallas_call(functools.partial(mlp_kernel, dims, min(256, rows), projec...]
    pallas_call x1, Pallas kernels: 95.9 us -> 87.6 us  [attend(): pl.pallas_call(functools.partial(attend_kernel, factor, block, dims, piec...]
    slice x10 -> x1, local copies, waits for them, and re-layouts: 8.11 us -> 0.7 us  [local(): small[:fsdp, table_at:table_at + table_rows, 2 * LANES:4 * LANES]]
    unnamed x16 -> x24, local copies, waits for them, and re-layouts: 4.73 us -> 12 us
where the time goes in v4:
time: 543 us; the launch traced here: 533 us
  Pallas kernels  489 us (90%)
  local copies, waits for them, and re-layouts  28.6 us (5%)
  other arithmetic  12.6 us (2%)
    pallas_call x1, Pallas kernels, mlp(): pl.pallas_call(functools.partial(mlp_kernel, dims, min(256, rows), projec...  124 us
    pallas_call x1, Pallas kernels, attend_back(): pl.pallas_call(functools.partial(attend_back_kernel, block, turns, scale,...  109 us
    pallas_call x1, Pallas kernels, end(): pl.pallas_call(functools.partial(end_kernel, dims, pieces, order, shares,...  88.6 us
    pallas_call x1, Pallas kernels, attend(): pl.pallas_call(functools.partial(attend_kernel, factor, block, dims, piec...  87.6 us
    pallas_call x1, Pallas kernels, begin(): pl.pallas_call(functools.partial(begin_kernel, dims, pieces, order, share...  79.1 us
    unnamed x24, local copies, waits for them, and re-layouts  12 us

profile of v4, /device:TPU:0, one launch (start us, length us, event | category | flops | bytes accessed | tf_op | source)
XLA Modules:
  0.0 532.6 jit_solution(16148024548249165163)
XLA Ops:
  0.7 0.7 convert_element_type.58
  1.5 0.7 broadcast_in_dim.94
  2.2 1.5 fusion.21.small_shard
  3.7 1.1 copy.73
  4.8 0.8 pad.73.time_weight
  5.6 1.8 pad_maximum_fusion.1.mixed_shard
  7.3 79.1 %begin.1 = (bf16[16,384,1152]{2,1,0:T(8,128)(2,1)}, bf16[2048,1152]{1,0:T(8,128)(2,1)}, bf16[32,16,1152]{2,1,0:T(8,128)(2,1)}, f32[32,8,128]{2,1,0:T(8,128)}) custom-call(bf16[144,1152]{1,0:T(8,128)(2,1)} %pad_maximum_fusion.1.mixed_shard, bf16[16,1152]{1,0:T(8,128)(2,1)} %fusion.21.small_shard, bf16[1152,128]{1,0:T(8,128)(2,1)} %pad.73.time_weight), custom_call_target="tpu_custom_call" | custom-call | tf_op jit(solution)/shard_map/begin/pallas_call | solution.py:437
  86.5 0.7 slice.79
  87.2 0.6 fusion.3
  87.8 0.3 reduce-precision_convert_fusion
  88.2 1.2 maximum_maximum_fusion.table
  89.6 0.3 copy.78
  89.9 0.9 pad_convert_fusion.mask_k.refs_5_.mask
  90.8 0.9 convert_bitcast_fusion
  91.7 0.7 reshape.202.vectors.refs_3_
  92.5 0.3 iota_compare_fusion.3
  92.8 1.2 add_convert_fusion.onehot
  94.0 0.2 copy.77
  94.2 0.9 fusion.6.mask_q
  95.1 0.5 broadcast_in_dim.95.large
  95.6 87.6 %attend.1 = (bf16[1024,1152]{1,0:T(8,128)(2,1)}, bf16[16,1024,128]{2,1,0:T(8,128)(2,1)}, bf16[16,1024,128]{2,1,0:T(8,128)(2,1)}, bf16[16,1024,128]{2,1,0:T(8,128...) custom-call(bf16[1024,1152]{1,0:T(8,128)(2,1)} %tokens.3, ...), custom_call_target="tpu_custom_call" | custom-call | tf_op jit(solution)/shard_map/attend/pallas_call | solution.py:570
  183.2 1.0 convert_reduce_fusion
  184.3 0.7 reshape.204.refs_6_
  185.0 124.4 %mlp.1 = (f32[1024,1152]{1,0:T(8,128)}, f32[1024,1152]{1,0:T(8,128)}, f32[1024,1152]{1,0:T(8,128)}, f32[6,1,768]{2,1,0:T(1,128)}, bf16[4,2,1,2,2,144,1152]{6,5,4...) custom-call(bf16[1024,1152]{1,0:T(8,128)(2,1)} %tokens.3, ...), custom_call_target="tpu_custom_call" | custom-call | tf_op jit(solution)/shard_map/mlp/pallas_call | solution.py:1003
  309.5 0.8 fusion.9.onehot_t
  310.2 109.0 %attend_back.1 = (bf16[1024,1152]{1,0:T(8,128)(2,1)}, f32[1024,1152]{1,0:T(8,128)}, f32[4,1152]{1,0:T(4,128)}, bf16[1024,6144]{1,0:T(8,128)(2,1)}, bf16[16,384,1...) custom-call(f32[1024,1152]{1,0:T(8,128)} %get-tuple-element.58.hidde, ...), custom_call_target="tpu_custom_call" | custom-call | tf_op jit(solution)/shard_map/attend_back/pallas_call | solution.py:738
  419.3 1.2 fusion.32
  420.5 0.7 convolution_bitcast_fusion
  421.6 0.8 select_maximum_fusion
  422.4 0.6 pad.78.vec_in
  423.1 88.6 %end.1 = (bf16[1024,1152]{1,0:T(8,128)(2,1)}, f32[16,1152]{1,0:T(8,128)}, f32[1152,128]{1,0:T(8,128)}, f32[1152,108]{1,0:T(8,128)}, f32[36,1152]{1,0:T(8,128)}) custom-call(bf16[1024,1152]{1,0:T(8,128)(2,1)} %tokens.3, bf16[1024,6144]{1,0:T(8,128)(2,1)} %get-tuple-element.71.dqkv, bf16[6144,1152]{1,0:T(8,128)(2,1)} %bitcast.63, ...), custom_call_target="tpu_custom_call" | custom-call | tf_op jit(solution)/shard_map/end/pallas_call | solution.py:1197
  511.7 2.3 copy.82
  513.9 2.0 copy.83
  515.9 1.4 slice.88
  517.3 0.8 constant_dynamic-slice_fusion
  518.1 0.5 slice_bitcast_fusion.4
  518.6 1.5 slice.95
  520.1 1.3 reshape.200
  521.5 1.3 dynamic_slice.11
  522.8 1.4 slice.97
  524.2 0.8 reshape.201
  524.9 0.6 dynamic-slice_bitcast_fusion
  525.5 1.2 copy.84
  526.7 1.4 copy.99
  528.1 1.1 copy-done.1
  529.2 1.4 copy.100
  530.7 0.7 copy.101
  531.3 0.8 copy.102
  (45 shorter events, 1.1 us)
Async XLA Ops:
  0.6 88.7 %copy-start.7 = (s32[4]{0:T(128)S(1)}, s32[4]{0:T(128)}, u32[]{:S(2)}) copy-start(s32[4]{0:T(128)} %param.20) | copy-start | bytes 52
  0.7 91.8 %copy-start.6 = (s32[1024]{0:T(1024)S(1)}, s32[1024]{0:T(1024)}, u32[]{:S(2)}) copy-start(s32[1024]{0:T(1024)} %param.22) | copy-start | bytes 12292
  310.2 111.0 %copy-start.5 = (f32[6,1,768]{2,1,0:T(1,128)S(1)}, f32[6,1,768]{2,1,0:T(1,128)}, u32[]{:S(2)}) copy-start(f32[6,1,768]{2,1,0:T(1,128)} %get-tuple-element.75) | copy-start | bytes 55300
  423.1 102.5 %copy-start.2 = (f32[1152,144]{1,0:T(8,128)S(1)}, f32[1152,144]{1,0:T(8,128)}, u32[]{:S(2)}) copy-start(f32[1152,144]{1,0:T(8,128)} %get-tuple-element.144) | copy-start | bytes 1990660
  511.7 15.1 %copy-start = (bf16[1024,1152]{1,0:T(8,128)(2,1)S(1)}, bf16[1024,1152]{1,0:T(8,128)(2,1)}, u32[]{:S(2)}) copy-start(bf16[1024,1152]{1,0:T(8,128)(2,1)} %get-tuple-element.190) | copy-start | bytes 7077892
  526.7 2.5 copy-start.1
  526.7 3.9 copy-start.4
  526.7 4.6 copy-start.3

commit v5 on v4

--- a/solution.py
+++ b/solution.py
@@ -258,8 +258,7 @@
 
         def body(i, carry):
             g1, g2 = i // at.G2, i % at.G2
-            total = target[g1, g2].astype(F32) + addend[g1, g2].astype(F32)
-            target[g1, g2] = total.astype(BF16)
+            target[g1, g2] = target[g1, g2] + addend[g1, g2]
             return carry
 
         lax.fori_loop(0, at.G1 * at.G2, body, 0)
@@ -387,7 +386,7 @@
 
 
 def begin_kernel(dims, pieces, order, shares, head_dim, mixed_shard, small_shard, time_weight, qkv_out, out_out, small_out,
-                 time_out, mixed, small, time_all, time_got, sems, own_sems, time_sems):
+                 time_out, qkv, outs, mixed, small, time_all, time_got, sems, own_sems, time_sems, laid_sems):
     work = Gather(dims, pieces, (small_shard, mixed_shard), (small, mixed), sems, own_sems)
     at = work.at
     devices = at.count()
@@ -420,10 +419,19 @@
         parts.append(jnp.zeros((LANES - head_dim, width), BF16))
         return jnp.concatenate(parts, axis=0)
 
+    def laid(number):
+        if number == HEADS:
+            return pltpu.make_async_copy(outs, out_out, laid_sems.at[number])
+        return pltpu.make_async_copy(qkv.at[number], qkv_out.at[number], laid_sems.at[number])
+
     for head in range(HEADS):
         for kind in range(3):
-            qkv_out[head, kind * LANES : (kind + 1) * LANES] = rows_of((kind * HEADS + head) * head_dim, shares[0], 0)
-        out_out[head * LANES : (head + 1) * LANES] = rows_of(head * head_dim, shares[1], shares[0])
+            qkv[head, kind * LANES : (kind + 1) * LANES] = rows_of((kind * HEADS + head) * head_dim, shares[0], 0)
+        laid(head).start()
+        outs[head * LANES : (head + 1) * LANES] = rows_of(head * head_dim, shares[1], shares[0])
+    laid(HEADS).start()
+    for number in range(HEADS + 1):
+        laid(number).wait()
 
 
 def begin(mixed_shard, small_shard, time_weight, dims, shares, head_dim):
@@ -437,7 +445,7 @@
     return pl.pallas_call(
         functools.partial(begin_kernel, dims, pieces, order, shares, head_dim),
         in_specs=[anywhere, anywhere, vmem],
-        out_specs=[vmem] * 4,
+        out_specs=[anywhere, anywhere, vmem, vmem],
         out_shape=[
             jax.ShapeDtypeStruct((HEADS, 3 * LANES, width), BF16),
             jax.ShapeDtypeStruct((HEADS * LANES, width), BF16),
@@ -445,12 +453,15 @@
             jax.ShapeDtypeStruct((devices, 8, LANES), F32),
         ],
         scratch_shapes=[
+            pltpu.VMEM((HEADS, 3 * LANES, width), BF16),
+            pltpu.VMEM((HEADS * LANES, width), BF16),
             pltpu.VMEM(spread_of(dims) + mixed_shard.shape, BF16),
             pltpu.VMEM(spread_of(dims) + small_shard.shape, BF16),
             pltpu.VMEM((devices, small_rows, LANES), F32),
             pltpu.VMEM((devices, 8, LANES), F32),
             *Gather.scratch(dims, pieces),
             pltpu.SemaphoreType.DMA((2,)),
+            pltpu.SemaphoreType.DMA((HEADS + 1,)),
         ],
         compiler_params=params(collective_id=1, has_side_effects=True),
         name="begin",
@@ -634,14 +645,9 @@
     ready = take(ready)
     out, dh_out, vec_out, dqkv_out, dw_out, dwo_out, sums_out, pair_out = take(8)
     results = take(2 if pieces else 0)
-    da_all, do_all, keys, grads, offsets, dk_sum, dv_sum = take(7)
-
-    def put(array, start, count, total):
-        if array == 0:
-            results[0][:, start : start + count] = total.T
-        else:
-            results[1][start : start + count] = total
-
+    da_all, do_all, keys, grads, offsets, dq_all, dk_sum, dv_sum = take(8)
+
+    put = store_rows(results)
     work = Scatter(dims, pieces, parts, put, *refs) if pieces else None
     rows = normed.shape[0]
     step = pl.program_id(0)
@@ -680,7 +686,7 @@
             centred = dot_nt(grads[span], values)
             ds = (p[0, span].astype(F32) * centred).astype(BF16)
             both = dot_nn(ds, keys[...])
-            dqkv_out[span, :LANES] = (both[:, :LANES] * scale).astype(BF16)
+            dq_all[span] = both[:, :LANES] * scale
             by_place = both[:, LANES:]
             upper = by_place.astype(BF16)
             offsets[span, :LANES] = upper
@@ -693,8 +699,11 @@
             else:
                 dk_sum[...] += dk
                 dv_sum[...] += dv
-        dqkv_out[:, LANES : 2 * LANES] = (dk_sum[...] * scale).T.astype(BF16)
+        dk_sum[...] = dk_sum[...] * scale
+        dqkv_out[:, :LANES] = dq_all[...].astype(BF16)
+        dqkv_out[:, LANES : 2 * LANES] = dk_sum[...].T.astype(BF16)
         dqkv_out[:, 2 * LANES :] = dv_sum[...].T.astype(BF16)
+        turned = jnp.concatenate([dq_all[...].T[:head], dk_sum[:head], dv_sum[:head]], axis=0)
         pair = dot_nn(onehot_t[...], offsets[...])
         pair_out[0] = pair[:, :LANES] + pair[:, LANES:]
         slot = SMALL * SMALL
@@ -708,7 +717,7 @@
             sums = [jnp.where(one, total if i == 0 else jnp.zeros_like(total), part) for i, part in enumerate(sums)]
             sums.append(jnp.zeros((8 - len(sums), LANES), F32))
             sums_out[kind, 0] = jnp.concatenate(sums, axis=0)
-        dw_out[0] = dot_tn(dqkv_out[...], normed[...]).astype(BF16)
+        dw_out[0] = dot_nn(turned.astype(BF16), normed[...]).astype(BF16)
         dwo_out[...] = dot_tn(o[...], da_all[...]).astype(BF16)
 
     if pieces:
@@ -723,6 +732,7 @@
     hidden, y, dn, cotangent, mask, vectors, weight, normed, p, q, k, v, o, onehot, onehot_t, large, scale, parts, ready, dims
 ):
     rows, width = normed.shape
+    head_dim = width // HEADS
     block = min(512, rows)
     turns = TURNS
     some = rows // turns
@@ -730,7 +740,7 @@
     if parts:
         shard_rows = parts[0].shape[5]
         pieces = pieces_of(summed_rows(shard_rows), shard_rows)
-        sum_shapes = [(width, shard_rows), (shard_rows, width)]
+        sum_shapes = [(shard_rows, width)] * 2
     anywhere = pl.BlockSpec(memory_space=pl.ANY)
     head_of = lambda s: jnp.maximum(s - turns, 0)
     per_head = lambda *shape: pl.BlockSpec((1,) + shape, lambda s: (head_of(s), 0, 0))
@@ -766,7 +776,7 @@
             by_rows,
             resident((4, width)),
             pl.BlockSpec((rows, 3 * LANES), lambda s: (0, head_of(s))),
-            per_head(3 * LANES, width),
+            per_head(3 * head_dim, width),
             pl.BlockSpec((LANES, width), lambda s: (head_of(s), 0)),
             pl.BlockSpec((2, 1, 8, LANES), lambda s: (0, head_of(s), 0, 0)),
             per_head(onehot_t.shape[0], LANES),
@@ -777,7 +787,7 @@
             jax.ShapeDtypeStruct(hidden.shape, F32),
             jax.ShapeDtypeStruct((4, width), F32),
             jax.ShapeDtypeStruct((rows, HEADS * 3 * LANES), BF16),
-            jax.ShapeDtypeStruct((HEADS, 3 * LANES, width), BF16),
+            jax.ShapeDtypeStruct((HEADS, 3 * head_dim, width), BF16),
             jax.ShapeDtypeStruct((HEADS * LANES, width), BF16),
             jax.ShapeDtypeStruct((2, HEADS, 8, LANES), F32),
             jax.ShapeDtypeStruct((HEADS, onehot_t.shape[0], LANES), F32),
@@ -789,6 +799,7 @@
             pltpu.VMEM((rows, 2 * LANES), BF16),
             pltpu.VMEM((rows, LANES), BF16),
             pltpu.VMEM((rows, 2 * LANES), BF16),
+            pltpu.VMEM((rows, LANES), F32),
             pltpu.VMEM((LANES, rows), F32),
             pltpu.VMEM((LANES, rows), F32),
             *(Scatter.scratch(dims, pieces, width) if pieces else []),
@@ -1095,8 +1106,8 @@
             self.total[...] = total
 
 
-def end_kernel(dims, pieces, order, shares, head_dim, tokens, dqkv, weight, vectors, dh, small, time_send, vec_in, dw, dw_out,
-               out, vec_out, time_out, qkv_out, out_out, mixed, dw_buffer, dw_sems, time_got, time_sems,
+def end_kernel(dims, pieces, order, shares, head_dim, tokens, dqkv, weight_all, vectors, dh, small, time_send, vec_in, dw, dw_out,
+               out, vec_out, time_out, qkv_out, out_out, weight, weight_sem, mixed, dw_buffer, dw_sems, time_got, time_sems,
                vec_total, vec_send, vec_got, vec_sems, *buffers):
     step = pl.program_id(0)
     steps = pl.num_programs(0)
@@ -1104,7 +1115,7 @@
     def put_sum(array, start, count, total):
         stop, cut_at = start + count, shares[0]
         if start < cut_at:
-            qkv_out[:, start : min(stop, cut_at)] = total[: min(stop, cut_at) - start].T
+            qkv_out[start : min(stop, cut_at)] = total[: min(stop, cut_at) - start]
         first, last = max(start, cut_at), min(stop, sum(shares))
         if first < last:
             out_out[first - cut_at : last - cut_at] = total[first - start : last - start]
@@ -1119,7 +1130,7 @@
     def fetch(number):
         slot = number % 2
         if number < HEADS:
-            return pltpu.make_async_copy(dw.at[number], dw_buffer.at[slot], dw_sems.at[slot])
+            return pltpu.make_async_copy(dw.at[number], dw_buffer.at[slot, pl.ds(0, dw.shape[1])], dw_sems.at[slot])
         source = dw_out.at[pl.ds((number - HEADS) * pair, pair)]
         return pltpu.make_async_copy(source, dw_buffer.at[slot, pl.ds(0, pair)], dw_sems.at[slot])
 
@@ -1141,6 +1152,7 @@
     @pl.when(step == 0)
     def _():
         fetch(0).start()
+        pltpu.make_async_copy(weight_all, weight, weight_sem).start()
         time_got[...] = jnp.zeros_like(time_got)
         at.barrier_all()
         exchange(at, time_send, time_got, time_sems)
@@ -1151,7 +1163,7 @@
             fetch(number).wait()
             if number < HEADS:
                 for kind in range(3):
-                    value = dw_buffer[number % 2, kind * LANES : kind * LANES + head_dim]
+                    value = dw_buffer[number % 2, kind * head_dim : (kind + 1) * head_dim]
                     put((kind * HEADS + number) * head_dim, shares[0], 0, value)
             else:
                 for i in range(2):
@@ -1162,11 +1174,15 @@
     for place in range(len(order) - 1):
         events(order, step, work, place)
 
+    @pl.when(step == 0)
+    def _():
+        pltpu.make_async_copy(weight_all, weight, weight_sem).wait()
+
     dn = dot_nn(dqkv[...], weight[...])
     back, unit = norm_back(tokens[...].astype(F32), vectors[0:1], dn)
     out[...] = (dh[...] + back).astype(BF16)
-    vec_total[0:1] += jnp.sum(dn * unit, axis=0, keepdims=True)
-    vec_total[1:2] += jnp.sum(dn, axis=0, keepdims=True)
+    vec_total[0:1, :width] += jnp.sum(dn * unit, axis=0, keepdims=True)
+    vec_total[1:2, :width] += jnp.sum(dn, axis=0, keepdims=True)
 
     @pl.when(step == steps - 1)
     def _():
@@ -1182,10 +1198,10 @@
         times = time_got[...].reshape(small.shape[0], LANES)
         high = times.astype(BF16)
         low = (times - high.astype(F32)).astype(BF16)
-        time_out[...] = dot_tn(small[...], high) + dot_tn(small[...], low)
-
-
-def end(tokens, dqkv, weight, vectors, dh, small, time_send, vec_in, dw, dw_out, dims, shares, head_dim):
+        time_out[...] = (dot_tn(high, small[...]) + dot_tn(low, small[...]))[: time_out.shape[0]]
+
+
+def end(tokens, dqkv, weight, vectors, dh, small, time_send, vec_in, dw, dw_out, dims, shares, time_share, head_dim):
     rows, width = tokens.shape
     block = rows // 8
     by_rows = lambda cols: pl.BlockSpec((block, cols), lambda i: (i, 0))
@@ -1200,7 +1216,7 @@
         in_specs=[
             by_rows(width),
             by_rows(dqkv.shape[1]),
-            resident(weight.shape),
+            anywhere,
             resident(vectors.shape),
             by_rows(width),
             resident(small.shape),
@@ -1212,20 +1228,22 @@
         out_specs=[
             by_rows(width),
             resident(vec_in.shape),
-            resident((width, LANES)),
-            resident((width, shares[0])),
+            resident((time_share, width)),
+            resident((shares[0], width)),
             resident((shares[1], width)),
         ],
         out_shape=[
             jax.ShapeDtypeStruct(tokens.shape, BF16),
             jax.ShapeDtypeStruct(vec_in.shape, F32),
-            jax.ShapeDtypeStruct((width, LANES), F32),
-            jax.ShapeDtypeStruct((width, shares[0]), F32),
+            jax.ShapeDtypeStruct((time_share, width), F32),
+            jax.ShapeDtypeStruct((shares[0], width), F32),
             jax.ShapeDtypeStruct((shares[1], width), F32),
         ],
         scratch_shapes=[
+            pltpu.VMEM(weight.shape, BF16),
+            pltpu.SemaphoreType.DMA,
             pltpu.VMEM(spread_of(dims) + (shard_rows, width), BF16),
-            pltpu.VMEM((2,) + dw.shape[1:], BF16),
+            pltpu.VMEM((2, 2 * LANES, width), BF16),
             pltpu.SemaphoreType.DMA((2,)),
             pltpu.VMEM((devices, small.shape[0] // devices, LANES), F32),
             pltpu.SemaphoreType.DMA((2,)),
@@ -1235,6 +1253,48 @@
         compiler_params=params(collective_id=4, has_side_effects=True),
         name="end",
     )(tokens, dqkv, weight, vectors, dh, small, time_send, vec_in, dw, dw_out)
+
+
+def split_kernel(width, share, unit_share, heads, total, *refs):
+    count = (len(refs) - 10) // 3
+    sources, outs, targets = refs[:count], refs[count : count + 9], refs[count + 9 : 2 * count + 9]
+    middles, sems = refs[2 * count + 9 : -1], refs[-1]
+    for i in range(count):
+        pltpu.make_async_copy(sources[i], middles[i], sems.at[i]).start()
+    for i in range(count):
+        pltpu.make_async_copy(sources[i], middles[i], sems.at[i]).wait()
+        pltpu.make_async_copy(middles[i], targets[i], sems.at[i]).start()
+    place = lax.axis_index("dp") * lax.axis_size("fsdp") + lax.axis_index("fsdp")
+    turned = pltpu.roll(total[0:8, :width], (width - place * share) % width, 1)
+    for i in range(6):
+        outs[i][...] = turned[i, :share]
+    per_row = width // unit_share
+    row = jnp.zeros((8, width), F32)
+    for i in range(4):
+        row = jnp.where(place // per_row == i, total[6 + i : 7 + i, :width], row)
+    row = pltpu.roll(row, (width - place % per_row * unit_share) % width, 1)
+    outs[6][...] = row[0, :unit_share]
+    mine = pl.ds(pl.multiple_of(lax.axis_index("fsdp") * heads, heads), heads)
+    for i in range(2):
+        outs[7 + i][...] = total[mine, width + i * LANES : width + i * LANES + 2 * GRID - 1]
+    for i in range(count):
+        pltpu.make_async_copy(middles[i], targets[i], sems.at[i]).wait()
+
+
+def split(total, width, share, unit_share, heads, results):
+    vmem, anywhere = pl.BlockSpec(memory_space=pltpu.VMEM), pl.BlockSpec(memory_space=pl.ANY)
+    shapes = [(share,)] * 6 + [(unit_share,)] + [(heads, 2 * GRID - 1)] * 2
+    return pl.pallas_call(
+        functools.partial(split_kernel, width, share, unit_share, heads),
+        in_specs=[vmem] + [anywhere] * len(results),
+        out_specs=[vmem] * len(shapes) + [anywhere] * len(results),
+        out_shape=[jax.ShapeDtypeStruct(shape, F32) for shape in shapes]
+        + [jax.ShapeDtypeStruct(result.shape, result.dtype) for result in results],
+        scratch_shapes=[pltpu.VMEM(result.shape, result.dtype) for result in results]
+        + [pltpu.SemaphoreType.DMA((len(results),))],
+        compiler_params=params(),
+        name="split",
+    )(total, *results)
 
 
 def time_embed(stamps, feat_width):
@@ -1362,7 +1422,7 @@
         (d_up, d_down) if beside else (), first_sums, dims,
     )
     if not beside:
-        unit_sums = scatter(d_up, dims, 6).T, scatter(d_down, dims, 7)
+        unit_sums = scatter(d_up, dims, 6), scatter(d_down, dims, 7)
     up_sum, down_sum = unit_sums
     time_send = slot_sums.reshape(2 * HEADS, 8, LANES)
     if time_share != head_dim:
@@ -1370,46 +1430,39 @@
         time_send = jnp.pad(time_send.transpose(1, 0, 2), ((0, 0), (0, 8 - per), (0, LANES - time_share)))
     pairs = jnp.concatenate([pair[:, :GRID, :GRID], pair[:, GRID : 2 * GRID, GRID : 2 * GRID]])
     tables = jnp.dot(pairs.reshape(2 * HEADS, GRID * GRID), diagonal.astype(F32), precision=HIGHEST)
-    tables = tables.reshape(2, HEADS * (2 * GRID - 1))
-    vec_in = jnp.concatenate(
-        [
-            jnp.zeros((2, width), F32),
-            vec_two,
-            db_up.reshape(units // width, width),
-            jnp.pad(tables, ((0, 0), (0, width - tables.shape[1]))),
-        ],
-        axis=0,
+    vec_rows, vec_width = HEADS, width + 2 * LANES
+    put_in = lambda part, row, lane: jnp.pad(
+        part, ((row, vec_rows - row - part.shape[0]), (lane, vec_width - lane - part.shape[1]))
     )
-    vec_in = jnp.pad(vec_in, ((0, -vec_in.shape[0] % 8), (0, 0)))
+    vec_in = put_in(vec_two, 2, 0) + put_in(db_up.reshape(units // width, width), 6, 0)
+    vec_in = vec_in + put_in(tables[:HEADS], 0, width) + put_in(tables[HEADS:], 0, width + LANES)
     input_grad, vec_all, time_grad, qkv_sum, out_sum = end(
         tokens, dqkv, qkv_full.reshape(HEADS * 3 * LANES, width), vectors, dh,
-        small.reshape(-1, width), time_send, vec_in, d_qkv, d_out, dims, shares, head_dim,
+        small.reshape(-1, width), time_send, vec_in, d_qkv, d_out, dims, shares, time_share, head_dim,
     )
 
-    place = lax.axis_index("dp") * fsdp + lax.axis_index("fsdp")
-    vec_sum = lax.dynamic_slice_in_dim(vec_all[:6], place * vector_share, vector_share, 1)
-    up_bias = vec_all[6 : 6 + units // width].reshape(units)
-    up_bias = lax.dynamic_slice_in_dim(up_bias, place * unit_share, unit_share)
-    tables = vec_all[6 + units // width :][:2, : HEADS * (2 * GRID - 1)].reshape(2, fsdp, -1, 2 * GRID - 1)
-    tables = lax.dynamic_index_in_dim(tables, lax.axis_index("fsdp"), 1, keepdims=False)
+    results = (layer_out, input_grad, qkv_sum, time_grad, out_sum, up_sum[:unit_share], down_sum[:unit_share])
+    found = split(vec_all, width, vector_share, unit_share, HEADS // fsdp, results)
+    vec_sum, (up_bias, row_sum, col_sum) = found[:6], found[6:9]
+    layer_out, input_grad, qkv_sum, time_grad, out_sum, up_sum, down_sum = found[9:]
 
     return (
         layer_out,
         input_grad,
         vec_sum[0],
         vec_sum[1],
-        qkv_sum,
-        time_grad[:, :time_share],
+        qkv_sum.T,
+        time_grad.T,
         out_sum,
         vec_sum[4],
         vec_sum[2],
         vec_sum[3],
-        up_sum[:, :unit_share],
+        up_sum.T,
         up_bias,
-        down_sum[:unit_share],
+        down_sum,
         vec_sum[5],
-        tables[0],
-        tables[1],
+        row_sum,
+        col_sum,
     )
 
 

time: 543 us -> 526 us (0.969)
  local copies, waits for them, and re-layouts: 28.6 us -> 7.39 us
  Pallas kernels: 489 us -> 495 us
    unnamed x24 -> x3, local copies, waits for them, and re-layouts: 12 us -> 1.13 us
    pallas_call x1, Pallas kernels: 124 us -> 134 us  [mlp(): pl.pallas_call(functools.partial(mlp_kernel, dims, min(256, rows), projec...]
    pallas_call x1, Pallas kernels: 109 us -> 102 us  [attend_back(): pl.pallas_call(functools.partial(attend_back_kernel, block, turns, scale,...]
    pallas_call x0 -> x1, Pallas kernels: none -> 6.48 us  [split(): pl.pallas_call(functools.partial(split_kernel, width, share, unit_share,...]
where the time goes in v5:
time: 526 us; the launch traced here: 521 us
  Pallas kernels  495 us (94%)
  other arithmetic  14.6 us (3%)
  local copies, waits for them, and re-layouts  7.39 us (1%)
    pallas_call x1, Pallas kernels, mlp(): pl.pallas_call(functools.partial(mlp_kernel, dims, min(256, rows), projec...  134 us
    pallas_call x1, Pallas kernels, attend_back(): pl.pallas_call(functools.partial(attend_back_kernel, block, turns, scale,...  102 us
    pallas_call x1, Pallas kernels, attend(): pl.pallas_call(functools.partial(attend_kernel, factor, block, dims, piec...  87.5 us
    pallas_call x1, Pallas kernels, end(): pl.pallas_call(functools.partial(end_kernel, dims, pieces, order, shares,...  86.4 us
    pallas_call x1, Pallas kernels, begin(): pl.pallas_call(functools.partial(begin_kernel, dims, pieces, order, share...  79.3 us

profile of v5, /device:TPU:0, one launch (start us, length us, event | category | flops | bytes accessed | tf_op | source)
XLA Modules:
  0.0 520.5 jit_solution(7867543042102119271)
XLA Ops:
  1.3 0.5 broadcast_in_dim.92.large
  1.8 0.7 convert_element_type.62
  2.5 0.1 pad.107.clone
  2.6 0.1 pad_add_fusion.2
  2.6 0.7 broadcast_in_dim.91
  3.3 0.7 select_reduce_fusion
  4.1 0.2 fusion.22
  4.3 0.7 add_select_fusion.2
  5.0 1.5 fusion.21.small_shard
  6.5 0.3 copy.69
  6.8 0.8 fusion.9.onehot_t
  7.6 0.9 pad_convert_fusion.mask_k.refs_5_.mask
  8.5 0.2 copy.68
  8.7 0.9 fusion.6.mask_q
  9.5 0.3 iota_compare_fusion.3
  9.9 1.2 add_convert_fusion.onehot
  11.1 1.1 copy.64
  12.2 0.8 pad.81.time_weight
  13.0 1.8 pad_maximum_fusion.1.mixed_shard
  14.7 79.3 %begin.1 = (bf16[16,384,1152]{2,1,0:T(8,128)(2,1)}, bf16[2048,1152]{1,0:T(8,128)(2,1)}, bf16[32,16,1152]{2,1,0:T(8,128)(2,1)}, f32[32,8,128]{2,1,0:T(8,128)}) custom-call(bf16[144,1152]{1,0:T(8,128)(2,1)} %pad_maximum_fusion.1.mixed_shard, bf16[16,1152]{1,0:T(8,128)(2,1)} %fusion.21.small_shard, bf16[1152,128]{1,0:T(8,128)(2,1)} %pad.81.time_weight), custom_call_target="tpu_custom_call" | custom-call | tf_op jit(solution)/shard_map/begin/pallas_call | solution.py:445
  94.0 0.7 slice.45
  94.8 1.0 convert_reduce_fusion
  95.8 0.1 reshape.191
  95.9 0.7 reshape.188.refs_6_
  96.6 0.9 convert_bitcast_fusion
  97.6 0.7 reshape.186.vectors.refs_3_
  98.3 0.6 fusion.3
  98.9 0.3 reduce-precision_convert_fusion
  99.2 1.2 maximum_maximum_fusion.table
  100.4 87.5 %attend.1 = (bf16[1024,1152]{1,0:T(8,128)(2,1)}, bf16[16,1024,128]{2,1,0:T(8,128)(2,1)}, bf16[16,1024,128]{2,1,0:T(8,128)(2,1)}, bf16[16,1024,128]{2,1,0:T(8,128...) custom-call(bf16[1024,1152]{1,0:T(8,128)(2,1)} %tokens.3, ...), custom_call_target="tpu_custom_call" | custom-call | tf_op jit(solution)/shard_map/attend/pallas_call | solution.py:581
  187.9 134.0 %mlp.1 = (f32[1024,1152]{1,0:T(8,128)}, f32[1024,1152]{1,0:T(8,128)}, f32[1024,1152]{1,0:T(8,128)}, f32[6,1,768]{2,1,0:T(1,128)}, bf16[4,2,1,2,2,144,1152]{6,5,4...) custom-call(bf16[1024,1152]{1,0:T(8,128)(2,1)} %tokens.3, ...), custom_call_target="tpu_custom_call" | custom-call | tf_op jit(solution)/shard_map/mlp/pallas_call | solution.py:1014
  322.0 0.0 copy-start
  322.0 101.6 %attend_back.1 = (bf16[1024,1152]{1,0:T(8,128)(2,1)}, f32[1024,1152]{1,0:T(8,128)}, f32[4,1152]{1,0:T(4,128)}, bf16[1024,6144]{1,0:T(8,128)(2,1)}, bf16[16,216,1...) custom-call(f32[1024,1152]{1,0:T(8,128)} %get-tuple-element.74.hidde, ...), custom_call_target="tpu_custom_call" | custom-call | tf_op jit(solution)/shard_map/attend_back/pallas_call | solution.py:748
  423.6 0.0 copy-done
  423.6 0.1 reshape.185
  423.8 0.1 reshape_reshape.3
  423.9 1.2 fusion.32
  425.1 0.7 convolution_bitcast_fusion
  425.8 1.4 pad_add_fusion.vec_in
  427.2 86.4 %end.1 = (bf16[1024,1152]{1,0:T(8,128)(2,1)}, f32[16,1408]{1,0:T(8,128)}, f32[72,1152]{1,0:T(8,128)}, f32[108,1152]{1,0:T(8,128)}, f32[36,1152]{1,0:T(8,128)}) custom-call(bf16[1024,1152]{1,0:T(8,128)(2,1)} %tokens.3, bf16[1024,6144]{1,0:T(8,128)(2,1)} %get-tuple-element.86.dqkv, bf16[6144,1152]{1,0:T(8,128)(2,1)} %bitcast.49, ...), custom_call_target="tpu_custom_call" | custom-call | tf_op jit(solution)/shard_map/end/pallas_call | solution.py:1213
  513.6 6.5 %split.1 = (f32[36]{0:T(128)}, f32[36]{0:T(128)}, f32[36]{0:T(128)}, f32[36]{0:T(128)}, f32[36]{0:T(128)}, /*index=5*/f32[36]{0:T(128)}, f32[144]{0:T(256)}, f32...) custom-call(f32[16,1408]{1,0:T(8,128)} %get-tuple-element.94.total, ...), custom_call_target="tpu_custom_call" | custom-call | tf_op jit(solution)/shard_map/split/pallas_call | solution.py:1287
  (20 shorter events, 0.3 us)
Async XLA Ops:
  322.0 101.6 %copy-start = (f32[6,1,768]{2,1,0:T(1,128)S(1)}, f32[6,1,768]{2,1,0:T(1,128)}, u32[]{:S(2)}) copy-start(f32[6,1,768]{2,1,0:T(1,128)} %get-tuple-element.90) | copy-start | bytes 55300

commit v6 on v5

--- a/solution.py
+++ b/solution.py
@@ -385,15 +385,44 @@
     wait_for(view, sems.at[0])
 
 
-def begin_kernel(dims, pieces, order, shares, head_dim, mixed_shard, small_shard, time_weight, qkv_out, out_out, small_out,
-                 time_out, qkv, outs, mixed, small, time_all, time_got, sems, own_sems, time_sems, laid_sems):
+def frame_arrays(head_dim, cells, cells_row, lengths, onehot, onehot_t, mask_q, mask_k, large):
+    rows = onehot.shape[0]
+    slot_rows = SMALL * SMALL
+    per = rows // slot_rows
+    lane = lax.broadcasted_iota(jnp.int32, (rows, LANES), 1)
+    row = lax.broadcasted_iota(jnp.int32, (rows, LANES), 0)
+    cell = jnp.broadcast_to(cells[...], (rows, LANES))
+    place = jnp.where(lane % (2 * GRID) < GRID, cell // GRID, cell % GRID)
+    onehot[...] = jnp.where(place == lane % GRID, 1.0, 0.0).astype(BF16)
+    index = lax.broadcasted_iota(jnp.int32, (2 * GRID, rows), 0)
+    cell = jnp.broadcast_to(cells_row[...], (2 * GRID, rows))
+    place = jnp.where(index < GRID, cell // GRID, cell % GRID)
+    onehot_t[...] = jnp.where(place == index % GRID, 1.0, 0.0).astype(BF16)
+    one = jnp.broadcast_to(lengths[0], (rows, LANES)) > slot_rows
+    slot = jnp.where(one, 0, row // slot_rows)
+    length = jnp.zeros((rows, LANES), jnp.int32)
+    for i in range(per):
+        length = jnp.where(slot == i, lengths[i], length)
+    valid = row - slot * slot_rows < length
+    own = slot == lane - head_dim
+    in_slots = (lane >= head_dim) & (lane < head_dim + per)
+    last = lane == head_dim + per
+    mask_q[...] = jnp.where(last | (in_slots & jnp.logical_not(own)), BIG, 0.0).astype(BF16)
+    mask_k[...] = jnp.where((in_slots & own) | (last & jnp.logical_not(valid)), 1.0, 0.0).astype(BF16)
+    large[...] = jnp.where(one[0:1], 1.0, 0.0)
+
+
+def begin_kernel(dims, pieces, order, shares, head_dim, mixed_shard, small_shard, time_weight, cells, cells_row, lengths, qkv_out, out_out, small_out,
+                 time_out, onehot_out, onehot_t_out, mask_q_out, mask_k_out, large_out, qkv, outs, mixed, small, time_all, time_got, sems, own_sems, time_sems, laid_sems):
     work = Gather(dims, pieces, (small_shard, mixed_shard), (small, mixed), sems, own_sems)
     at = work.at
     devices = at.count()
     width = mixed.shape[-1]
     at.barrier_all()
-    for event in order:
+    for count, event in enumerate(order):
         work.stage(*divmod(event, 10))
+        if count == 5:
+            frame_arrays(head_dim, cells, cells_row, lengths, onehot_out, onehot_t_out, mask_q_out, mask_k_out, large_out)
         if event == STAGES - 1:
             small_out[...] = small[...].reshape(small_out.shape)
             for start in range(0, devices, 32):
@@ -434,9 +463,10 @@
         laid(number).wait()
 
 
-def begin(mixed_shard, small_shard, time_weight, dims, shares, head_dim):
+def begin(mixed_shard, small_shard, time_weight, patch_cells, image_lengths, dims, shares, head_dim):
     width = mixed_shard.shape[1]
     small_rows = small_shard.shape[0]
+    rows = patch_cells.shape[0]
     devices = dims[0] * dims[1] * 8
     pieces = [(0, 0, small_rows)] + cut(1, mixed_shard.shape[0], BEGIN_ROWS)
     (order,) = order_for(BEGIN_ORDER, pieces, 1)
@@ -444,13 +474,18 @@
     vmem = pl.BlockSpec(memory_space=pltpu.VMEM)
     return pl.pallas_call(
         functools.partial(begin_kernel, dims, pieces, order, shares, head_dim),
-        in_specs=[anywhere, anywhere, vmem],
-        out_specs=[anywhere, anywhere, vmem, vmem],
+        in_specs=[anywhere, anywhere, vmem, vmem, vmem, pl.BlockSpec(memory_space=pltpu.SMEM)],
+        out_specs=[anywhere, anywhere] + [vmem] * 7,
         out_shape=[
             jax.ShapeDtypeStruct((HEADS, 3 * LANES, width), BF16),
             jax.ShapeDtypeStruct((HEADS * LANES, width), BF16),
             jax.ShapeDtypeStruct((devices, small_rows, width), BF16),
             jax.ShapeDtypeStruct((devices, 8, LANES), F32),
+            jax.ShapeDtypeStruct((rows, LANES), BF16),
+            jax.ShapeDtypeStruct((2 * GRID, rows), BF16),
+            jax.ShapeDtypeStruct((rows, LANES), BF16),
+            jax.ShapeDtypeStruct((rows, LANES), BF16),
+            jax.ShapeDtypeStruct((1, LANES), F32),
         ],
         scratch_shapes=[
             pltpu.VMEM((HEADS, 3 * LANES, width), BF16),
@@ -465,7 +500,7 @@
         ],
         compiler_params=params(collective_id=1, has_side_effects=True),
         name="begin",
-    )(mixed_shard, small_shard, time_weight)
+    )(mixed_shard, small_shard, time_weight, patch_cells[:, None], patch_cells[None], image_lengths)
 
 
 def store_rows(results):
@@ -1350,7 +1385,9 @@
     small_shard = functools.reduce(jnp.add, spots_of)
     time_padded = jnp.pad(time_weight, ((0, 0), (0, LANES - time_share)))
     shares = (qkv_share, out_share)
-    qkv_full, out_full, small, times = begin(mixed_shard, small_shard, time_padded, dims, shares, head_dim)
+    qkv_full, out_full, small, times, onehot, onehot_t, mask_q, mask_k, large_lanes = begin(
+        mixed_shard, small_shard, time_padded, patch_cells, image_lengths, dims, shares, head_dim
+    )
     vector_share = norm1_gain.shape[0]
     vectors = small[:, per : per + 6, :vector_share].transpose(1, 0, 2).reshape(6, width).astype(F32)
     b_up = small[:, per + 6, :unit_share].astype(F32)
@@ -1361,27 +1398,7 @@
     tables = small[:fsdp, table_at : table_at + table_rows, 2 * LANES : 4 * LANES].reshape(HEADS, 2, LANES)
     tables = tables.transpose(1, 0, 2).reshape(2 * HEADS, LANES)[:, :table_width]
 
-    lengths = image_lengths
-    large = lengths[0] > slot_rows
-    local_rows = jnp.arange(rows, dtype=jnp.int32)
-    slot = jnp.where(large, 0, local_rows // slot_rows)
-    spots = jnp.arange(per, dtype=jnp.int32)
-    slot_pick = slot[:, None] == spots[None, :]
-    slot_length = jnp.sum(jnp.where(slot_pick, lengths[None, :], 0), axis=1)
-    valid = local_rows - slot * slot_rows < slot_length
     grid_index = jnp.arange(GRID, dtype=jnp.int32)
-    row_hot = ((patch_cells // GRID)[:, None] == grid_index[None, :]).astype(BF16)
-    col_hot = ((patch_cells % GRID)[:, None] == grid_index[None, :]).astype(BF16)
-    onehot = jnp.concatenate([row_hot, col_hot, row_hot, col_hot], axis=1)
-    both_index = jnp.concatenate([grid_index, grid_index])[:, None]
-    both_cells = jnp.where(jnp.arange(2 * GRID)[:, None] < GRID, patch_cells // GRID, patch_cells % GRID)
-    onehot_t = (both_cells == both_index).astype(BF16)
-    lanes_left = ((0, 0), (head_dim, LANES - head_dim - per - 1))
-    mask_q = jnp.concatenate(
-        [jnp.where(slot_pick, 0.0, BIG), jnp.full((rows, 1), BIG, F32)], axis=1
-    ).astype(BF16)
-    mask_k = jnp.concatenate([slot_pick, jnp.logical_not(valid)[:, None]], axis=1).astype(BF16)
-    mask_q, mask_k = jnp.pad(mask_q, lanes_left), jnp.pad(mask_k, lanes_left)
 
     offsets = grid_index[:, None] - grid_index[None, :] + GRID - 1
     diagonal = offsets[:, :, None] == jnp.arange(2 * GRID - 1, dtype=jnp.int32)[None, None, :]
@@ -1404,7 +1421,6 @@
         times = jnp.pad(times.transpose(1, 0, 2), ((0, 0), (0, 8 - per), (0, LANES - head_dim)))
 
     scale = 1.0 / math.sqrt(head_dim)
-    large_lanes = jnp.broadcast_to(large.astype(F32), (1, LANES))
     normed_one, q, k, v, o, p, up, down = attend(
         tokens, vectors, qkv_full, times, large_lanes, table, onehot, mask_q, mask_k,
         scale * math.log2(math.e), unit_shards, dims,

time: 526 us -> 527 us (level)
  Pallas kernels: 495 us -> 503 us
  other arithmetic: 14.6 us -> 8.95 us
    pallas_call x1, Pallas kernels: 102 us -> 107 us  [attend_back(): pl.pallas_call(functools.partial(attend_back_kernel, block, turns, scale,...]
where the time goes in v6:
time: 527 us; the launch traced here: 522 us
  Pallas kernels  503 us (95%)
  other arithmetic  8.95 us (2%)
  local copies, waits for them, and re-layouts  8.09 us (2%)
    pallas_call x1, Pallas kernels, mlp(): pl.pallas_call(functools.partial(mlp_kernel, dims, min(256, rows), projec...  135 us
    pallas_call x1, Pallas kernels, attend_back(): pl.pallas_call(functools.partial(attend_back_kernel, block, turns, scale,...  107 us
    pallas_call x1, Pallas kernels, attend(): pl.pallas_call(functools.partial(attend_kernel, factor, block, dims, piec...  87.4 us
    pallas_call x1, Pallas kernels, end(): pl.pallas_call(functools.partial(end_kernel, dims, pieces, order, shares,...  86.7 us
    pallas_call x1, Pallas kernels, begin(): pl.pallas_call(functools.partial(begin_kernel, dims, pieces, order, share...  80.4 us

profile of v6, /device:TPU:0, one launch (start us, length us, event | category | flops | bytes accessed | tf_op | source)
XLA Modules:
  0.0 522.4 jit_solution(10431699340497951979)
XLA Ops:
  0.6 0.7 convert_element_type.49
  1.3 0.1 pad.85.clone
  1.4 0.7 broadcast_in_dim.45
  2.1 0.2 fusion.19
  2.2 1.5 fusion.18.small_shard
  3.7 1.1 copy.41
  4.9 0.8 pad.70.time_weight
  5.6 1.8 pad_maximum_fusion.1.mixed_shard
  7.4 1.7 copy.42.cells
  9.1 80.4 %begin.1 = (bf16[16,384,1152]{2,1,0:T(8,128)(2,1)}, bf16[2048,1152]{1,0:T(8,128)(2,1)}, bf16[32,16,1152]{2,1,0:T(8,128)(2,1)}, f32[32,8,128]{2,1,0:T(8,128)}, bf...) custom-call(bf16[144,1152]{1,0:T(8,128)(2,1)} %pad_maximum_fusion.1., ...), custom_call_target="tpu_custom_call" | custom-call | tf_op jit(solution)/shard_map/begin/pallas_call | solution.py:475
  89.5 0.7 slice.41
  90.3 1.0 convert_reduce_fusion
  91.3 0.1 reshape.122
  91.4 0.7 reshape.119.refs_6_
  92.1 0.9 convert_bitcast_fusion
  93.0 0.7 reshape.117.vectors.refs_3_
  93.8 0.6 fusion.3
  94.3 0.3 reduce-precision_convert_fusion
  94.7 1.2 maximum_maximum_fusion.table
  95.9 87.4 %attend.1 = (bf16[1024,1152]{1,0:T(8,128)(2,1)}, bf16[16,1024,128]{2,1,0:T(8,128)(2,1)}, bf16[16,1024,128]{2,1,0:T(8,128)(2,1)}, bf16[16,1024,128]{2,1,0:T(8,128...) custom-call(bf16[1024,1152]{1,0:T(8,128)(2,1)} %tokens.3, ...), custom_call_target="tpu_custom_call" | custom-call | tf_op jit(solution)/shard_map/attend/pallas_call | solution.py:616
  183.3 134.7 %mlp.1 = (f32[1024,1152]{1,0:T(8,128)}, f32[1024,1152]{1,0:T(8,128)}, f32[1024,1152]{1,0:T(8,128)}, f32[6,1,768]{2,1,0:T(1,128)}, bf16[4,2,1,2,2,144,1152]{6,5,4...) custom-call(bf16[1024,1152]{1,0:T(8,128)(2,1)} %tokens.3, ...), custom_call_target="tpu_custom_call" | custom-call | tf_op jit(solution)/shard_map/mlp/pallas_call | solution.py:1049
  318.0 0.0 copy-start
  318.0 107.1 %attend_back.1 = (bf16[1024,1152]{1,0:T(8,128)(2,1)}, f32[1024,1152]{1,0:T(8,128)}, f32[4,1152]{1,0:T(4,128)}, bf16[1024,6144]{1,0:T(8,128)(2,1)}, bf16[16,216,1...) custom-call(f32[1024,1152]{1,0:T(8,128)} %get-tuple-element.83.hidde, ...), custom_call_target="tpu_custom_call" | custom-call | tf_op jit(solution)/shard_map/attend_back/pallas_call | solution.py:783
  425.1 0.0 copy-done
  425.2 0.1 reshape.116
  425.3 0.1 reshape_reshape.3
  425.4 1.2 fusion.21
  426.6 0.7 convolution_bitcast_fusion
  427.4 1.4 pad_add_fusion.vec_in
  428.7 86.7 %end.1 = (bf16[1024,1152]{1,0:T(8,128)(2,1)}, f32[16,1408]{1,0:T(8,128)}, f32[72,1152]{1,0:T(8,128)}, f32[108,1152]{1,0:T(8,128)}, f32[36,1152]{1,0:T(8,128)}) custom-call(bf16[1024,1152]{1,0:T(8,128)(2,1)} %tokens.3, bf16[1024,6144]{1,0:T(8,128)(2,1)} %get-tuple-element.96.dqkv, bf16[6144,1152]{1,0:T(8,128)(2,1)} %bitcast.48, ...), custom_call_target="tpu_custom_call" | custom-call | tf_op jit(solution)/shard_map/end/pallas_call | solution.py:1248
  515.5 6.5 %split.1 = (f32[36]{0:T(128)}, f32[36]{0:T(128)}, f32[36]{0:T(128)}, f32[36]{0:T(128)}, f32[36]{0:T(128)}, /*index=5*/f32[36]{0:T(128)}, f32[144]{0:T(256)}, f32...) custom-call(f32[16,1408]{1,0:T(8,128)} %get-tuple-element.104.total,, ...), custom_call_target="tpu_custom_call" | custom-call | tf_op jit(solution)/shard_map/split/pallas_call | solution.py:1322
  (13 shorter events, 0.3 us)
Async XLA Ops:
  318.0 107.1 %copy-start = (f32[6,1,768]{2,1,0:T(1,128)S(1)}, f32[6,1,768]{2,1,0:T(1,128)}, u32[]{:S(2)}) copy-start(f32[6,1,768]{2,1,0:T(1,128)} %get-tuple-element.100) | copy-start | bytes 55300
